TPU v7x, 32 devices: a whole 2x2x4 slice. The times are simulated.
32 devices in a mesh: section: 4 (over x, core), seq: 8 (over z, y).
Axes of the slice: x: 2, y: 2, z: 4, core: 2. Of those that a mesh axis runs over, the one named last changes fastest.
Arguments:
- query: bfloat16 [4, 4096, 1024], P('section', 'seq'), may hold values from -6 to 6
- key: bfloat16 [4, 4096, 1024], P('section', 'seq'), may hold values from -6 to 6
- value: bfloat16 [4, 4096, 1024], P('section', 'seq'), may hold values from -6 to 6
- grad_sent: bfloat16 [4, 4096, 2048], P('section', 'seq'), may hold values from -6 to 6
- out_weight: bfloat16 [4, 1024, 2048], P('section'), may hold values from -0.125 to 0.125
- assign: int32 [4, 4, 4096], P('section', None, 'seq'), may hold values from 0 to 1, as said below
Outputs:
- grad_query: bfloat16 [4, 4096, 1024], P('section', 'seq')
- grad_key: bfloat16 [4, 4096, 1024], P('section', 'seq')
- grad_value: bfloat16 [4, 4096, 1024], P('section', 'seq')
Inputs may be any that keep to these rules, and one draw needn't show every extreme that they name: `assign`: for each section and routing head, every cluster holds exactly 2048 tokens. The 512 tokens of one device put 1, 3, 5 or 7 times 448 // 7 tokens into one cluster, so at most 448, and some device reaches 448 for every section and head.
All inputs are finite; a program needn't handle non-finite values.
Results may differ from a plain program's by a relative error of at most 0.0058.
Values may be sent and summed in bfloat16 or wider, within the bound.
No kernel may reach another device: no remote copies, remote signals or barrier semaphores. Data moves between devices by JAX's collectives and lax.ppermute only.
A program may use at most 128 MiB of HBM per device.

v0:
```python
import functools

import jax
import jax.numpy as jnp
from jax import lax
from jax.experimental import pallas as pl
from jax.experimental.pallas import tpu as pltpu
from jax.sharding import PartitionSpec as P

HR = 4
HL = 4
HD = 128
CS = 2048
WIN = 512
QB = 256
MIB = 1024 * 1024
NT = (((1,), (1,)), ((), ()))
F32 = jnp.float32
BF16 = jnp.bfloat16


def vmem(count=1):
    return [pl.BlockSpec(memory_space=pltpu.VMEM)] * count


def smem(count=1):
    return [pl.BlockSpec(memory_space=pltpu.SMEM)] * count


def params(mib):
    return pltpu.CompilerParams(vmem_limit_bytes=mib * MIB)


def dot(a, b):
    return jnp.dot(a, b, preferred_element_type=F32)


def dot_nt(a, b):
    return lax.dot_general(a, b, NT, preferred_element_type=F32)


def rows(start, size):
    return pl.ds(pl.multiple_of(start, size), size)


def pack_kernel(unit, place, x0, x1, x2, x3, sorted_ref, send_ref, slot_row, slot_col, kept_ref):
    tok = x0.shape[0] - 16
    tok = tok // 3
    side = place[1]
    lane = lax.broadcasted_iota(jnp.int32, (1, tok), 1).astype(F32)
    labels = []
    for x in (x0, x1, x2, x3):
        block = x[3 * tok :, :].astype(F32)
        labels.append(jnp.concatenate([block[r : r + 1, :] for r in range(tok // 128)], axis=1))
    label = jnp.concatenate(labels + [jnp.zeros((4, tok), F32)], axis=0)
    upper = (
        lax.broadcasted_iota(jnp.int32, (tok, tok), 0) <= lax.broadcasted_iota(jnp.int32, (tok, tok), 1)
    ).astype(BF16)
    ones = dot(label.astype(BF16), upper)
    totals = [jnp.sum(row).astype(jnp.int32) for row in labels]
    whole = totals[0] + totals[1] + totals[2] + totals[3]
    half = CS // 2
    keep_one = jnp.where(side == 0, (whole > half).astype(jnp.int32), (whole >= half).astype(jnp.int32))
    keep_f = keep_one.astype(F32)
    slots = []
    for d in range(4):
        kept = jnp.where(keep_one == 1, totals[d], tok - totals[d])
        kept_ref[d] = kept // unit
        is_kept = labels[d] * keep_f + (1.0 - labels[d]) * (1.0 - keep_f)
        ones_d = ones[d : d + 1, :]
        count = ones_d * keep_f + (lane + 1.0 - ones_d) * (1.0 - keep_f)
        slot = jnp.where(is_kept > 0.5, count - 1.0, kept.astype(F32) + lane - count)
        slots.append(slot)
    slots_all = jnp.concatenate(slots + [jnp.zeros((124, tok), F32)], axis=0)
    slot_row[...] = slots_all[:8, :]
    slot_col[...] = slots_all.T
    row_index = lax.broadcasted_iota(jnp.int32, (tok, tok), 0).astype(F32)
    for d, x in enumerate((x0, x1, x2, x3)):
        move = (row_index == slots[d]).astype(BF16)
        for i in range(3):
            sorted_ref[d, i] = dot(move, x[i * tok : (i + 1) * tok, :]).astype(BF16)
    offset = jnp.int32(0)
    info_row = lax.broadcasted_iota(jnp.int32, (16, HD), 0)
    info = jnp.zeros((16, HD), F32)
    for d in range(4):
        kept = kept_ref[d]
        info = jnp.where(info_row == d, kept.astype(F32), info)

        def put(u, carry, d=d, offset=offset, kept=kept):
            for i in range(3):
                send_ref[rows(i * half + (offset + u - kept) * unit, unit), :] = sorted_ref[d, i, rows(u * unit, unit), :]
            return carry

        lax.fori_loop(kept, tok // unit, put, 0)
        offset = offset + tok // unit - kept
    send_ref[3 * half :, :] = info.astype(BF16)


def pack_one_kernel(unit, slot_row, kept_ref, x0, x1, x2, x3, sorted_ref, send_ref):
    tok = x0.shape[0]
    row_index = lax.broadcasted_iota(jnp.int32, (tok, tok), 0).astype(F32)
    for d, x in enumerate((x0, x1, x2, x3)):
        move = (row_index == slot_row[d : d + 1, :]).astype(BF16)
        sorted_ref[d] = dot(move, x[...]).astype(BF16)
    offset = jnp.int32(0)
    for d in range(4):
        kept = kept_ref[d]

        def put(u, carry, d=d, offset=offset, kept=kept):
            send_ref[rows((offset + u - kept) * unit, unit), :] = sorted_ref[d, rows(u * unit, unit), :]
            return carry

        lax.fori_loop(kept, tok // unit, put, 0)
        offset = offset + tok // unit - kept


def each_unit(units, place, kept_ref, got_ref, own, got):
    first, side = place[0], place[1]
    pos = jnp.int32(0)
    for z in range(4):
        d = lax.rem(first - z + 4, 4)
        kept = kept_ref[d]
        came = units - got_ref[d]
        at = jnp.int32(0)
        for e in range(4):
            at = at + jnp.where(e < d, units - got_ref[e], 0)
        own_pos = pos + jnp.where(side == 0, 0, came)
        got_pos = pos + jnp.where(side == 0, kept, 0)

        def own_step(u, carry, d=d, own_pos=own_pos):
            own(d, u, own_pos + u)
            return carry

        def got_step(u, carry, at=at, got_pos=got_pos):
            got(at + u, got_pos + u)
            return carry

        lax.fori_loop(0, kept, own_step, 0)
        lax.fori_loop(0, came, got_step, 0)
        pos = pos + kept + came


def probs_kernel(unit, place, kept_ref, sorted_ref, came_ref, got_ref, q_ref, k_ref, v_ref, kt_ref, ot_ref, p_ref, vt, s_ref):
    tok = sorted_ref.shape[2]
    half = CS // 2
    info = came_ref[3 * half :, :].astype(F32)
    for d in range(4):
        got_ref[d] = jnp.max(info[d : d + 1, :]).astype(jnp.int32)
    outs = (q_ref, k_ref, v_ref)

    def own(d, u, to):
        for i in range(3):
            outs[i][rows(to * unit, unit), :] = sorted_ref[d, i, rows(u * unit, unit), :]

    def got(at, to):
        for i in range(3):
            outs[i][rows(to * unit, unit), :] = came_ref[rows(i * half + at * unit, unit), :]

    each_unit(tok // unit, place, kept_ref, got_ref, own, got)
    kt_ref[...] = k_ref[...].astype(F32).T.astype(BF16)
    vt[...] = v_ref[...].astype(F32).T.astype(BF16)
    factor = HD**-0.5
    low = lax.broadcasted_iota(jnp.int32, (QB, QB), 0) <= lax.broadcasted_iota(jnp.int32, (QB, QB), 1)
    for j in range(CS // QB):
        q = q_ref[j * QB : (j + 1) * QB, :]
        top = None
        for i in range(j + 1):
            s = dot_nt(k_ref[i * QB : (i + 1) * QB, :], q) * factor
            if i == j:
                s = jnp.where(low, s, -1e30)
            s_ref[i * QB : (i + 1) * QB, :] = s
            peak = jnp.max(s.reshape(QB // 8, 8, QB), axis=0)
            top = peak if top is None else jnp.maximum(top, peak)
        top = jnp.max(top, axis=0, keepdims=True)
        total = None
        for i in range(j + 1):
            w = jnp.exp(s_ref[i * QB : (i + 1) * QB, :] - top)
            s_ref[i * QB : (i + 1) * QB, :] = w
            part = jnp.sum(w.reshape(QB // 8, 8, QB), axis=0)
            total = part if total is None else total + part
        scale = 1.0 / jnp.sum(total, axis=0, keepdims=True)
        for i in range(j + 1):
            p_ref[i * QB : (i + 1) * QB, j * QB : (j + 1) * QB] = (s_ref[i * QB : (i + 1) * QB, :] * scale).astype(BF16)
        end = (j + 1) * QB
        ot_ref[:, j * QB : end] = dot(vt[:, :end], p_ref[:end, j * QB : end])


def grads_kernel(
    unit, place, kept_ref, got_ref, sorted_ref, came_ref, q_ref, k_ref, v_ref, kt_ref, ot_ref, p_hbm,
    own_ref, back_ref, g_ref, p_ref, dqt, res, sems,
):
    tok = sorted_ref.shape[1]
    half = CS // 2
    count = CS // QB
    copies = []
    for i in range(count):
        span = (slice(i * QB, (i + 1) * QB), slice(i * QB, CS))
        copy = pltpu.make_async_copy(p_hbm.at[span], p_ref.at[span], sems.at[i])
        copy.start()
        copies.append(copy)

    def own(d, u, to):
        g_ref[rows(to * unit, unit), :] = sorted_ref[d, rows(u * unit, unit), :]

    def got(at, to):
        g_ref[rows(to * unit, unit), :] = came_ref[rows(at * unit, unit), :]

    each_unit(tok // unit, place, kept_ref, got_ref, own, got)
    delta = jnp.sum(g_ref[...].astype(F32).T * ot_ref[...], axis=0, keepdims=True)
    factor = HD**-0.5
    for i in range(count):
        copies[i].wait()
        lo, hi = i * QB, (i + 1) * QB
        p = p_ref[lo:hi, lo:]
        g = g_ref[lo:, :]
        res[2, lo:hi, :] = dot(p, g).astype(BF16)
        dp = dot_nt(v_ref[lo:hi, :], g)
        ds = (p.astype(F32) * (dp - delta[:, lo:])).astype(BF16)
        res[1, lo:hi, :] = (dot(ds, q_ref[lo:, :]) * factor).astype(BF16)
        part = dot(kt_ref[:, lo:hi], ds)
        dqt[:, lo:] = part if i == 0 else dqt[:, lo:] + part
    res[0] = (dqt[...].T * factor).astype(BF16)

    def own_out(d, u, to):
        for i in range(3):
            own_ref[d, i, rows(u * unit, unit), :] = res[i, rows(to * unit, unit), :]

    def got_out(at, to):
        for i in range(3):
            back_ref[i, rows(at * unit, unit), :] = res[i, rows(to * unit, unit), :]

    each_unit(tok // unit, place, kept_ref, got_ref, own_out, got_out)


def unsort_kernel(unit, kept_ref, slot_col, own_ref, back_ref, y0, y1, y2, y3, full):
    tok = own_ref.shape[2]
    col_index = lax.broadcasted_iota(jnp.int32, (tok, tok), 1).astype(F32)
    offset = jnp.int32(0)
    for d, y in enumerate((y0, y1, y2, y3)):
        kept = kept_ref[d]

        def own(u, carry, d=d):
            for i in range(3):
                full[i, rows(u * unit, unit), :] = own_ref[d, i, rows(u * unit, unit), :]
            return carry

        def got(u, carry, offset=offset, kept=kept):
            for i in range(3):
                full[i, rows(u * unit, unit), :] = back_ref[i, rows((offset + u - kept) * unit, unit), :]
            return carry

        lax.fori_loop(0, kept, own, 0)
        lax.fori_loop(kept, tok // unit, got, 0)
        offset = offset + tok // unit - kept
        move = (col_index == slot_col[:, d : d + 1]).astype(BF16)
        for i in range(3):
            y[i] = dot(move, full[i]).astype(BF16)


def window_kernel(place, q_ref, k_ref, v_ref, g_ref, prior_ref, dq_ref, own_ref, carry_ref, keys, values, kt, dk, dv):
    tok = q_ref.shape[0]
    keys[:tok, :] = prior_ref[0]
    keys[tok:, :] = k_ref[...]
    values[:tok, :] = prior_ref[1]
    values[tok:, :] = v_ref[...]
    kt[...] = keys[...].astype(F32).T.astype(BF16)
    factor = HD**-0.5
    r = lax.broadcasted_iota(jnp.int32, (QB, QB), 0)
    c = lax.broadcasted_iota(jnp.int32, (QB, QB), 1)
    span = tok + QB
    edge = tok - (tok // QB - 1) * QB
    started = place[0] > 0
    for j in range(tok // QB):
        lo, hi = j * QB, j * QB + span
        q = q_ref[j * QB : (j + 1) * QB, :]
        g = g_ref[j * QB : (j + 1) * QB, :]
        s = dot_nt(keys[lo:hi, :], q) * factor
        first = jnp.where(r > c, s[:QB], -1e30)
        last = jnp.where(r <= c, s[span - QB :], -1e30)
        s = jnp.concatenate([first, s[QB : span - QB], last], axis=0)
        before = tok - lo
        s = jnp.concatenate([jnp.where(started, s[:before], -1e30), s[before:]], axis=0)
        top = jnp.max(s, axis=0, keepdims=True)
        w = jnp.exp(s - top)
        p = w * (1.0 / jnp.sum(w, axis=0, keepdims=True))
        dp = dot_nt(values[lo:hi, :], g)
        delta = jnp.sum(p * dp, axis=0, keepdims=True)
        pb = p.astype(BF16)
        ds = (p * (dp - delta)).astype(BF16)
        dq_ref[j * QB : (j + 1) * QB, :] = (dot(kt[:, lo:hi], ds).T * factor).astype(BF16)
        part_k = dot(ds, q) * factor
        part_v = dot(pb, g)
        if j == 0:
            dk[lo:hi, :] = part_k
            dv[lo:hi, :] = part_v
        else:
            dk[lo : hi - QB, :] = dk[lo : hi - QB, :] + part_k[:-QB]
            dv[lo : hi - QB, :] = dv[lo : hi - QB, :] + part_v[:-QB]
            dk[hi - QB : hi, :] = part_k[-QB:]
            dv[hi - QB : hi, :] = part_v[-QB:]
    carry_ref[0] = dk[:tok, :].astype(BF16)
    carry_ref[1] = dv[:tok, :].astype(BF16)
    own_ref[0] = dk[tok:, :]
    own_ref[1] = dv[tok:, :]


def join_kernel(place, y0, y1, y2, y3, local_dq, own_ref, carry_ref, dq_ref, dk_ref, dv_ref):
    outs = (dq_ref, dk_ref, dv_ref)
    for d, y in enumerate((y0, y1, y2, y3)):
        at = lax.rem(place[0] + d, 4) * HD
        for i in range(3):
            outs[i][:, pl.ds(pl.multiple_of(at, HD), HD)] = y[i]
    side = HR * HD
    dq_ref[:, side:] = local_dq[...]
    dk_ref[:, side:] = (own_ref[0] + carry_ref[0].astype(F32)).astype(BF16)
    dv_ref[:, side:] = (own_ref[1] + carry_ref[1].astype(F32)).astype(BF16)


def struct(*shape, dtype=BF16):
    return jax.ShapeDtypeStruct(shape, dtype)


def pair_body(query, key, value, grad_sent, out_weight, assign):
    tok = query.shape[1]
    devices = lax.axis_size("seq")
    place = lax.axis_index("seq")
    first, side = place // 2, place % 2
    where = jnp.stack([first, side]).astype(jnp.int32)
    unit = CS // (4 * devices)
    half = CS // 2

    def among_groups(block, shift):
        route = [(i, ((i // 2 + shift) % HR) * 2 + i % 2) for i in range(devices)]
        return lax.ppermute(block, "seq", route)

    def swap(block):
        return lax.ppermute(block, "seq", [(i, i ^ 1) for i in range(devices)])

    boundary = from_behind(grad_sent, "section", -1)[0]
    labels = assign[0].astype(BF16).reshape(HR, tok // HD, HD)
    labels = jnp.pad(labels, ((0, 0), (0, 16 - tok // HD), (0, 0)))

    def head_of(array, head):
        return lax.dynamic_slice_in_dim(array, head * HD, HD, 1)

    sent = []
    for d in range(HR):
        head = (first + d) % HR
        sent.append(
            jnp.concatenate(
                [head_of(query[0], head), head_of(key[0], head), head_of(value[0], head)]
                + [lax.dynamic_index_in_dim(labels, head, 0, keepdims=False)],
                axis=0,
            )
        )
    arrived = [sent[0]] + [among_groups(sent[d], d) for d in range(1, HR)]

    local = slice(HR * HD, (HR + HL) * HD)
    prior = shifted(jnp.stack([key[0][:, local], value[0][:, local]]), "seq", 1)

    attn_grad = lax.dot_general(
        boundary, out_weight[0], (((1,), (1,)), ((), ())), preferred_element_type=F32
    ).astype(BF16)
    g_sent = [head_of(attn_grad, (first + d) % HR) for d in range(HR)]
    g_arrived = [g_sent[0]] + [among_groups(g_sent[d], d) for d in range(1, HR)]

    ordered, send, slot_row, slot_col, kept = pl.pallas_call(
        functools.partial(pack_kernel, unit),
        out_shape=[
            struct(HR, 3, tok, HD),
            struct(3 * half + 16, HD),
            struct(8, tok, dtype=F32),
            struct(tok, HD, dtype=F32),
            struct(HR, dtype=jnp.int32),
        ],
        in_specs=smem() + vmem(4),
        out_specs=vmem(4) + smem(),
        compiler_params=params(32),
        name="pack",
    )(where, *arrived)
    came = swap(send)
    got, q, k, v, kt, ot, p = pl.pallas_call(
        functools.partial(probs_kernel, unit),
        out_shape=[struct(HR, dtype=jnp.int32)]
        + [struct(CS, HD)] * 3
        + [struct(HD, CS), struct(HD, CS, dtype=F32), struct(CS, CS)],
        in_specs=smem(2) + vmem(2),
        out_specs=smem() + vmem(6),
        scratch_shapes=[pltpu.VMEM((HD, CS), BF16), pltpu.VMEM((CS, QB), F32)],
        compiler_params=params(40),
        name="probs",
    )(where, kept, ordered, came)

    g_ordered, g_out = pl.pallas_call(
        functools.partial(pack_one_kernel, unit),
        out_shape=[struct(HR, tok, HD), struct(half, HD)],
        in_specs=vmem() + smem() + vmem(4),
        out_specs=vmem(2),
        compiler_params=params(32),
        name="pack_grad",
    )(slot_row, kept, *g_arrived)
    g_came = swap(g_out)

    own, back = pl.pallas_call(
        functools.partial(grads_kernel, unit),
        out_shape=[struct(HR, 3, tok, HD), struct(3, half, HD)],
        in_specs=smem(3) + vmem(7) + [pl.BlockSpec(memory_space=pl.ANY)],
        out_specs=vmem(2),
        scratch_shapes=[
            pltpu.VMEM((CS, HD), BF16),
            pltpu.VMEM((CS, CS), BF16),
            pltpu.VMEM((HD, CS), F32),
            pltpu.VMEM((3, CS, HD), BF16),
            pltpu.SemaphoreType.DMA((CS // QB,)),
        ],
        compiler_params=params(40),
        name="grads",
    )(where, kept, got, g_ordered, g_came, q, k, v, kt, ot, p)
    returned = swap(back)
    natural = pl.pallas_call(
        functools.partial(unsort_kernel, unit),
        out_shape=[struct(3, tok, HD)] * 4,
        in_specs=smem() + vmem(3),
        out_specs=vmem(4),
        scratch_shapes=[pltpu.VMEM((3, tok, HD), BF16)],
        compiler_params=params(32),
        name="unsort",
    )(kept, slot_col, own, returned)
    home = [natural[0]] + [among_groups(natural[d], -d) for d in range(1, HR)]

    local_dq, local_own, carry = pl.pallas_call(
        window_kernel,
        grid=(HL,),
        out_shape=[struct(tok, HL * HD), struct(2, tok, HL * HD, dtype=F32), struct(2, tok, HL * HD)],
        in_specs=smem()
        + [pl.BlockSpec((tok, HD), lambda h: (0, HR + h))] * 4
        + [pl.BlockSpec((2, tok, HD), lambda h: (0, 0, h))],
        out_specs=[
            pl.BlockSpec((tok, HD), lambda h: (0, h)),
            pl.BlockSpec((2, tok, HD), lambda h: (0, 0, h)),
            pl.BlockSpec((2, tok, HD), lambda h: (0, 0, h)),
        ],
        scratch_shapes=[
            pltpu.VMEM((2 * tok, HD), BF16),
            pltpu.VMEM((2 * tok, HD), BF16),
            pltpu.VMEM((HD, 2 * tok), BF16),
            pltpu.VMEM((2 * tok, HD), F32),
            pltpu.VMEM((2 * tok, HD), F32),
        ],
        compiler_params=params(32),
        name="window",
    )(place.astype(jnp.int32).reshape(1), query[0], key[0], value[0], attn_grad, prior)
    carried = shifted(carry, "seq", -1)

    outs = pl.pallas_call(
        join_kernel,
        out_shape=[struct(tok, (HR + HL) * HD)] * 3,
        in_specs=smem() + vmem(7),
        out_specs=vmem(3),
        compiler_params=params(32),
        name="join",
    )(where, *home, local_dq, local_own, carried)
    return tuple(out[None] for out in outs)


def from_behind(block, axis, distance):
    devices = range(lax.axis_size(axis))
    route = [((i - distance) % len(devices), i) for i in devices]
    return lax.ppermute(block, axis, route)


def shifted(block, axis, distance):
    devices = range(lax.axis_size(axis))
    route = [(i - distance, i) for i in devices if i - distance in devices]
    return lax.ppermute(block, axis, route)


def cluster_block(query_rows, key_rows, value_rows, grad_rows, allowed, factor):
    scores = jnp.dot(query_rows, key_rows.T, preferred_element_type=jnp.float32) * factor
    scores = jnp.where(allowed, scores, -1e30)
    highest = jnp.max(scores, axis=1, keepdims=True)
    weights = jnp.exp(scores - highest)
    probs = weights / jnp.sum(weights, axis=1, keepdims=True)
    dprob = jnp.dot(grad_rows, value_rows.T, preferred_element_type=jnp.float32)
    delta = jnp.sum(probs * dprob, axis=1, keepdims=True)
    dscore = probs * (dprob - delta)
    probs_b = probs.astype(jnp.bfloat16)
    dscore_b = dscore.astype(jnp.bfloat16)
    grad_query = jnp.dot(dscore_b, key_rows, preferred_element_type=jnp.float32) * factor
    grad_key = jnp.dot(dscore_b.T, query_rows, preferred_element_type=jnp.float32) * factor
    grad_value = jnp.dot(probs_b.T, grad_rows, preferred_element_type=jnp.float32)
    return (grad_query, grad_key, grad_value)


def cluster_grads(query_rows, key_rows, value_rows, grad_rows, factor):
    length = query_rows.shape[0]
    span = min(512, length)
    pieces = []
    total_key = jnp.zeros(key_rows.shape, jnp.float32)
    total_value = jnp.zeros(value_rows.shape, jnp.float32)
    for index in range(length // span):
        first = index * span
        end = first + span
        allowed = (
            jnp.arange(end, dtype=jnp.int32)[None, :]
            <= (first + jnp.arange(span, dtype=jnp.int32))[:, None]
        )
        part_query, part_key, part_value = cluster_block(
            query_rows[first:end],
            key_rows[:end],
            value_rows[:end],
            grad_rows[first:end],
            allowed,
            factor,
        )
        pieces.append(part_query)
        total_key = total_key.at[:end].add(part_key)
        total_value = total_value.at[:end].add(part_value)
    return (jnp.concatenate(pieces, axis=0), total_key, total_value)


def window_block(query_rows, key_rows, value_rows, grad_rows, allowed, factor):
    scores = (
        jnp.einsum("qhd,khd->hqk", query_rows, key_rows, preferred_element_type=jnp.float32)
        * factor
    )
    scores = jnp.where(allowed[None], scores, -1e30)
    highest = jnp.max(scores, axis=2, keepdims=True)
    weights = jnp.exp(scores - highest)
    probs = weights / jnp.sum(weights, axis=2, keepdims=True)
    dprob = jnp.einsum("qhd,khd->hqk", grad_rows, value_rows, preferred_element_type=jnp.float32)
    delta = jnp.sum(probs * dprob, axis=2, keepdims=True)
    dscore = probs * (dprob - delta)
    probs_b = probs.astype(jnp.bfloat16)
    dscore_b = dscore.astype(jnp.bfloat16)
    grad_query = (
        jnp.einsum("hqk,khd->qhd", dscore_b, key_rows, preferred_element_type=jnp.float32) * factor
    )
    grad_key = (
        jnp.einsum("hqk,qhd->khd", dscore_b, query_rows, preferred_element_type=jnp.float32)
        * factor
    )
    grad_value = jnp.einsum("hqk,qhd->khd", probs_b, grad_rows, preferred_element_type=jnp.float32)
    return (grad_query, grad_key, grad_value)


def window_mask(query_pos, key_pos):
    return (
        (key_pos[None, :] > query_pos[:, None] - WIN)
        & (key_pos[None, :] <= query_pos[:, None])
        & (key_pos[None, :] >= 0)
    )


def general_body(query, key, value, grad_sent, out_weight, assign):
    tok_rows = query.shape[1]
    heads = HR + HL
    devices = lax.axis_size("seq")
    place = lax.axis_index("seq")
    factor = HD ** (-0.5)
    boundary = from_behind(grad_sent, "section", -1)[0]
    attn_grad = lax.dot_general(
        boundary, out_weight[0], (((1,), (1,)), ((), ())), preferred_element_type=jnp.float32
    ).astype(jnp.bfloat16)
    query_heads = query[0].reshape(tok_rows, heads, HD)
    key_heads = key[0].reshape(tok_rows, heads, HD)
    value_heads = value[0].reshape(tok_rows, heads, HD)
    grad_heads = attn_grad.reshape(tok_rows, heads, HD)
    clusters = tok_rows * devices // CS
    owned = HR * tok_rows // CS
    capacity = 7 * CS // (4 * devices)
    unit_rows = capacity // 7
    width = owned * capacity
    head_slots = clusters * capacity
    labels = assign[0]
    members = (labels[:, :, None] == jnp.arange(clusters, dtype=jnp.int32)[None, None, :]).astype(
        jnp.bfloat16
    )
    token_ids = jnp.arange(tok_rows, dtype=jnp.int32)
    lower = (token_ids[:, None] >= token_ids[None, :]).astype(jnp.bfloat16)
    running_counts = jnp.einsum("ts,hsc->htc", lower, members, preferred_element_type=jnp.float32)
    ranks = (jnp.sum(running_counts * members.astype(jnp.float32), axis=2) - 1.0).astype(jnp.int32)
    local_slot = labels * capacity + ranks
    slot_hit = jnp.arange(head_slots, dtype=jnp.int32)[None, :, None] == local_slot[:, None, :]
    slot_table = slot_hit.astype(jnp.bfloat16)
    routed_in = jnp.concatenate(
        [query_heads[:, :HR], key_heads[:, :HR], value_heads[:, :HR], grad_heads[:, :HR]], axis=2
    )
    packed = jnp.einsum(
        "hst,thd->hsd", slot_table, routed_in, preferred_element_type=jnp.float32
    ).astype(jnp.bfloat16)
    packed = packed.reshape(devices, width, 4 * HD)
    token_pos = place * tok_rows + token_ids
    slot_pos = jnp.max(jnp.where(slot_hit, token_pos[None, None, :], -1), axis=2).reshape(
        devices, width
    )
    send_query = packed[:, :, :HD]
    send_key = packed[:, :, HD : 2 * HD]
    send_value = packed[:, :, 2 * HD : 3 * HD]
    send_grad = packed[:, :, 3 * HD :]
    arrived_query, arrived_key, arrived_value, arrived_grad, arrived_pos = (
        lax.all_to_all(send_query, "seq", split_axis=0, concat_axis=0, tiled=True),
        lax.all_to_all(send_key, "seq", split_axis=0, concat_axis=0, tiled=True),
        lax.all_to_all(send_value, "seq", split_axis=0, concat_axis=0, tiled=True),
        lax.all_to_all(send_grad, "seq", split_axis=0, concat_axis=0, tiled=True),
        lax.all_to_all(slot_pos, "seq", split_axis=0, concat_axis=0, tiled=True),
    )
    arrived_all = jnp.concatenate([arrived_query, arrived_key, arrived_value, arrived_grad], axis=2)
    unit_index = jnp.arange(7, dtype=jnp.int32)
    target_units = jnp.arange(CS // unit_rows, dtype=jnp.int32)
    block = arrived_all.reshape(devices * 7, unit_rows * 4 * HD)
    live_counts = jnp.sum((arrived_pos >= 0).astype(jnp.int32), axis=1)
    units = live_counts // unit_rows
    starts = jnp.cumsum(units) - units
    picker = (target_units[:, None, None] == starts[None, :, None] + unit_index[None, None, :]) & (
        unit_index[None, None, :] < units[None, :, None]
    )
    picker = picker.reshape(CS // unit_rows, devices * 7).astype(jnp.bfloat16)
    compact = (
        jnp.dot(picker, block, preferred_element_type=jnp.float32)
        .astype(jnp.bfloat16)
        .reshape(CS, 4 * HD)
    )
    results = cluster_grads(
        compact[:, :HD],
        compact[:, HD : 2 * HD],
        compact[:, 2 * HD : 3 * HD],
        compact[:, 3 * HD :],
        factor,
    )
    answer = jnp.concatenate([result.astype(jnp.bfloat16) for result in results], axis=1).reshape(
        CS // unit_rows, unit_rows * 3 * HD
    )
    spread = jnp.dot(picker.T, answer, preferred_element_type=jnp.float32).astype(jnp.bfloat16)
    outgoing = spread.reshape(devices, capacity, 3 * HD)
    back_query, back_key, back_value = (
        lax.all_to_all(outgoing[:, :, :HD], "seq", split_axis=0, concat_axis=0, tiled=True),
        lax.all_to_all(outgoing[:, :, HD : 2 * HD], "seq", split_axis=0, concat_axis=0, tiled=True),
        lax.all_to_all(outgoing[:, :, 2 * HD :], "seq", split_axis=0, concat_axis=0, tiled=True),
    )
    back_all = jnp.concatenate([back_query, back_key, back_value], axis=2).reshape(
        HR, head_slots, 3 * HD
    )
    routed_out = jnp.einsum(
        "hst,hsd->thd", slot_table, back_all, preferred_element_type=jnp.float32
    ).astype(jnp.bfloat16)
    routed_query = routed_out[:, :, :HD]
    routed_key = routed_out[:, :, HD : 2 * HD]
    routed_value = routed_out[:, :, 2 * HD :]
    local_query = query_heads[:, HR:]
    local_key = key_heads[:, HR:]
    local_value = value_heads[:, HR:]
    local_grad = grad_heads[:, HR:]
    prior_key, prior_value = shifted((local_key, local_value), "seq", 1)
    keys_all = jnp.concatenate([prior_key, local_key], axis=0)
    values_all = jnp.concatenate([prior_value, local_value], axis=0)
    key_positions = (place - 1) * tok_rows + jnp.arange(2 * tok_rows, dtype=jnp.int32)
    query_positions = place * tok_rows + jnp.arange(tok_rows, dtype=jnp.int32)
    span = min(512, tok_rows)
    total_key = jnp.zeros((2 * tok_rows, HL, HD), jnp.float32)
    total_value = jnp.zeros((2 * tok_rows, HL, HD), jnp.float32)
    start = tok_rows - WIN
    allowed = window_mask(query_positions, key_positions)
    part_query, part_key, part_value = window_block(
        local_query, keys_all, values_all, local_grad, allowed, factor
    )
    total_key = total_key.at[start : start + span + WIN].add(part_key)
    total_value = total_value.at[start : start + span + WIN].add(part_value)
    tail = tok_rows - WIN
    carried_key, carried_value = (
        shifted(total_key[tail:tok_rows].astype(jnp.bfloat16), "seq", -1).astype(jnp.float32),
        shifted(total_value[tail:tok_rows].astype(jnp.bfloat16), "seq", -1).astype(jnp.float32),
    )
    local_dk = total_key[tok_rows:].at[tail:].add(carried_key)
    local_dv = total_value[tok_rows:].at[tail:].add(carried_value)
    local_dq = part_query.astype(jnp.bfloat16)
    grad_query = jnp.concatenate([routed_query, local_dq], axis=1).reshape(1, tok_rows, heads * HD)
    grad_key = jnp.concatenate([routed_key, local_dk.astype(jnp.bfloat16)], axis=1).reshape(
        1, tok_rows, heads * HD
    )
    grad_value = jnp.concatenate([routed_value, local_dv.astype(jnp.bfloat16)], axis=1).reshape(
        1, tok_rows, heads * HD
    )
    return (grad_query, grad_key, grad_value)


def body(query, key, value, grad_sent, out_weight, assign):
    clusters = query.shape[1] * lax.axis_size("seq") // CS
    plan = pair_body if clusters == 2 else general_body
    return plan(query, key, value, grad_sent, out_weight, assign)


def solution(mesh):
    placed = (
        P("section", "seq", None),
        P("section", "seq", None),
        P("section", "seq", None),
        P("section", "seq", None),
        P("section", None, None),
        P("section", None, "seq"),
    )
    return jax.shard_map(
        body,
        mesh=mesh,
        in_specs=placed,
        out_specs=(P("section", "seq", None), P("section", "seq", None), P("section", "seq", None)),
        check_vma=False,
    )
```

profile of v0, /device:TPU:0, one launch (start us, length us, event | category | flops | bytes accessed | tf_op | source)
XLA Modules:
  0.0 187.5 jit_solution(14297311090871019620)
XLA Ops:
  0.6 2.4 %collective-permute-start.4 = (bf16[1,512,2048]{2,1,0:T(8,128)(2,1)}, bf16[1,512,2048]{2,1,0:T(8,128)(2,1)}, u32[]{:S(2)}, u32[]{:S(2)}) collective-permute-start(bf16[1,512,2048]{2,1,0:T(8,128)(2,1)} %param.9), channel_id=1, source_target_pairs={{8,0},{16,8},{24,16},{0,24},{9,1},{17,9},{25,17},{1,25},{10,2},{18... | collective-permute-start | bytes 6291464 | tf_op jit(solution)/shard_map/ppermute | solution.py:469
  3.8 1.8 dynamic-slice_bitcast_fusion.2
  5.6 2.2 %dynamic-slice_bitcast_fusion = (bf16[512,128]{1,0:T(8,128)(2,1)S(1)}, bf16[512,128]{1,0:T(8,128)(2,1)S(1)}, bf16[512,128]{1,0:T(8,128)(2,1)S(1)}, bf16[512,128]...) fusion(bf16[1,512,1024]{2,1,0:T(8,128)(2,1)} %param.8, ...), kind=kLoop, calls=%fused_computation.11 | loop fusion | bytes 2097168 | tf_op jit(solution)/shard_map/dynamic_slice | solution.py:344
  8.6 1.6 collective-permute-start
  10.9 2.6 %collective-permute-start.1 = (bf16[1552,128]{1,0:T(8,128)(2,1)}, bf16[1552,128]{1,0:T(8,128)(2,1)}, u32[]{:S(2)}, u32[]{:S(2)}) collective-permute-start(bf16[1552,128]{1,0:T(8,128)(2,1)} %pad_maximum_fusion.3), channel_id=1, source_target_pairs={{0,4},{1,5},{2,6},{3,7},{4,0},{5,1},{6,2},{7,3},{8,12},{9,13},{10,... | collective-permute-start | bytes 1191944 | tf_op jit(solution)/shard_map/ppermute | solution.py:334
  14.3 1.3 collective-permute-start.2
  15.8 1.1 pad_maximum_fusion
  16.8 3.5 %collective-permute-start.13 = (bf16[2,512,512]{2,1,0:T(8,128)(2,1)}, bf16[2,512,512]{2,1,0:T(8,128)(2,1)S(1)}, u32[]{:S(2)}, u32[]{:S(2)}) collective-permute-start(bf16[2,512,512]{2,1,0:T(8,128)(2,1)} %pad_maximum_fusion), channel_id=1, source_target_pairs={{0,1},{1,2},{2,3},{3,4},{4,5},{5,6},{6,7},{8,9},{9,10},{10,11},{11... | collective-permute-start | bytes 3145736 | tf_op jit(solution)/shard_map/ppermute | solution.py:475
  20.4 1.1 pad_maximum_fusion.1.x0
  21.5 1.4 collective-permute-done.x1
  22.9 15.8 %collective-permute-done.1.x2 = bf16[1552,128]{1,0:T(8,128)(2,1)} collective-permute-done((bf16[1552,128]{1,0:T(8,128)(2,1)}, bf16[1552,128]{1,0:T(8,128)(2,1)}, u32[]{:S(2)}, u32[]{:S(2)}) %collective-permute-start.1) | collective-permute-done | bytes 397344 | tf_op jit(solution)/shard_map/ppermute | solution.py:334
  38.6 3.8 %pack.1 = (bf16[4,3,512,128]{3,2,1,0:T(8,128)(2,1)S(1)}, bf16[3088,128]{1,0:T(8,128)(2,1)S(1)}, f32[8,512]{1,0:T(8,128)S(1)}, f32[512,128]{1,0:T(8,128)S(1)}, s32[4]{0:T(128)S(1)}) custom-call(s32[2]{0:T(128)S(1)} %pad_add_fusion.place, bf16[1552,128]{1,0:T(8,128)(2,1)S(1)} %pad_maximum_fusion.1.x0, bf16[1552,128]{1,0:T(8,128)(2,1)S(1)} %collective-permute-done.x1, ...), custom_call_target="tpu_custom_call" | custom-call | tf_op jit(solution)/shard_map/pack/pallas_call | solution.py:367
  42.4 1.6 collective-permute-start.3
  44.0 5.2 %fusion.3.g_ref = bf16[512,1024]{1,0:T(8,128)(2,1)S(1)} fusion(bf16[1,1024,2048]{2,1,0:T(8,128)(2,1)} %param.10, bf16[1,512,2048]{2,1,0:T(8,128)(2,1)} %collective-permute-done.4), kind=kOutput, calls=%fused_computation.3 | convolution fusion | flops 2148007936 | bytes 7340032 | tf_op jit(solution)/shard_map/dot_general | solution.py:361
  49.4 9.0 %collective-permute-start.5 = (bf16[512,128]{1,0:T(8,128)(2,1)S(1)}, bf16[512,128]{1,0:T(8,128)(2,1)S(1)}, u32[]{:S(2)}, u32[]{:S(2)}) collective-permute-start(bf16[512,128]{1,0:T(8,128)(2,1)S(1)} %get-tuple-element.57), channel_id=1, source_target_pairs={{0,2},{1,3},{2,4},{3,5},{4,6},{5,7},{6,0},{7,1},{8,10},{9,11},{10,... | collective-permute-start | bytes 393224 | tf_op jit(solution)/shard_map/ppermute | solution.py:334
  58.4 3.1 %collective-permute-start.6 = (bf16[512,128]{1,0:T(8,128)(2,1)S(1)}, bf16[512,128]{1,0:T(8,128)(2,1)S(1)}, u32[]{:S(2)}, u32[]{:S(2)}) collective-permute-start(bf16[512,128]{1,0:T(8,128)(2,1)S(1)} %get-tuple-element.56), channel_id=1, source_target_pairs={{0,4},{1,5},{2,6},{3,7},{4,0},{5,1},{6,2},{7,3},{8,12},{9,13},{10,... | collective-permute-start | bytes 393224 | tf_op jit(solution)/shard_map/ppermute | solution.py:334
  61.5 3.9 %collective-permute-done.5.x1 = bf16[512,128]{1,0:T(8,128)(2,1)S(1)} collective-permute-done((bf16[512,128]{1,0:T(8,128)(2,1)S(1)}, bf16[512,128]{1,0:T(8,128)(2,1)S(1)}, u32[]{:S(2)}, u32[]{:S(2)}) %collective-permute-start.5) | collective-permute-done | bytes 131104 | tf_op jit(solution)/shard_map/ppermute | solution.py:334
  65.4 3.0 %collective-permute-done.6.x2 = bf16[512,128]{1,0:T(8,128)(2,1)S(1)} collective-permute-done((bf16[512,128]{1,0:T(8,128)(2,1)S(1)}, bf16[512,128]{1,0:T(8,128)(2,1)S(1)}, u32[]{:S(2)}, u32[]{:S(2)}) %collective-permute-start.6) | collective-permute-done | bytes 131104 | tf_op jit(solution)/shard_map/ppermute | solution.py:334
  68.4 1.4 pack_grad.1
  70.2 7.7 %probs.1 = (s32[4]{0:T(128)S(1)}, bf16[2048,128]{1,0:T(8,128)(2,1)S(1)}, bf16[2048,128]{1,0:T(8,128)(2,1)S(1)}, bf16[2048,128]{1,0:T(8,128)(2,1)S(1)}, bf16[128,...) custom-call(s32[2]{0:T(128)S(1)} %pad_add_fusion.place, ...), custom_call_target="tpu_custom_call" | custom-call | tf_op jit(solution)/shard_map/probs/pallas_call | solution.py:382
  78.0 3.3 %copy-done = bf16[2048,2048]{1,0:T(8,128)(2,1)} copy-done((bf16[2048,2048]{1,0:T(8,128)(2,1)}, bf16[2048,2048]{1,0:T(8,128)(2,1)S(1)}, u32[]{:S(2)}) %copy-start) | copy-done | bytes 8388632
  81.2 8.0 %grads.1 = (bf16[4,3,512,128]{3,2,1,0:T(8,128)(2,1)S(1)}, bf16[3,1024,128]{2,1,0:T(8,128)(2,1)S(1)}) custom-call(s32[2]{0:T(128)S(1)} %pad_add_fusion.place, s32[4]{0:T(128)S(1)} %get-tuple-element.29.kept_ref, s32[4]{0:T(128)S(1)} %get-tuple-element.33.got_ref, bf16[4,512,128]{2,1,0:T(8,128)(2,1)S(1)} %get-tuple-element.35.sorted_ref, ...), custom_call_target="tpu_custom_call" | custom-call | tf_op jit(solution)/shard_map/grads/pallas_call | solution.py:404
  89.2 1.7 collective-permute-start.9
  90.9 9.7 %window.1 = (bf16[512,512]{1,0:T(8,128)(2,1)S(1)}, f32[2,512,512]{2,1,0:T(8,128)S(1)}, bf16[2,512,512]{2,1,0:T(8,128)(2,1)S(1)}) custom-call(s32[1]{0:T(128)} %bitcast.20.place, bf16[512,1024]{1,0:T(8,128)(2,1)S(1)} %bitcast.59, bf16[512,1024]{1,0:T(8,128)(2,1)S(1)} %bitcast.58, bf16[512,1024]{1,0:T(8,128)(2,1)S(1)} %bitcast.56, ...), custom_call_target="tpu_custom_call" | custom-call | tf_op jit(solution)/shard_map/window/pallas_call | solution.py:431
  100.7 1.3 collective-permute-start.14
  102.0 7.7 %collective-permute-done.9.back_ref = bf16[3,1024,128]{2,1,0:T(8,128)(2,1)S(1)} collective-permute-done((bf16[3,1024,128]{2,1,0:T(8,128)(2,1)S(1)}, bf16[3,1024,128]{2,1,0:T(8,128)(2,1)S(1)}, u32[]{:S(2)}, u32[]{:S(2)}) %collective-permute-start.9) | collective-permute-done | bytes 786464 | tf_op jit(solution)/shard_map/ppermute | solution.py:337
  109.7 3.8 %unsort.1 = (bf16[3,512,128]{2,1,0:T(8,128)(2,1)S(1)}, bf16[3,512,128]{2,1,0:T(8,128)(2,1)S(1)}, bf16[3,512,128]{2,1,0:T(8,128)(2,1)S(1)}, bf16[3,512,128]{2,1,0:T(8,128)(2,1)S(1)}) custom-call(s32[4]{0:T(128)S(1)} %get-tuple-element.29.kept_ref, f32[512,128]{1,0:T(8,128)S(1)} %get-tuple-element.30.slot_col, ...), custom_call_target="tpu_custom_call" | custom-call | tf_op jit(solution)/shard_map/unsort/pallas_call | solution.py:420
  113.5 15.2 %collective-permute-start.10 = (bf16[3,512,128]{2,1,0:T(8,128)(2,1)S(1)}, bf16[3,512,128]{2,1,0:T(8,128)(2,1)S(1)}, u32[]{:S(2)}, u32[]{:S(2)}) collective-permute-start(bf16[3,512,128]{2,1,0:T(8,128)(2,1)S(1)} %get-tuple-element.46), channel_id=1, source_target_pairs={{0,6},{1,7},{2,0},{3,1},{4,2},{5,3},{6,4},{7,5},{8,14},{9,15},{10,... | collective-permute-start | bytes 1179656 | tf_op jit(solution)/shard_map/ppermute | solution.py:334
  128.7 22.0 %collective-permute-start.11 = (bf16[3,512,128]{2,1,0:T(8,128)(2,1)S(1)}, bf16[3,512,128]{2,1,0:T(8,128)(2,1)S(1)}, u32[]{:S(2)}, u32[]{:S(2)}) collective-permute-start(bf16[3,512,128]{2,1,0:T(8,128)(2,1)S(1)} %get-tuple-element.47), channel_id=1, source_target_pairs={{0,4},{1,5},{2,6},{3,7},{4,0},{5,1},{6,2},{7,3},{8,12},{9,13},{10,... | collective-permute-start | bytes 1179656 | tf_op jit(solution)/shard_map/ppermute | solution.py:334
  150.8 1.9 %collective-permute-start.12 = (bf16[3,512,128]{2,1,0:T(8,128)(2,1)S(1)}, bf16[3,512,128]{2,1,0:T(8,128)(2,1)S(1)}, u32[]{:S(2)}, u32[]{:S(2)}) collective-permute-start(bf16[3,512,128]{2,1,0:T(8,128)(2,1)S(1)} %get-tuple-element.48), channel_id=1, source_target_pairs={{0,2},{1,3},{2,4},{3,5},{4,6},{5,7},{6,0},{7,1},{8,10},{9,11},{10,... | collective-permute-start | bytes 1179656 | tf_op jit(solution)/shard_map/ppermute | solution.py:334
  152.7 32.0 %collective-permute-done.11.y2 = bf16[3,512,128]{2,1,0:T(8,128)(2,1)S(1)} collective-permute-done((bf16[3,512,128]{2,1,0:T(8,128)(2,1)S(1)}, bf16[3,512,128]{2,1,0:T(8,128)(2,1)S(1)}, u32[]{:S(2)}, u32[]{:S(2)}) %collective-permute-start.11) | collective-permute-done | bytes 393248 | tf_op jit(solution)/shard_map/ppermute | solution.py:334
  184.7 2.8 %join.1 = (bf16[512,1024]{1,0:T(8,128)(2,1)}, bf16[512,1024]{1,0:T(8,128)(2,1)}, bf16[512,1024]{1,0:T(8,128)(2,1)}) custom-call(s32[2]{0:T(128)S(1)} %pad_add_fusion.place, bf16[3,512,128]{2,1,0:T(8,128)(2,1)S(1)} %get-tuple-element.45.y0, bf16[3,512,128]{2,1,0:T(8,128)(2,1)S(1)} %collective-permute-done.10.y1, ...), custom_call_target="tpu_custom_call" | custom-call | tf_op jit(solution)/shard_map/join/pallas_call | solution.py:455
  (27 shorter events, 3.9 us)
Async XLA Ops:
  0.6 43.4 %collective-permute-start.4 = (bf16[1,512,2048]{2,1,0:T(8,128)(2,1)}, bf16[1,512,2048]{2,1,0:T(8,128)(2,1)}, u32[]{:S(2)}, u32[]{:S(2)}) collective-permute-start(bf16[1,512,2048]{2,1,0:T(8,128)(2,1)} %param.9), channel_id=1, source_target_pairs={{8,0},{16,8},{24,16},{0,24},{9,1},{17,9},{25,17},{1,25},{10,2},{18... | collective-permute-start | bytes 6291464 | tf_op jit(solution)/shard_map/ppermute | solution.py:469
  5.6 10.1 %copy-start.1 = (bf16[1,512,1024]{2,1,0:T(8,128)(2,1)S(1)}, bf16[1,512,1024]{2,1,0:T(8,128)(2,1)}, u32[]{:S(2)}) copy-start(bf16[1,512,1024]{2,1,0:T(8,128)(2,1)} %param.8) | copy-start | bytes 3145732
  5.6 10.1 %copy-start.2 = (bf16[1,512,1024]{2,1,0:T(8,128)(2,1)S(1)}, bf16[1,512,1024]{2,1,0:T(8,128)(2,1)}, u32[]{:S(2)}) copy-start(bf16[1,512,1024]{2,1,0:T(8,128)(2,1)} %param.7) | copy-start | bytes 3145732
  8.6 14.3 %collective-permute-start = (bf16[1552,128]{1,0:T(8,128)(2,1)}, bf16[1552,128]{1,0:T(8,128)(2,1)S(1)}, u32[]{:S(2)}, u32[]{:S(2)}) collective-permute-start(bf16[1552,128]{1,0:T(8,128)(2,1)} %pad_maximum_fusion.2), channel_id=1, source_target_pairs={{0,2},{1,3},{2,4},{3,5},{4,6},{5,7},{6,0},{7,1},{8,10},{9,11},{10,... | collective-permute-start | bytes 1191944 | tf_op jit(solution)/shard_map/ppermute | solution.py:334
  10.9 27.7 %collective-permute-start.1 = (bf16[1552,128]{1,0:T(8,128)(2,1)}, bf16[1552,128]{1,0:T(8,128)(2,1)}, u32[]{:S(2)}, u32[]{:S(2)}) collective-permute-start(bf16[1552,128]{1,0:T(8,128)(2,1)} %pad_maximum_fusion.3), channel_id=1, source_target_pairs={{0,4},{1,5},{2,6},{3,7},{4,0},{5,1},{6,2},{7,3},{8,12},{9,13},{10,... | collective-permute-start | bytes 1191944 | tf_op jit(solution)/shard_map/ppermute | solution.py:334
  14.3 24.3 %collective-permute-start.2 = (bf16[1552,128]{1,0:T(8,128)(2,1)}, bf16[1552,128]{1,0:T(8,128)(2,1)}, u32[]{:S(2)}, u32[]{:S(2)}) collective-permute-start(bf16[1552,128]{1,0:T(8,128)(2,1)} %pad_maximum_fusion.4), channel_id=1, source_target_pairs={{0,6},{1,7},{2,0},{3,1},{4,2},{5,3},{6,4},{7,5},{8,14},{9,15},{10,... | collective-permute-start | bytes 1191944 | tf_op jit(solution)/shard_map/ppermute | solution.py:334
  16.8 74.1 %collective-permute-start.13 = (bf16[2,512,512]{2,1,0:T(8,128)(2,1)}, bf16[2,512,512]{2,1,0:T(8,128)(2,1)S(1)}, u32[]{:S(2)}, u32[]{:S(2)}) collective-permute-start(bf16[2,512,512]{2,1,0:T(8,128)(2,1)} %pad_maximum_fusion), channel_id=1, source_target_pairs={{0,1},{1,2},{2,3},{3,4},{4,5},{5,6},{6,7},{8,9},{9,10},{10,11},{11... | collective-permute-start | bytes 3145736 | tf_op jit(solution)/shard_map/ppermute | solution.py:475
  42.4 27.8 %collective-permute-start.3 = (bf16[3088,128]{1,0:T(8,128)(2,1)S(1)}, bf16[3088,128]{1,0:T(8,128)(2,1)S(1)}, u32[]{:S(2)}, u32[]{:S(2)}) collective-permute-start(bf16[3088,128]{1,0:T(8,128)(2,1)S(1)} %get-tuple-element.32), channel_id=1, source_target_pairs={{0,1},{1,0},{2,3},{3,2},{4,5},{5,4},{6,7},{7,6},{8,9},{9,8},{10,11... | collective-permute-start | bytes 2371592 | tf_op jit(solution)/shard_map/ppermute | solution.py:337
  49.4 16.0 %collective-permute-start.5 = (bf16[512,128]{1,0:T(8,128)(2,1)S(1)}, bf16[512,128]{1,0:T(8,128)(2,1)S(1)}, u32[]{:S(2)}, u32[]{:S(2)}) collective-permute-start(bf16[512,128]{1,0:T(8,128)(2,1)S(1)} %get-tuple-element.57), channel_id=1, source_target_pairs={{0,2},{1,3},{2,4},{3,5},{4,6},{5,7},{6,0},{7,1},{8,10},{9,11},{10,... | collective-permute-start | bytes 393224 | tf_op jit(solution)/shard_map/ppermute | solution.py:334
  58.4 10.0 %collective-permute-start.6 = (bf16[512,128]{1,0:T(8,128)(2,1)S(1)}, bf16[512,128]{1,0:T(8,128)(2,1)S(1)}, u32[]{:S(2)}, u32[]{:S(2)}) collective-permute-start(bf16[512,128]{1,0:T(8,128)(2,1)S(1)} %get-tuple-element.56), channel_id=1, source_target_pairs={{0,4},{1,5},{2,6},{3,7},{4,0},{5,1},{6,2},{7,3},{8,12},{9,13},{10,... | collective-permute-start | bytes 393224 | tf_op jit(solution)/shard_map/ppermute | solution.py:334
  61.5 6.9 %collective-permute-start.7 = (bf16[512,128]{1,0:T(8,128)(2,1)S(1)}, bf16[512,128]{1,0:T(8,128)(2,1)S(1)}, u32[]{:S(2)}, u32[]{:S(2)}) collective-permute-start(bf16[512,128]{1,0:T(8,128)(2,1)S(1)} %get-tuple-element.55), channel_id=1, source_target_pairs={{0,6},{1,7},{2,0},{3,1},{4,2},{5,3},{6,4},{7,5},{8,14},{9,15},{10,... | collective-permute-start | bytes 393224 | tf_op jit(solution)/shard_map/ppermute | solution.py:334
  69.8 11.5 %collective-permute-start.8 = (bf16[1024,128]{1,0:T(8,128)(2,1)S(1)}, bf16[1024,128]{1,0:T(8,128)(2,1)S(1)}, u32[]{:S(2)}, u32[]{:S(2)}) collective-permute-start(bf16[1024,128]{1,0:T(8,128)(2,1)S(1)} %get-tuple-element.36), channel_id=1, source_target_pairs={{0,1},{1,0},{2,3},{3,2},{4,5},{5,4},{6,7},{7,6},{8,9},{9,8},{10,11... | collective-permute-start | bytes 786440 | tf_op jit(solution)/shard_map/ppermute | solution.py:337
  78.0 3.3 %copy-start = (bf16[2048,2048]{1,0:T(8,128)(2,1)}, bf16[2048,2048]{1,0:T(8,128)(2,1)S(1)}, u32[]{:S(2)}) copy-start(bf16[2048,2048]{1,0:T(8,128)(2,1)S(1)} %get-tuple-element.42.p_hbm) | copy-start | bytes 25165828
  81.2 9.7 %copy-start.3 = (bf16[1,512,1024]{2,1,0:T(8,128)(2,1)S(1)}, bf16[1,512,1024]{2,1,0:T(8,128)(2,1)}, u32[]{:S(2)}) copy-start(bf16[1,512,1024]{2,1,0:T(8,128)(2,1)} %param.6) | copy-start | bytes 3145732
  89.2 20.5 %collective-permute-start.9 = (bf16[3,1024,128]{2,1,0:T(8,128)(2,1)S(1)}, bf16[3,1024,128]{2,1,0:T(8,128)(2,1)S(1)}, u32[]{:S(2)}, u32[]{:S(2)}) collective-permute-start(bf16[3,1024,128]{2,1,0:T(8,128)(2,1)S(1)} %get-tuple-element.44), channel_id=1, source_target_pairs={{0,1},{1,0},{2,3},{3,2},{4,5},{5,4},{6,7},{7,6},{8,9},{9,8},{10,11... | collective-permute-start | bytes 2359304 | tf_op jit(solution)/shard_map/ppermute | solution.py:337
  100.7 52.0 %collective-permute-start.14 = (bf16[2,512,512]{2,1,0:T(8,128)(2,1)S(1)}, bf16[2,512,512]{2,1,0:T(8,128)(2,1)S(1)}, u32[]{:S(2)}, u32[]{:S(2)}) collective-permute-start(bf16[2,512,512]{2,1,0:T(8,128)(2,1)S(1)} %get-tuple-element.51), channel_id=1, source_target_pairs={{1,0},{2,1},{3,2},{4,3},{5,4},{6,5},{7,6},{9,8},{10,9},{11,10},{12... | collective-permute-start | bytes 3145736 | tf_op jit(solution)/shard_map/ppermute | solution.py:475
  113.5 39.2 %collective-permute-start.10 = (bf16[3,512,128]{2,1,0:T(8,128)(2,1)S(1)}, bf16[3,512,128]{2,1,0:T(8,128)(2,1)S(1)}, u32[]{:S(2)}, u32[]{:S(2)}) collective-permute-start(bf16[3,512,128]{2,1,0:T(8,128)(2,1)S(1)} %get-tuple-element.46), channel_id=1, source_target_pairs={{0,6},{1,7},{2,0},{3,1},{4,2},{5,3},{6,4},{7,5},{8,14},{9,15},{10,... | collective-permute-start | bytes 1179656 | tf_op jit(solution)/shard_map/ppermute | solution.py:334
  128.7 55.9 %collective-permute-start.11 = (bf16[3,512,128]{2,1,0:T(8,128)(2,1)S(1)}, bf16[3,512,128]{2,1,0:T(8,128)(2,1)S(1)}, u32[]{:S(2)}, u32[]{:S(2)}) collective-permute-start(bf16[3,512,128]{2,1,0:T(8,128)(2,1)S(1)} %get-tuple-element.47), channel_id=1, source_target_pairs={{0,4},{1,5},{2,6},{3,7},{4,0},{5,1},{6,2},{7,3},{8,12},{9,13},{10,... | collective-permute-start | bytes 1179656 | tf_op jit(solution)/shard_map/ppermute | solution.py:334
  150.8 33.9 %collective-permute-start.12 = (bf16[3,512,128]{2,1,0:T(8,128)(2,1)S(1)}, bf16[3,512,128]{2,1,0:T(8,128)(2,1)S(1)}, u32[]{:S(2)}, u32[]{:S(2)}) collective-permute-start(bf16[3,512,128]{2,1,0:T(8,128)(2,1)S(1)} %get-tuple-element.48), channel_id=1, source_target_pairs={{0,2},{1,3},{2,4},{3,5},{4,6},{5,7},{6,0},{7,1},{8,10},{9,11},{10,... | collective-permute-start | bytes 1179656 | tf_op jit(solution)/shard_map/ppermute | solution.py:334
where the time goes:
time: 188 us
  starting transfers between devices  67.8 us (36%)
  waiting for transfers between devices  63.8 us (34%)
  Pallas kernels  37.2 us (20%)
  local copies, waits for them, and re-layouts  7.58 us (4%)
  other arithmetic  5.23 us (3%)
  matrix products  5.18 us (3%)
    ppermute x9, starting transfers between devices, among_groups(): return lax.ppermute(block, 'seq', route)  56.8 us
    ppermute x9, waiting for transfers between devices, among_groups(): return lax.ppermute(block, 'seq', route)  56 us
    pallas_call x1, Pallas kernels, pair_body(): pl.pallas_call(window_kernel, grid=(HL,), out_shape=[struct(tok, HL * HD)...  9.74 us
    pallas_call x1, Pallas kernels, pair_body(): pl.pallas_call(functools.partial(grads_kernel, unit), out_shape=[struct(H...  7.95 us
    ppermute x3, waiting for transfers between devices, swap(): return lax.ppermute(block, 'seq', [(i, i ^ 1) for i in range(devices)])  7.74 us
    pallas_call x1, Pallas kernels, pair_body(): pl.pallas_call(functools.partial(probs_kernel, unit), out_shape=[struct(H...  7.72 us
    dot_general x1, matrix products, pair_body(): lax.dot_general(boundary, out_weight[0], (((1,), (1,)), ((), ())), prefer...  5.18 us
    ppermute x2, starting transfers between devices, shifted(): return lax.ppermute(block, axis, route)  4.77 us
  transfers between devices with their start and end apart: 15, of which 6 were waited for; matrix products, arithmetic and copies ran while one was open for 8% of the time, Pallas kernels for 18%

commit v1 on v0

--- a/solution.py
+++ b/solution.py
@@ -14,6 +14,7 @@
 WIN = 512
 QB = 256
 MIB = 1024 * 1024
+SPLIT_MIB = 56
 NT = (((1,), (1,)), ((), ()))
 F32 = jnp.float32
 BF16 = jnp.bfloat16
@@ -39,18 +40,97 @@
     return lax.dot_general(a, b, NT, preferred_element_type=F32)
 
 
+def takes(microseconds):
+    return pl.CostEstimate(
+        flops=int(microseconds * 1.1e9), bytes_accessed=int(microseconds * 3.5e6), transcendentals=0
+    )
+
+
 def rows(start, size):
     return pl.ds(pl.multiple_of(start, size), size)
 
 
-def pack_kernel(unit, place, x0, x1, x2, x3, sorted_ref, send_ref, slot_row, slot_col, kept_ref):
+def start_all(copies):
+    for copy in copies:
+        copy.start()
+
+
+def wait_all(copies):
+    for copy in copies:
+        copy.wait()
+
+
+def head_columns(place, d):
+    return pl.ds(pl.multiple_of(lax.rem(place[0] + d, HR) * HD, HD), HD)
+
+
+def split_kernel(place, labels, q_hbm, k_hbm, v_hbm, x0, x1, x2, x3, own, send, held, sems):
+    tok = q_hbm.shape[0]
+    copies = [pltpu.make_async_copy(source, held.at[i], sems.at[i]) for i, source in enumerate((q_hbm, k_hbm, v_hbm))]
+    start_all(copies)
+    for d, x in enumerate((x0, x1, x2, x3)):
+        line = labels[pl.ds(lax.rem(place[0] + d, HR), 1), :].astype(F32)
+        parts = [line[:, r * HD : (r + 1) * HD] for r in range(tok // HD)]
+        parts.append(jnp.zeros((16 - tok // HD, HD), F32))
+        x[2 * tok :, :] = jnp.concatenate(parts, axis=0).astype(BF16)
+    width = HL * HD // 2
+    for i in range(3):
+        copies[i].wait()
+        for d, x in enumerate((x0, x1, x2, x3)):
+            if i < 2:
+                x[i * tok : (i + 1) * tok, :] = held[i, :, head_columns(place, d)]
+        for out, side in ((send, 1 - place[1]), (own, place[1])):
+            out[i] = held[i, :, pl.ds(pl.multiple_of(HR * HD + side * width, width), width)]
+
+
+def split_value_kernel(place, _after1, _after2, _after3, v_ref, x0, x1, x2, x3):
+    for d, x in enumerate((x0, x1, x2, x3)):
+        x[...] = v_ref[:, head_columns(place, d)]
+
+
+def project_kernel(place, _after, _after_local, rows_ref, weight, g0, g1, g2, g3, own_ref, send_ref):
+    step = pl.program_id(0)
+    part = dot_nt(rows_ref[...], weight[...]).astype(BF16)
+
+    @pl.when(step < HR // 2)
+    def _():
+        for i in range(2):
+            d = lax.rem(2 * step + i - place[0] + 4, 4)
+            for e, g in enumerate((g0, g1, g2, g3)):
+
+                @pl.when(d == e)
+                def _(g=g, i=i):
+                    g[...] = part[:, i * HD : (i + 1) * HD]
+
+    @pl.when(step >= HR // 2)
+    def _():
+        @pl.when(step - HR // 2 == place[1])
+        def _():
+            own_ref[...] = part
+
+        @pl.when(step - HR // 2 != place[1])
+        def _():
+            send_ref[...] = part
+
+
+def edge_kernel(place, _after, own, got, out):
+    @pl.when(place[1] == 1)
+    def _():
+        out[...] = own[1:]
+
+    @pl.when(place[1] == 0)
+    def _():
+        out[...] = got[1:]
+
+
+def pack_kernel(unit, place, _after, x0, x1, x2, x3, sorted_ref, send_ref, slot_row, slot_col, kept_ref):
     tok = x0.shape[0] - 16
-    tok = tok // 3
+    tok = tok // 2
     side = place[1]
     lane = lax.broadcasted_iota(jnp.int32, (1, tok), 1).astype(F32)
     labels = []
     for x in (x0, x1, x2, x3):
-        block = x[3 * tok :, :].astype(F32)
+        block = x[2 * tok :, :].astype(F32)
         labels.append(jnp.concatenate([block[r : r + 1, :] for r in range(tok // 128)], axis=1))
     label = jnp.concatenate(labels + [jnp.zeros((4, tok), F32)], axis=0)
     upper = (
@@ -77,7 +157,7 @@
     row_index = lax.broadcasted_iota(jnp.int32, (tok, tok), 0).astype(F32)
     for d, x in enumerate((x0, x1, x2, x3)):
         move = (row_index == slots[d]).astype(BF16)
-        for i in range(3):
+        for i in range(2):
             sorted_ref[d, i] = dot(move, x[i * tok : (i + 1) * tok, :]).astype(BF16)
     offset = jnp.int32(0)
     info_row = lax.broadcasted_iota(jnp.int32, (16, HD), 0)
@@ -87,16 +167,16 @@
         info = jnp.where(info_row == d, kept.astype(F32), info)
 
         def put(u, carry, d=d, offset=offset, kept=kept):
-            for i in range(3):
+            for i in range(2):
                 send_ref[rows(i * half + (offset + u - kept) * unit, unit), :] = sorted_ref[d, i, rows(u * unit, unit), :]
             return carry
 
         lax.fori_loop(kept, tok // unit, put, 0)
         offset = offset + tok // unit - kept
-    send_ref[3 * half :, :] = info.astype(BF16)
-
-
-def pack_one_kernel(unit, slot_row, kept_ref, x0, x1, x2, x3, sorted_ref, send_ref):
+    send_ref[2 * half :, :] = info.astype(BF16)
+
+
+def pack_one_kernel(unit, kept_ref, _after, slot_row, x0, x1, x2, x3, sorted_ref, send_ref):
     tok = x0.shape[0]
     row_index = lax.broadcasted_iota(jnp.int32, (tok, tok), 0).astype(F32)
     for d, x in enumerate((x0, x1, x2, x3)):
@@ -140,25 +220,24 @@
         pos = pos + kept + came
 
 
-def probs_kernel(unit, place, kept_ref, sorted_ref, came_ref, got_ref, q_ref, k_ref, v_ref, kt_ref, ot_ref, p_ref, vt, s_ref):
+def probs_kernel(unit, place, kept_ref, _after, sorted_ref, came_ref, got_ref, q_ref, k_ref, kt_ref, p_ref, s_ref):
     tok = sorted_ref.shape[2]
     half = CS // 2
-    info = came_ref[3 * half :, :].astype(F32)
+    info = came_ref[2 * half :, :].astype(F32)
     for d in range(4):
         got_ref[d] = jnp.max(info[d : d + 1, :]).astype(jnp.int32)
-    outs = (q_ref, k_ref, v_ref)
+    outs = (q_ref, k_ref)
 
     def own(d, u, to):
-        for i in range(3):
+        for i in range(2):
             outs[i][rows(to * unit, unit), :] = sorted_ref[d, i, rows(u * unit, unit), :]
 
     def got(at, to):
-        for i in range(3):
+        for i in range(2):
             outs[i][rows(to * unit, unit), :] = came_ref[rows(i * half + at * unit, unit), :]
 
     each_unit(tok // unit, place, kept_ref, got_ref, own, got)
     kt_ref[...] = k_ref[...].astype(F32).T.astype(BF16)
-    vt[...] = v_ref[...].astype(F32).T.astype(BF16)
     factor = HD**-0.5
     low = lax.broadcasted_iota(jnp.int32, (QB, QB), 0) <= lax.broadcasted_iota(jnp.int32, (QB, QB), 1)
     for j in range(CS // QB):
@@ -181,24 +260,29 @@
         scale = 1.0 / jnp.sum(total, axis=0, keepdims=True)
         for i in range(j + 1):
             p_ref[i * QB : (i + 1) * QB, j * QB : (j + 1) * QB] = (s_ref[i * QB : (i + 1) * QB, :] * scale).astype(BF16)
+
+
+def mix_kernel(unit, place, kept_ref, got_ref, _after, sorted_ref, came_ref, p_ref, v_ref, ot_ref, vt):
+    def own(d, u, to):
+        v_ref[rows(to * unit, unit), :] = sorted_ref[d, rows(u * unit, unit), :]
+
+    def got(at, to):
+        v_ref[rows(to * unit, unit), :] = came_ref[rows(at * unit, unit), :]
+
+    each_unit(sorted_ref.shape[1] // unit, place, kept_ref, got_ref, own, got)
+    vt[...] = v_ref[...].astype(F32).T.astype(BF16)
+    for j in range(CS // QB):
         end = (j + 1) * QB
         ot_ref[:, j * QB : end] = dot(vt[:, :end], p_ref[:end, j * QB : end])
 
 
 def grads_kernel(
-    unit, place, kept_ref, got_ref, sorted_ref, came_ref, q_ref, k_ref, v_ref, kt_ref, ot_ref, p_hbm,
-    own_ref, back_ref, g_ref, p_ref, dqt, res, sems,
+    unit, place, kept_ref, got_ref, sorted_ref, came_ref, q_ref, k_ref, v_ref, kt_ref, ot_ref, p_ref,
+    own_v, back_v, own_ref, back_ref, g_ref, dqt, res,
 ):
     tok = sorted_ref.shape[1]
     half = CS // 2
     count = CS // QB
-    copies = []
-    for i in range(count):
-        span = (slice(i * QB, (i + 1) * QB), slice(i * QB, CS))
-        copy = pltpu.make_async_copy(p_hbm.at[span], p_ref.at[span], sems.at[i])
-        copy.start()
-        copies.append(copy)
-
     def own(d, u, to):
         g_ref[rows(to * unit, unit), :] = sorted_ref[d, rows(u * unit, unit), :]
 
@@ -209,7 +293,6 @@
     delta = jnp.sum(g_ref[...].astype(F32).T * ot_ref[...], axis=0, keepdims=True)
     factor = HD**-0.5
     for i in range(count):
-        copies[i].wait()
         lo, hi = i * QB, (i + 1) * QB
         p = p_ref[lo:hi, lo:]
         g = g_ref[lo:, :]
@@ -222,17 +305,19 @@
     res[0] = (dqt[...].T * factor).astype(BF16)
 
     def own_out(d, u, to):
-        for i in range(3):
+        own_v[d, 0, rows(u * unit, unit), :] = res[2, rows(to * unit, unit), :]
+        for i in range(2):
             own_ref[d, i, rows(u * unit, unit), :] = res[i, rows(to * unit, unit), :]
 
     def got_out(at, to):
-        for i in range(3):
+        back_v[0, rows(at * unit, unit), :] = res[2, rows(to * unit, unit), :]
+        for i in range(2):
             back_ref[i, rows(at * unit, unit), :] = res[i, rows(to * unit, unit), :]
 
     each_unit(tok // unit, place, kept_ref, got_ref, own_out, got_out)
 
 
-def unsort_kernel(unit, kept_ref, slot_col, own_ref, back_ref, y0, y1, y2, y3, full):
+def unsort_kernel(unit, kept_ref, _after, slot_col, own_ref, back_ref, y0, y1, y2, y3, full):
     tok = own_ref.shape[2]
     col_index = lax.broadcasted_iota(jnp.int32, (tok, tok), 1).astype(F32)
     offset = jnp.int32(0)
@@ -240,12 +325,12 @@
         kept = kept_ref[d]
 
         def own(u, carry, d=d):
-            for i in range(3):
+            for i in range(full.shape[0]):
                 full[i, rows(u * unit, unit), :] = own_ref[d, i, rows(u * unit, unit), :]
             return carry
 
         def got(u, carry, offset=offset, kept=kept):
-            for i in range(3):
+            for i in range(full.shape[0]):
                 full[i, rows(u * unit, unit), :] = back_ref[i, rows((offset + u - kept) * unit, unit), :]
             return carry
 
@@ -253,67 +338,96 @@
         lax.fori_loop(kept, tok // unit, got, 0)
         offset = offset + tok // unit - kept
         move = (col_index == slot_col[:, d : d + 1]).astype(BF16)
-        for i in range(3):
+        for i in range(full.shape[0]):
             y[i] = dot(move, full[i]).astype(BF16)
 
 
-def window_kernel(place, q_ref, k_ref, v_ref, g_ref, prior_ref, dq_ref, own_ref, carry_ref, keys, values, kt, dk, dv):
-    tok = q_ref.shape[0]
-    keys[:tok, :] = prior_ref[0]
-    keys[tok:, :] = k_ref[...]
-    values[:tok, :] = prior_ref[1]
-    values[tok:, :] = v_ref[...]
-    kt[...] = keys[...].astype(F32).T.astype(BF16)
+def window_kernel(
+    place, _after, own, got, g_own, g_got, edge, dq_ref, early_ref, late_ref, carry_ref, *scratch
+):
+    tok = own.shape[1]
+    pair = 2 * tok
     factor = HD**-0.5
     r = lax.broadcasted_iota(jnp.int32, (QB, QB), 0)
     c = lax.broadcasted_iota(jnp.int32, (QB, QB), 1)
-    span = tok + QB
-    edge = tok - (tok // QB - 1) * QB
+    span = WIN + QB
     started = place[0] > 0
-    for j in range(tok // QB):
-        lo, hi = j * QB, j * QB + span
-        q = q_ref[j * QB : (j + 1) * QB, :]
-        g = g_ref[j * QB : (j + 1) * QB, :]
-        s = dot_nt(keys[lo:hi, :], q) * factor
-        first = jnp.where(r > c, s[:QB], -1e30)
-        last = jnp.where(r <= c, s[span - QB :], -1e30)
-        s = jnp.concatenate([first, s[QB : span - QB], last], axis=0)
-        before = tok - lo
-        s = jnp.concatenate([jnp.where(started, s[:before], -1e30), s[before:]], axis=0)
-        top = jnp.max(s, axis=0, keepdims=True)
-        w = jnp.exp(s - top)
-        p = w * (1.0 / jnp.sum(w, axis=0, keepdims=True))
-        dp = dot_nt(values[lo:hi, :], g)
-        delta = jnp.sum(p * dp, axis=0, keepdims=True)
-        pb = p.astype(BF16)
-        ds = (p * (dp - delta)).astype(BF16)
-        dq_ref[j * QB : (j + 1) * QB, :] = (dot(kt[:, lo:hi], ds).T * factor).astype(BF16)
-        part_k = dot(ds, q) * factor
-        part_v = dot(pb, g)
-        if j == 0:
-            dk[lo:hi, :] = part_k
-            dv[lo:hi, :] = part_v
-        else:
-            dk[lo : hi - QB, :] = dk[lo : hi - QB, :] + part_k[:-QB]
-            dv[lo : hi - QB, :] = dv[lo : hi - QB, :] + part_v[:-QB]
-            dk[hi - QB : hi, :] = part_k[-QB:]
-            dv[hi - QB : hi, :] = part_v[-QB:]
-    carry_ref[0] = dk[:tok, :].astype(BF16)
-    carry_ref[1] = dv[:tok, :].astype(BF16)
-    own_ref[0] = dk[tok:, :]
-    own_ref[1] = dv[tok:, :]
-
-
-def join_kernel(place, y0, y1, y2, y3, local_dq, own_ref, carry_ref, dq_ref, dk_ref, dv_ref):
+    own_at, got_at = place[1] * tok, (1 - place[1]) * tok
+    for h in range(HL // 2):
+        part = slice(h * HD, (h + 1) * HD)
+        queries, grads, keys, values, kt, dk, dv = (ref.at[h] for ref in scratch)
+        for at, block, g_block in ((own_at, own, g_own), (got_at, got, g_got)):
+            queries[rows(at, tok), :] = block[0, :, part]
+            grads[rows(at, tok), :] = g_block[:, part]
+            keys[rows(at + WIN, tok), :] = block[1, :, part]
+            values[rows(at + WIN, tok), :] = block[2, :, part]
+        keys[:WIN, :] = edge[0, :, part]
+        values[:WIN, :] = edge[1, :, part]
+        kt[...] = keys[...].astype(F32).T.astype(BF16)
+        for j in range(pair // QB):
+            lo, hi = j * QB, j * QB + span
+            q = queries[j * QB : (j + 1) * QB, :]
+            g = grads[j * QB : (j + 1) * QB, :]
+            s = dot_nt(keys[lo:hi, :], q) * factor
+            first = jnp.where(r > c, s[:QB], -1e30)
+            last = jnp.where(r <= c, s[span - QB :], -1e30)
+            s = jnp.concatenate([first, s[QB : span - QB], last], axis=0)
+            if lo < WIN:
+                s = jnp.concatenate([jnp.where(started, s[: WIN - lo], -1e30), s[WIN - lo :]], axis=0)
+            top = jnp.max(s, axis=0, keepdims=True)
+            w = jnp.exp(s - top)
+            p = w * (1.0 / jnp.sum(w, axis=0, keepdims=True))
+            dp = dot_nt(values[lo:hi, :], g)
+            delta = jnp.sum(p * dp, axis=0, keepdims=True)
+            pb = p.astype(BF16)
+            ds = (p * (dp - delta)).astype(BF16)
+            side, at = divmod(j * QB, tok)
+            dq_ref[side, at : at + QB, part] = (dot(kt[:, lo:hi], ds).T * factor).astype(BF16)
+            part_k = dot(ds, q) * factor
+            part_v = dot(pb, g)
+            if j == 0:
+                dk[lo:hi, :] = part_k
+                dv[lo:hi, :] = part_v
+            else:
+                dk[lo : hi - QB, :] = dk[lo : hi - QB, :] + part_k[:-QB]
+                dv[lo : hi - QB, :] = dv[lo : hi - QB, :] + part_v[:-QB]
+                dk[hi - QB : hi, :] = part_k[-QB:]
+                dv[hi - QB : hi, :] = part_v[-QB:]
+        for i, total in enumerate((dk, dv)):
+            carry_ref[i, :, part] = total[:WIN, :].astype(BF16)
+            early_ref[i, :, part] = total[WIN : WIN + tok, :].astype(BF16)
+            late_ref[i, :, part] = total[WIN + tok :, :]
+
+
+def settle_kernel(place, _after, dq_ref, early_ref, late_ref, carry_ref, own, send):
+    late = (late_ref[...] + carry_ref[...].astype(F32)).astype(BF16)
+    for side, (near, far) in enumerate(((own, send), (send, own))):
+
+        @pl.when(place[1] == side)
+        def _(near=near, far=far):
+            near[0] = dq_ref[0]
+            near[1:] = early_ref[...]
+            far[0] = dq_ref[1]
+            far[1:] = late
+
+
+def join_value_kernel(place, _after, v0, v1, v2, v3, out):
+    for d, v in enumerate((v0, v1, v2, v3)):
+        out[:, head_columns(place, d)] = v[0]
+
+
+def join_kernel(place, value_ref, y0, y1, y2, y3, own, got, dq_ref, dk_ref, dv_ref):
     outs = (dq_ref, dk_ref, dv_ref)
+    dv_ref[:, : HR * HD] = value_ref[...]
     for d, y in enumerate((y0, y1, y2, y3)):
-        at = lax.rem(place[0] + d, 4) * HD
+        at = head_columns(place, d)
+        for i in range(2):
+            outs[i][:, at] = y[i]
+    width = HL * HD // 2
+    for block, side in ((own, place[1]), (got, 1 - place[1])):
+        at = pl.ds(pl.multiple_of(HR * HD + side * width, width), width)
         for i in range(3):
-            outs[i][:, pl.ds(pl.multiple_of(at, HD), HD)] = y[i]
-    side = HR * HD
-    dq_ref[:, side:] = local_dq[...]
-    dk_ref[:, side:] = (own_ref[0] + carry_ref[0].astype(F32)).astype(BF16)
-    dv_ref[:, side:] = (own_ref[1] + carry_ref[1].astype(F32)).astype(BF16)
+            outs[i][:, at] = block[i]
 
 
 def struct(*shape, dtype=BF16):
@@ -336,121 +450,195 @@
     def swap(block):
         return lax.ppermute(block, "seq", [(i, i ^ 1) for i in range(devices)])
 
+    hbm = [pl.BlockSpec(memory_space=pltpu.HBM)]
+    width = HL * HD // 2
     boundary = from_behind(grad_sent, "section", -1)[0]
-    labels = assign[0].astype(BF16).reshape(HR, tok // HD, HD)
-    labels = jnp.pad(labels, ((0, 0), (0, 16 - tok // HD), (0, 0)))
-
-    def head_of(array, head):
-        return lax.dynamic_slice_in_dim(array, head * HD, HD, 1)
-
-    sent = []
-    for d in range(HR):
-        head = (first + d) % HR
-        sent.append(
-            jnp.concatenate(
-                [head_of(query[0], head), head_of(key[0], head), head_of(value[0], head)]
-                + [lax.dynamic_index_in_dim(labels, head, 0, keepdims=False)],
-                axis=0,
-            )
-        )
+    *sent, local_own, local_send = pl.pallas_call(
+        split_kernel,
+        out_shape=[struct(2 * tok + 16, HD)] * HR + [struct(3, tok, width)] * 2,
+        in_specs=smem() + vmem() + hbm * 3,
+        out_specs=vmem(6),
+        scratch_shapes=[pltpu.VMEM((3, tok, query.shape[2]), BF16), pltpu.SemaphoreType.DMA((3,))],
+        compiler_params=params(SPLIT_MIB),
+        cost_estimate=takes(2),
+        name="split",
+    )(where, assign[0], query[0], key[0], value[0])
     arrived = [sent[0]] + [among_groups(sent[d], d) for d in range(1, HR)]
-
-    local = slice(HR * HD, (HR + HL) * HD)
-    prior = shifted(jnp.stack([key[0][:, local], value[0][:, local]]), "seq", 1)
-
-    attn_grad = lax.dot_general(
-        boundary, out_weight[0], (((1,), (1,)), ((), ())), preferred_element_type=F32
-    ).astype(BF16)
-    g_sent = [head_of(attn_grad, (first + d) % HR) for d in range(HR)]
-    g_arrived = [g_sent[0]] + [among_groups(g_sent[d], d) for d in range(1, HR)]
+    local_got = swap(local_send)
+    v_sent = pl.pallas_call(
+        split_value_kernel,
+        out_shape=[struct(tok, HD)] * HR,
+        in_specs=smem() + vmem(4),
+        out_specs=vmem(4),
+        compiler_params=params(20),
+        cost_estimate=takes(1),
+        name="split_value",
+    )(where, *arrived[1:], value[0])
+    v_arrived = [v_sent[0]] + [among_groups(v_sent[d], d) for d in range(1, HR)]
 
     ordered, send, slot_row, slot_col, kept = pl.pallas_call(
         functools.partial(pack_kernel, unit),
         out_shape=[
-            struct(HR, 3, tok, HD),
-            struct(3 * half + 16, HD),
+            struct(HR, 2, tok, HD),
+            struct(2 * half + 16, HD),
             struct(8, tok, dtype=F32),
             struct(tok, HD, dtype=F32),
             struct(HR, dtype=jnp.int32),
         ],
-        in_specs=smem() + vmem(4),
+        in_specs=smem() + vmem(5),
         out_specs=vmem(4) + smem(),
         compiler_params=params(32),
+        cost_estimate=takes(2.6),
         name="pack",
-    )(where, *arrived)
+    )(where, v_sent[0], *arrived)
     came = swap(send)
-    got, q, k, v, kt, ot, p = pl.pallas_call(
+
+    *g_sent, g_own, g_send = pl.pallas_call(
+        project_kernel,
+        grid=(4,),
+        out_shape=[struct(tok, HD)] * HR + [struct(tok, width)] * 2,
+        in_specs=smem()
+        + [
+            pl.BlockSpec((16, HD), lambda n: (0, 0)),
+            pl.BlockSpec((1, 16, HD), lambda n: (0, 0, 0)),
+            pl.BlockSpec(boundary.shape, lambda n: (0, 0)),
+            pl.BlockSpec((2 * HD, boundary.shape[1]), lambda n: (n, 0)),
+        ],
+        out_specs=[pl.BlockSpec((tok, HD), lambda n: (0, 0))] * HR
+        + [pl.BlockSpec((tok, width), lambda n: (0, 0))] * 2,
+        compiler_params=params(32),
+        cost_estimate=takes(3.8),
+        name="project",
+    )(where, send, local_got, boundary, out_weight[0])
+    g_arrived = [g_sent[0]] + [among_groups(g_sent[d], d) for d in range(1, HR)]
+
+    def pack_one(after, blocks, name):
+        return pl.pallas_call(
+            functools.partial(pack_one_kernel, unit),
+            out_shape=[struct(HR, tok, HD), struct(half, HD)],
+            in_specs=smem() + vmem(6),
+            out_specs=vmem(2),
+            compiler_params=params(20),
+            cost_estimate=takes(1.4),
+            name=name,
+        )(kept, after, slot_row, *blocks)
+
+    v_ordered, v_out = pack_one(g_sent[0], v_arrived, "pack_value")
+    v_came = swap(v_out)
+
+    got, q, k, kt, p = pl.pallas_call(
         functools.partial(probs_kernel, unit),
-        out_shape=[struct(HR, dtype=jnp.int32)]
-        + [struct(CS, HD)] * 3
-        + [struct(HD, CS), struct(HD, CS, dtype=F32), struct(CS, CS)],
-        in_specs=smem(2) + vmem(2),
-        out_specs=smem() + vmem(6),
-        scratch_shapes=[pltpu.VMEM((HD, CS), BF16), pltpu.VMEM((CS, QB), F32)],
-        compiler_params=params(40),
+        out_shape=[struct(HR, dtype=jnp.int32)] + [struct(CS, HD)] * 2 + [struct(HD, CS), struct(CS, CS)],
+        in_specs=smem(2) + vmem(3),
+        out_specs=smem() + vmem(4),
+        scratch_shapes=[pltpu.VMEM((CS, QB), F32)],
+        compiler_params=params(24),
+        cost_estimate=takes(5),
         name="probs",
-    )(where, kept, ordered, came)
-
-    g_ordered, g_out = pl.pallas_call(
-        functools.partial(pack_one_kernel, unit),
-        out_shape=[struct(HR, tok, HD), struct(half, HD)],
-        in_specs=vmem() + smem() + vmem(4),
+    )(where, kept, v_out, ordered, came)
+
+    g_ordered, g_out = pack_one(kt, g_arrived, "pack_grad")
+    g_came = swap(g_out)
+
+    edge = pl.pallas_call(
+        edge_kernel,
+        out_shape=struct(2, tok, width),
+        in_specs=smem() + vmem(3),
+        out_specs=vmem()[0],
+        compiler_params=params(16),
+        cost_estimate=takes(0.6),
+        name="edge",
+    )(where, g_out, local_own, local_got)
+    edge_got = lax.ppermute(edge, "seq", [(i, i + 2) for i in range(devices - 2)])
+    g_got = swap(g_send)
+
+    v, ot = pl.pallas_call(
+        functools.partial(mix_kernel, unit),
+        out_shape=[struct(CS, HD), struct(HD, CS, dtype=F32)],
+        in_specs=smem(3) + vmem(4),
         out_specs=vmem(2),
-        compiler_params=params(32),
-        name="pack_grad",
-    )(slot_row, kept, *g_arrived)
-    g_came = swap(g_out)
-
-    own, back = pl.pallas_call(
+        scratch_shapes=[pltpu.VMEM((HD, CS), BF16)],
+        compiler_params=params(20),
+        cost_estimate=takes(1.7),
+        name="mix",
+    )(where, kept, got, edge, v_ordered, v_came, p)
+
+    own_v, back_v, own, back = pl.pallas_call(
         functools.partial(grads_kernel, unit),
-        out_shape=[struct(HR, 3, tok, HD), struct(3, half, HD)],
-        in_specs=smem(3) + vmem(7) + [pl.BlockSpec(memory_space=pl.ANY)],
-        out_specs=vmem(2),
+        out_shape=[struct(HR, 1, tok, HD), struct(1, half, HD), struct(HR, 2, tok, HD), struct(2, half, HD)],
+        in_specs=smem(3) + vmem(8),
+        out_specs=vmem(4),
         scratch_shapes=[
             pltpu.VMEM((CS, HD), BF16),
-            pltpu.VMEM((CS, CS), BF16),
             pltpu.VMEM((HD, CS), F32),
             pltpu.VMEM((3, CS, HD), BF16),
-            pltpu.SemaphoreType.DMA((CS // QB,)),
         ],
-        compiler_params=params(40),
+        compiler_params=params(24),
+        cost_estimate=takes(6.3),
         name="grads",
     )(where, kept, got, g_ordered, g_came, q, k, v, kt, ot, p)
-    returned = swap(back)
-    natural = pl.pallas_call(
-        functools.partial(unsort_kernel, unit),
-        out_shape=[struct(3, tok, HD)] * 4,
-        in_specs=smem() + vmem(3),
+
+    def bring_home(after, own, back, name):
+        count = own.shape[1]
+        returned = swap(back)
+        natural = pl.pallas_call(
+            functools.partial(unsort_kernel, unit),
+            out_shape=[struct(count, tok, HD)] * HR,
+            in_specs=smem() + vmem(4),
+            out_specs=vmem(4),
+            scratch_shapes=[pltpu.VMEM((count, tok, HD), BF16)],
+            compiler_params=params(32),
+        cost_estimate=takes(2),
+            name=name,
+        )(kept, after, slot_col, own, returned)
+        return [natural[0]] + [among_groups(natural[d], -d) for d in range(1, HR)]
+
+    pair = 2 * tok
+    dq_local, early, late, carry = pl.pallas_call(
+        window_kernel,
+        out_shape=[
+            struct(2, tok, width),
+            struct(2, tok, width),
+            struct(2, tok, width, dtype=F32),
+            struct(2, tok, width),
+        ],
+        in_specs=smem() + vmem(6),
         out_specs=vmem(4),
-        scratch_shapes=[pltpu.VMEM((3, tok, HD), BF16)],
-        compiler_params=params(32),
-        name="unsort",
-    )(kept, slot_col, own, returned)
-    home = [natural[0]] + [among_groups(natural[d], -d) for d in range(1, HR)]
-
-    local_dq, local_own, carry = pl.pallas_call(
-        window_kernel,
-        grid=(HL,),
-        out_shape=[struct(tok, HL * HD), struct(2, tok, HL * HD, dtype=F32), struct(2, tok, HL * HD)],
-        in_specs=smem()
-        + [pl.BlockSpec((tok, HD), lambda h: (0, HR + h))] * 4
-        + [pl.BlockSpec((2, tok, HD), lambda h: (0, 0, h))],
-        out_specs=[
-            pl.BlockSpec((tok, HD), lambda h: (0, h)),
-            pl.BlockSpec((2, tok, HD), lambda h: (0, 0, h)),
-            pl.BlockSpec((2, tok, HD), lambda h: (0, 0, h)),
+        scratch_shapes=[
+            pltpu.VMEM((HL // 2, pair, HD), BF16),
+            pltpu.VMEM((HL // 2, pair, HD), BF16),
+            pltpu.VMEM((HL // 2, pair + WIN, HD), BF16),
+            pltpu.VMEM((HL // 2, pair + WIN, HD), BF16),
+            pltpu.VMEM((HL // 2, HD, pair + WIN), BF16),
+            pltpu.VMEM((HL // 2, pair + WIN, HD), F32),
+            pltpu.VMEM((HL // 2, pair + WIN, HD), F32),
         ],
-        scratch_shapes=[
-            pltpu.VMEM((2 * tok, HD), BF16),
-            pltpu.VMEM((2 * tok, HD), BF16),
-            pltpu.VMEM((HD, 2 * tok), BF16),
-            pltpu.VMEM((2 * tok, HD), F32),
-            pltpu.VMEM((2 * tok, HD), F32),
-        ],
-        compiler_params=params(32),
+        compiler_params=params(24),
+        cost_estimate=takes(7.8),
         name="window",
-    )(place.astype(jnp.int32).reshape(1), query[0], key[0], value[0], attn_grad, prior)
-    carried = shifted(carry, "seq", -1)
+    )(where, back_v, local_own, local_got, g_own, g_got, edge_got)
+    carry_got = lax.ppermute(carry, "seq", [(i + 2, i) for i in range(devices - 2)])
+    home_v = bring_home(carry, own_v, back_v, "unsort_value")
+    home = bring_home(home_v[0], own, back, "unsort_query_key")
+    settled_own, settled_send = pl.pallas_call(
+        settle_kernel,
+        out_shape=[struct(3, tok, width)] * 2,
+        in_specs=smem() + vmem(5),
+        out_specs=vmem(2),
+        compiler_params=params(16),
+        cost_estimate=takes(0.8),
+        name="settle",
+    )(where, home[0], dq_local, early, late, carry_got)
+    settled_got = swap(settled_send)
+    value_left = pl.pallas_call(
+        join_value_kernel,
+        out_shape=struct(tok, HR * HD),
+        in_specs=smem() + vmem(5),
+        out_specs=vmem()[0],
+        compiler_params=params(16),
+        cost_estimate=takes(0.7),
+        name="join_value",
+    )(where, settled_send, *home_v)
 
     outs = pl.pallas_call(
         join_kernel,
@@ -458,8 +646,9 @@
         in_specs=smem() + vmem(7),
         out_specs=vmem(3),
         compiler_params=params(32),
+        cost_estimate=takes(2.8),
         name="join",
-    )(where, *home, local_dq, local_own, carried)
+    )(where, value_left, *home, settled_own, settled_got)
     return tuple(out[None] for out in outs)
 
 

time: 188 us -> 139 us (0.74)
  starting transfers between devices: 67.8 us -> 46 us
  waiting for transfers between devices: 63.8 us -> 45.1 us
  Pallas kernels: 37.2 us -> 45.1 us
  local copies, waits for them, and re-layouts: 7.58 us -> 0.97 us
  matrix products: 5.18 us -> 0 us
  other arithmetic: 5.23 us -> 0.61 us
    ppermute x9 -> x15, starting transfers between devices: 56.8 us -> 31.7 us  [among_groups(): return lax.ppermute(block, 'seq', route)]
    ppermute x9 -> x15, waiting for transfers between devices: 56 us -> 34.7 us  [among_groups(): return lax.ppermute(block, 'seq', route)]
    pallas_call x3 -> x12, Pallas kernels: 14.9 us -> 28.2 us  [the longest x1 7.76 us: pair_body(): pl.pallas_call(window_kernel, out_shape=[struct(2, tok, width), struct(2,...]
    ppermute x3 -> x8, starting transfers between devices: 3.75 us -> 9.21 us  [swap(): return lax.ppermute(block, 'seq', [(i, i ^ 1) for i in range(devices)])]
    dot_general x1 -> x0, matrix products: 5.18 us -> none  [pair_body(): lax.dot_general(boundary, out_weight[0], (((1,), (1,)), ((), ())), prefer...]
    dynamic_slice x3 -> x0, local copies, waits for them, and re-layouts: 4.18 us -> none  [head_of(): return lax.dynamic_slice_in_dim(array, head * HD, HD, 1)]
    concatenate x4 -> x0, other arithmetic: 3.39 us -> none  [pair_body(): jnp.concatenate([head_of(query[0], head), head_of(key[0], head), head_of(...]
    ppermute x2, waiting for transfers between devices: 0.01 us -> 3.25 us  [the longest x1 3.24 us: pair_body(): lax.ppermute(carry, 'seq', [(i + 2, i) for i in range(devices - 2)])]
  transfers between devices with their start and end apart: 15 -> 26, of which waited for: 6 -> 10; matrix products, arithmetic and copies ran while one was open for 8% -> 0% of each run, Pallas kernels for 18% -> 30%
where the time goes in v1:
time: 139 us
  starting transfers between devices  46 us (33%)
  Pallas kernels  45.1 us (32%)
  waiting for transfers between devices  45.1 us (32%)
    ppermute x15, waiting for transfers between devices, among_groups(): return lax.ppermute(block, 'seq', route)  34.7 us
    ppermute x15, starting transfers between devices, among_groups(): return lax.ppermute(block, 'seq', route)  31.7 us
    ppermute x8, starting transfers between devices, swap(): return lax.ppermute(block, 'seq', [(i, i ^ 1) for i in range(devices)])  9.21 us
    pallas_call x1, Pallas kernels, pair_body(): pl.pallas_call(window_kernel, out_shape=[struct(2, tok, width), struct(2,...  7.76 us
    ppermute x8, waiting for transfers between devices, swap(): return lax.ppermute(block, 'seq', [(i, i ^ 1) for i in range(devices)])  7.14 us
    pallas_call x1, Pallas kernels, pair_body(): pl.pallas_call(functools.partial(grads_kernel, unit), out_shape=[struct(H...  6.39 us
    pallas_call x2, Pallas kernels, bring_home(): pl.pallas_call(functools.partial(unsort_kernel, unit), out_shape=[struct(...  5.29 us
    pallas_call x1, Pallas kernels, pair_body(): pl.pallas_call(functools.partial(probs_kernel, unit), out_shape=[struct(H...  5.1 us
  transfers between devices with their start and end apart: 26, of which 10 were waited for; matrix products, arithmetic and copies ran while one was open for 0% of the time, Pallas kernels for 30%

profile of v1, /device:TPU:0, one launch (start us, length us, event | category | flops | bytes accessed | tf_op | source)
XLA Modules:
  0.0 138.6 jit_solution(2682531116048783786)
XLA Ops:
  0.6 2.4 %collective-permute-start.4 = (bf16[1,512,2048]{2,1,0:T(8,128)(2,1)}, bf16[1,512,2048]{2,1,0:T(8,128)(2,1)S(1)}, u32[]{:S(2)}, u32[]{:S(2)}) collective-permute-start(bf16[1,512,2048]{2,1,0:T(8,128)(2,1)} %param.9), channel_id=1, source_target_pairs={{8,0},{16,8},{24,16},{0,24},{9,1},{17,9},{25,17},{1,25},{10,2},{18... | collective-permute-start | bytes 6291464 | tf_op jit(solution)/shard_map/ppermute | solution.py:658
  3.7 4.1 %split.1 = (bf16[1040,128]{1,0:T(8,128)(2,1)}, bf16[1040,128]{1,0:T(8,128)(2,1)}, bf16[1040,128]{1,0:T(8,128)(2,1)}, bf16[1040,128]{1,0:T(8,128)(2,1)}, bf16[3,5...) custom-call(s32[2]{0:T(128)} %pad_add_fusion.place, s32[4,512]{1,0:T(4,128)} %bitcast.17, bf16[512,1024]{1,0:T(8,128)(2,1)} %bitcast.15, ...), custom_call_target="tpu_custom_call" | custom-call | flops 2200000000 | bytes 7000000 | tf_op jit(solution)/shard_map/split/pallas_call | solution.py:456
  7.8 1.6 %collective-permute-start.3 = (bf16[3,512,256]{2,1,0:T(8,128)(2,1)}, bf16[3,512,256]{2,1,0:T(8,128)(2,1)S(1)}, u32[]{:S(2)}, u32[]{:S(2)}) collective-permute-start(bf16[3,512,256]{2,1,0:T(8,128)(2,1)} %get-tuple-element.63), channel_id=1, source_target_pairs={{0,1},{1,0},{2,3},{3,2},{4,5},{5,4},{6,7},{7,6},{8,9},{9,8},{10,11... | collective-permute-start | bytes 2359304 | tf_op jit(solution)/shard_map/ppermute | solution.py:451
  9.4 1.6 %collective-permute-start = (bf16[1040,128]{1,0:T(8,128)(2,1)}, bf16[1040,128]{1,0:T(8,128)(2,1)S(1)}, u32[]{:S(2)}, u32[]{:S(2)}) collective-permute-start(bf16[1040,128]{1,0:T(8,128)(2,1)} %get-tuple-element.56), channel_id=1, source_target_pairs={{0,2},{1,3},{2,4},{3,5},{4,6},{5,7},{6,0},{7,1},{8,10},{9,11},{10,... | collective-permute-start | bytes 798728 | tf_op jit(solution)/shard_map/ppermute | solution.py:448
  11.0 2.6 %collective-permute-start.1 = (bf16[1040,128]{1,0:T(8,128)(2,1)}, bf16[1040,128]{1,0:T(8,128)(2,1)S(1)}, u32[]{:S(2)}, u32[]{:S(2)}) collective-permute-start(bf16[1040,128]{1,0:T(8,128)(2,1)} %get-tuple-element.57), channel_id=1, source_target_pairs={{0,4},{1,5},{2,6},{3,7},{4,0},{5,1},{6,2},{7,3},{8,12},{9,13},{10,... | collective-permute-start | bytes 798728 | tf_op jit(solution)/shard_map/ppermute | solution.py:448
  13.6 1.3 collective-permute-start.2
  14.9 6.0 %collective-permute-done._after1.x1 = bf16[1040,128]{1,0:T(8,128)(2,1)S(1)} collective-permute-done((bf16[1040,128]{1,0:T(8,128)(2,1)}, bf16[1040,128]{1,0:T(8,128)(2,1)S(1)}, u32[]{:S(2)}, u32[]{:S(2)}) %collective-permute-start) | collective-permute-done | bytes 266272 | tf_op jit(solution)/shard_map/ppermute | solution.py:448
  20.9 9.7 %collective-permute-done.1._after2.x2 = bf16[1040,128]{1,0:T(8,128)(2,1)S(1)} collective-permute-done((bf16[1040,128]{1,0:T(8,128)(2,1)}, bf16[1040,128]{1,0:T(8,128)(2,1)S(1)}, u32[]{:S(2)}, u32[]{:S(2)}) %collective-permute-start.1) | collective-permute-done | bytes 266272 | tf_op jit(solution)/shard_map/ppermute | solution.py:448
  31.3 6.2 %collective-permute-start.5 = (bf16[512,128]{1,0:T(8,128)(2,1)S(1)}, bf16[512,128]{1,0:T(8,128)(2,1)S(1)}, u32[]{:S(2)}, u32[]{:S(2)}) collective-permute-start(bf16[512,128]{1,0:T(8,128)(2,1)S(1)} %get-tuple-element.66), channel_id=1, source_target_pairs={{0,2},{1,3},{2,4},{3,5},{4,6},{5,7},{6,0},{7,1},{8,10},{9,11},{10,... | collective-permute-start | bytes 393224 | tf_op jit(solution)/shard_map/ppermute | solution.py:448
  37.5 1.6 %collective-permute-start.6 = (bf16[512,128]{1,0:T(8,128)(2,1)S(1)}, bf16[512,128]{1,0:T(8,128)(2,1)S(1)}, u32[]{:S(2)}, u32[]{:S(2)}) collective-permute-start(bf16[512,128]{1,0:T(8,128)(2,1)S(1)} %get-tuple-element.67), channel_id=1, source_target_pairs={{0,4},{1,5},{2,6},{3,7},{4,0},{5,1},{6,2},{7,3},{8,12},{9,13},{10,... | collective-permute-start | bytes 393224 | tf_op jit(solution)/shard_map/ppermute | solution.py:448
  40.9 2.7 %pack.1 = (bf16[4,2,512,128]{3,2,1,0:T(8,128)(2,1)S(1)}, bf16[2064,128]{1,0:T(8,128)(2,1)S(1)}, f32[8,512]{1,0:T(8,128)S(1)}, f32[512,128]{1,0:T(8,128)S(1)}, s32[4]{0:T(128)S(1)}) custom-call(s32[2]{0:T(128)S(1)} %copy-done, bf16[512,128]{1,0:T(8,128)(2,1)S(1)} %get-tuple-element.59._after.x0, bf16[1040,128]{1,0:T(8,128)(2,1)S(1)} %copy-done.4, ...), custom_call_target="tpu_custom_call" | custom-call | flops 2860000000 | bytes 9100000 | tf_op jit(solution)/shard_map/pack/pallas_call | solution.py:479
  44.2 3.8 %project.1 = (bf16[512,128]{1,0:T(8,128)(2,1)S(1)}, bf16[512,128]{1,0:T(8,128)(2,1)S(1)}, bf16[512,128]{1,0:T(8,128)(2,1)S(1)}, bf16[512,128]{1,0:T(8,128)(2,1)S...) custom-call(s32[2]{0:T(128)S(1)} %copy-done, bf16[2064,128]{1,0:T(8,128)(2,1)S(1)} %get-tuple-element.62._after, ...), custom_call_target="tpu_custom_call" | custom-call | flops 4180000000 | bytes 13300000 | tf_op jit(solution)/shard_map/project/pallas_call | solution.py:496
  50.5 2.1 %collective-permute-start.11 = (bf16[512,128]{1,0:T(8,128)(2,1)S(1)}, bf16[512,128]{1,0:T(8,128)(2,1)S(1)}, u32[]{:S(2)}, u32[]{:S(2)}) collective-permute-start(bf16[512,128]{1,0:T(8,128)(2,1)S(1)} %get-tuple-element.75), channel_id=1, source_target_pairs={{0,6},{1,7},{2,0},{3,1},{4,2},{5,3},{6,4},{7,5},{8,14},{9,15},{10,... | collective-permute-start | bytes 393224 | tf_op jit(solution)/shard_map/ppermute | solution.py:448
  52.6 1.4 pack_value.1
  54.9 3.7 %collective-permute-done.8.came_ref = bf16[2064,128]{1,0:T(8,128)(2,1)S(1)} collective-permute-done((bf16[2064,128]{1,0:T(8,128)(2,1)S(1)}, bf16[2064,128]{1,0:T(8,128)(2,1)S(1)}, u32[]{:S(2)}, u32[]{:S(2)}) %collective-permute-start.8) | collective-permute-done | bytes 528416 | tf_op jit(solution)/shard_map/ppermute | solution.py:451
  58.6 5.1 %probs.1 = (s32[4]{0:T(128)S(1)}, bf16[2048,128]{1,0:T(8,128)(2,1)S(1)}, bf16[2048,128]{1,0:T(8,128)(2,1)S(1)}, bf16[128,2048]{1,0:T(8,128)(2,1)S(1)}, bf16[2048,2048]{1,0:T(8,128)(2,1)S(1)}) custom-call(s32[2]{0:T(128)S(1)} %copy-done, s32[4]{0:T(128)S(1)} %get-tuple-element.61.kept_ref, bf16[1024,128]{1,0:T(8,128)(2,1)S(1)} %get-tuple-element.69._after, ...), custom_call_target="tpu_custom_call" | custom-call | flops 5500000256 | bytes 17500000 | tf_op jit(solution)/shard_map/probs/pallas_call | solution.py:529
  63.8 1.4 pack_grad.1
  65.5 1.8 %collective-permute-start.14 = (bf16[512,256]{1,0:T(8,128)(2,1)S(1)}, bf16[512,256]{1,0:T(8,128)(2,1)S(1)}, u32[]{:S(2)}, u32[]{:S(2)}) collective-permute-start(bf16[512,256]{1,0:T(8,128)(2,1)S(1)} %get-tuple-element.87), channel_id=1, source_target_pairs={{0,1},{1,0},{2,3},{3,2},{4,5},{5,4},{6,7},{7,6},{8,9},{9,8},{10,11... | collective-permute-start | bytes 786440 | tf_op jit(solution)/shard_map/ppermute | solution.py:451
  69.2 1.7 %mix.1 = (bf16[2048,128]{1,0:T(8,128)(2,1)S(1)}, f32[128,2048]{1,0:T(8,128)S(1)}) custom-call(s32[2]{0:T(128)S(1)} %copy-done, s32[4]{0:T(128)S(1)} %get-tuple-element.61.kept_ref, s32[4]{0:T(128)S(1)} %get-tuple-element.71.got_ref, bf16[2,512,256]{2,1,0:T(8,128)(2,1)S(1)} %edge.1._after, bf16[4,512,128]{2,1,0:T(8,128)(2,1)S(1)} %get-tuple-element.81.sorted_ref, ...), custom_call_target="tpu_custom_call" | custom-call | flops 1870000000 | bytes 5950000 | tf_op jit(solution)/shard_map/mix/pallas_call | solution.py:555
  70.9 2.2 %collective-permute-done.12.came_ref = bf16[1024,128]{1,0:T(8,128)(2,1)S(1)} collective-permute-done((bf16[1024,128]{1,0:T(8,128)(2,1)S(1)}, bf16[1024,128]{1,0:T(8,128)(2,1)S(1)}, u32[]{:S(2)}, u32[]{:S(2)}) %collective-permute-start.12) | collective-permute-done | bytes 262176 | tf_op jit(solution)/shard_map/ppermute | solution.py:451
  73.1 6.4 %grads.1 = (bf16[4,1,512,128]{3,2,1,0:T(8,128)(2,1)S(1)}, bf16[1,1024,128]{2,1,0:T(8,128)(2,1)S(1)}, bf16[4,2,512,128]{3,2,1,0:T(8,128)(2,1)S(1)}, bf16[2,1024,128]{2,1,0:T(8,128)(2,1)S(1)}) custom-call(s32[2]{0:T(128)S(1)} %copy-done, s32[4]{0:T(128)S(1)} %get-tuple-element.61.kept_ref, s32[4]{0:T(128)S(1)} %get-tuple-element.71.got_ref, ...), custom_call_target="tpu_custom_call" | custom-call | flops 6929999872 | bytes 22050000 | tf_op jit(solution)/shard_map/grads/pallas_call | solution.py:566
  80.1 1.5 %collective-permute-start.17 = (bf16[2,1024,128]{2,1,0:T(8,128)(2,1)S(1)}, bf16[2,1024,128]{2,1,0:T(8,128)(2,1)S(1)}, u32[]{:S(2)}, u32[]{:S(2)}) collective-permute-start(bf16[2,1024,128]{2,1,0:T(8,128)(2,1)S(1)} %get-tuple-element.93), channel_id=1, source_target_pairs={{0,1},{1,0},{2,3},{3,2},{4,5},{5,4},{6,7},{7,6},{8,9},{9,8},{10,11... | collective-permute-start | bytes 1572872 | tf_op jit(solution)/shard_map/ppermute | solution.py:451
  81.6 7.8 %window.1 = (bf16[2,512,256]{2,1,0:T(8,128)(2,1)S(1)}, bf16[2,512,256]{2,1,0:T(8,128)(2,1)S(1)}, f32[2,512,256]{2,1,0:T(8,128)S(1)}, bf16[2,512,256]{2,1,0:T(8,128)(2,1)S(1)}) custom-call(s32[2]{0:T(128)S(1)} %copy-done, bf16[1,1024,128]{2,1,0:T(8,128)(2,1)S(1)} %get-tuple-element.85._after, bf16[3,512,256]{2,1,0:T(8,128)(2,1)S(1)} %copy-done.3, ...), custom_call_target="tpu_custom_call" | custom-call | flops 8579999744 | bytes 27300000 | tf_op jit(solution)/shard_map/window/pallas_call | solution.py:597
  90.7 2.6 %unsort_value.1 = (bf16[1,512,128]{2,1,0:T(8,128)(2,1)S(1)}, bf16[1,512,128]{2,1,0:T(8,128)(2,1)S(1)}, bf16[1,512,128]{2,1,0:T(8,128)(2,1)S(1)}, bf16[1,512,128]{2,1,0:T(8,128)(2,1)S(1)}) custom-call(s32[4]{0:T(128)S(1)} %get-tuple-element.61.kept_ref, bf16[2,512,256]{2,1,0:T(8,128)(2,1)S(1)} %get-tuple-element.88._after, ...), custom_call_target="tpu_custom_call" | custom-call | flops 2200000000 | bytes 7000000 | tf_op jit(solution)/shard_map/unsort_value/pallas_call | solution.py:584
  94.5 2.7 %unsort_query_key.1 = (bf16[2,512,128]{2,1,0:T(8,128)(2,1)S(1)}, bf16[2,512,128]{2,1,0:T(8,128)(2,1)S(1)}, bf16[2,512,128]{2,1,0:T(8,128)(2,1)S(1)}, bf16[2,512,128]{2,1,0:T(8,128)(2,1)S(1)}) custom-call(s32[4]{0:T(128)S(1)} %get-tuple-element.61.kept_ref, bf16[1,512,128]{2,1,0:T(8,128)(2,1)S(1)} %get-tuple-element.91._after.v0, ...), custom_call_target="tpu_custom_call" | custom-call | flops 2200000000 | bytes 7000000 | tf_op jit(solution)/shard_map/unsort_query_key/pallas_call | solution.py:584
  97.2 3.2 %collective-permute-done.18.carry_ref = bf16[2,512,256]{2,1,0:T(8,128)(2,1)S(1)} collective-permute-done((bf16[2,512,256]{2,1,0:T(8,128)(2,1)S(1)}, bf16[2,512,256]{2,1,0:T(8,128)(2,1)S(1)}, u32[]{:S(2)}, u32[]{:S(2)}) %collective-permute-start.18) | collective-permute-done | bytes 524320 | tf_op jit(solution)/shard_map/ppermute | solution.py:620
  101.3 2.0 %collective-permute-start.25 = (bf16[3,512,256]{2,1,0:T(8,128)(2,1)S(1)}, bf16[3,512,256]{2,1,0:T(8,128)(2,1)S(1)}, u32[]{:S(2)}, u32[]{:S(2)}) collective-permute-start(bf16[3,512,256]{2,1,0:T(8,128)(2,1)S(1)} %get-tuple-element.98._after), channel_id=1, source_target_pairs={{0,1},{1,0},{2,3},{3,2},{4,5},{5,4},{6,7},{7,6},{8,9},{9,8},{10,11... | collective-permute-start | bytes 2359304 | tf_op jit(solution)/shard_map/ppermute | solution.py:451
  103.7 2.7 %collective-permute-start.20 = (bf16[1,512,128]{2,1,0:T(8,128)(2,1)S(1)}, bf16[1,512,128]{2,1,0:T(8,128)(2,1)S(1)}, u32[]{:S(2)}, u32[]{:S(2)}) collective-permute-start(bf16[1,512,128]{2,1,0:T(8,128)(2,1)S(1)} %get-tuple-element.100), channel_id=1, source_target_pairs={{0,4},{1,5},{2,6},{3,7},{4,0},{5,1},{6,2},{7,3},{8,12},{9,13},{10,... | collective-permute-start | bytes 393224 | tf_op jit(solution)/shard_map/ppermute | solution.py:448
  109.2 7.9 %collective-permute-start.24 = (bf16[2,512,128]{2,1,0:T(8,128)(2,1)S(1)}, bf16[2,512,128]{2,1,0:T(8,128)(2,1)S(1)}, u32[]{:S(2)}, u32[]{:S(2)}) collective-permute-start(bf16[2,512,128]{2,1,0:T(8,128)(2,1)S(1)} %get-tuple-element.104), channel_id=1, source_target_pairs={{0,2},{1,3},{2,4},{3,5},{4,6},{5,7},{6,0},{7,1},{8,10},{9,11},{10,... | collective-permute-start | bytes 786440 | tf_op jit(solution)/shard_map/ppermute | solution.py:448
  117.1 10.0 %collective-permute-done.20.v2 = bf16[1,512,128]{2,1,0:T(8,128)(2,1)S(1)} collective-permute-done((bf16[1,512,128]{2,1,0:T(8,128)(2,1)S(1)}, bf16[1,512,128]{2,1,0:T(8,128)(2,1)S(1)}, u32[]{:S(2)}, u32[]{:S(2)}) %collective-permute-start.20) | collective-permute-done | bytes 131104 | tf_op jit(solution)/shard_map/ppermute | solution.py:448
  127.1 6.9 %collective-permute-done.21.v3 = bf16[1,512,128]{2,1,0:T(8,128)(2,1)S(1)} collective-permute-done((bf16[1,512,128]{2,1,0:T(8,128)(2,1)S(1)}, bf16[1,512,128]{2,1,0:T(8,128)(2,1)S(1)}, u32[]{:S(2)}, u32[]{:S(2)}) %collective-permute-start.21) | collective-permute-done | bytes 131104 | tf_op jit(solution)/shard_map/ppermute | solution.py:448
  135.8 2.8 %join.1 = (bf16[512,1024]{1,0:T(8,128)(2,1)}, bf16[512,1024]{1,0:T(8,128)(2,1)}, bf16[512,1024]{1,0:T(8,128)(2,1)}) custom-call(s32[2]{0:T(128)S(1)} %copy-done, bf16[512,512]{1,0:T(8,128)(2,1)S(1)} %join_value.1.value_ref, bf16[2,512,128]{2,1,0:T(8,128)(2,1)S(1)} %get-tuple-element.94._after.y0, bf16[2,512,128]{2,1,0:T(8,128)(2,1)S(1)} %collective-permute-done.22.y1, ...), custom_call_target="tpu_custom_call" | custom-call | flops 3080000000 | bytes 9800000 | tf_op jit(solution)/shard_map/join/pallas_call | solution.py:643
  (47 shorter events, 18.4 us)
Async XLA Ops:
  0.6 30.0 %copy-start.2 = (bf16[1,512,1024]{2,1,0:T(8,128)(2,1)S(1)}, bf16[1,512,1024]{2,1,0:T(8,128)(2,1)}, u32[]{:S(2)}) copy-start(bf16[1,512,1024]{2,1,0:T(8,128)(2,1)} %param.8) | copy-start | bytes 3145732
  0.6 43.5 %collective-permute-start.4 = (bf16[1,512,2048]{2,1,0:T(8,128)(2,1)}, bf16[1,512,2048]{2,1,0:T(8,128)(2,1)S(1)}, u32[]{:S(2)}, u32[]{:S(2)}) collective-permute-start(bf16[1,512,2048]{2,1,0:T(8,128)(2,1)} %param.9), channel_id=1, source_target_pairs={{8,0},{16,8},{24,16},{0,24},{9,1},{17,9},{25,17},{1,25},{10,2},{18... | collective-permute-start | bytes 6291464 | tf_op jit(solution)/shard_map/ppermute | solution.py:658
  3.7 26.9 %copy-start = (s32[2]{0:T(128)S(1)}, s32[2]{0:T(128)}, u32[]{:S(2)}) copy-start(s32[2]{0:T(128)} %pad_add_fusion.place) | copy-start | bytes 28
  7.8 35.8 %collective-permute-start.3 = (bf16[3,512,256]{2,1,0:T(8,128)(2,1)}, bf16[3,512,256]{2,1,0:T(8,128)(2,1)S(1)}, u32[]{:S(2)}, u32[]{:S(2)}) collective-permute-start(bf16[3,512,256]{2,1,0:T(8,128)(2,1)} %get-tuple-element.63), channel_id=1, source_target_pairs={{0,1},{1,0},{2,3},{3,2},{4,5},{5,4},{6,7},{7,6},{8,9},{9,8},{10,11... | collective-permute-start | bytes 2359304 | tf_op jit(solution)/shard_map/ppermute | solution.py:451
  9.4 11.5 %collective-permute-start = (bf16[1040,128]{1,0:T(8,128)(2,1)}, bf16[1040,128]{1,0:T(8,128)(2,1)S(1)}, u32[]{:S(2)}, u32[]{:S(2)}) collective-permute-start(bf16[1040,128]{1,0:T(8,128)(2,1)} %get-tuple-element.56), channel_id=1, source_target_pairs={{0,2},{1,3},{2,4},{3,5},{4,6},{5,7},{6,0},{7,1},{8,10},{9,11},{10,... | collective-permute-start | bytes 798728 | tf_op jit(solution)/shard_map/ppermute | solution.py:448
  11.0 19.6 %collective-permute-start.1 = (bf16[1040,128]{1,0:T(8,128)(2,1)}, bf16[1040,128]{1,0:T(8,128)(2,1)S(1)}, u32[]{:S(2)}, u32[]{:S(2)}) collective-permute-start(bf16[1040,128]{1,0:T(8,128)(2,1)} %get-tuple-element.57), channel_id=1, source_target_pairs={{0,4},{1,5},{2,6},{3,7},{4,0},{5,1},{6,2},{7,3},{8,12},{9,13},{10,... | collective-permute-start | bytes 798728 | tf_op jit(solution)/shard_map/ppermute | solution.py:448
  13.6 17.1 %collective-permute-start.2 = (bf16[1040,128]{1,0:T(8,128)(2,1)}, bf16[1040,128]{1,0:T(8,128)(2,1)S(1)}, u32[]{:S(2)}, u32[]{:S(2)}) collective-permute-start(bf16[1040,128]{1,0:T(8,128)(2,1)} %get-tuple-element.58), channel_id=1, source_target_pairs={{0,6},{1,7},{2,0},{3,1},{4,2},{5,3},{6,4},{7,5},{8,14},{9,15},{10,... | collective-permute-start | bytes 798728 | tf_op jit(solution)/shard_map/ppermute | solution.py:448
  31.3 17.9 %collective-permute-start.5 = (bf16[512,128]{1,0:T(8,128)(2,1)S(1)}, bf16[512,128]{1,0:T(8,128)(2,1)S(1)}, u32[]{:S(2)}, u32[]{:S(2)}) collective-permute-start(bf16[512,128]{1,0:T(8,128)(2,1)S(1)} %get-tuple-element.66), channel_id=1, source_target_pairs={{0,2},{1,3},{2,4},{3,5},{4,6},{5,7},{6,0},{7,1},{8,10},{9,11},{10,... | collective-permute-start | bytes 393224 | tf_op jit(solution)/shard_map/ppermute | solution.py:448
  37.5 13.0 %collective-permute-start.6 = (bf16[512,128]{1,0:T(8,128)(2,1)S(1)}, bf16[512,128]{1,0:T(8,128)(2,1)S(1)}, u32[]{:S(2)}, u32[]{:S(2)}) collective-permute-start(bf16[512,128]{1,0:T(8,128)(2,1)S(1)} %get-tuple-element.67), channel_id=1, source_target_pairs={{0,4},{1,5},{2,6},{3,7},{4,0},{5,1},{6,2},{7,3},{8,12},{9,13},{10,... | collective-permute-start | bytes 393224 | tf_op jit(solution)/shard_map/ppermute | solution.py:448
  39.1 13.5 %collective-permute-start.7 = (bf16[512,128]{1,0:T(8,128)(2,1)S(1)}, bf16[512,128]{1,0:T(8,128)(2,1)S(1)}, u32[]{:S(2)}, u32[]{:S(2)}) collective-permute-start(bf16[512,128]{1,0:T(8,128)(2,1)S(1)} %get-tuple-element.68), channel_id=1, source_target_pairs={{0,6},{1,7},{2,0},{3,1},{4,2},{5,3},{6,4},{7,5},{8,14},{9,15},{10,... | collective-permute-start | bytes 393224 | tf_op jit(solution)/shard_map/ppermute | solution.py:448
  40.0 1.0 copy-start.4
  40.9 3.3 %copy-start.1 = (bf16[1,1024,2048]{2,1,0:T(8,128)(2,1)S(1)}, bf16[1,1024,2048]{2,1,0:T(8,128)(2,1)}, u32[]{:S(2)}) copy-start(bf16[1,1024,2048]{2,1,0:T(8,128)(2,1)} %param.10) | copy-start | bytes 12582916
  43.6 15.0 %collective-permute-start.8 = (bf16[2064,128]{1,0:T(8,128)(2,1)S(1)}, bf16[2064,128]{1,0:T(8,128)(2,1)S(1)}, u32[]{:S(2)}, u32[]{:S(2)}) collective-permute-start(bf16[2064,128]{1,0:T(8,128)(2,1)S(1)} %get-tuple-element.62._after), channel_id=1, source_target_pairs={{0,1},{1,0},{2,3},{3,2},{4,5},{5,4},{6,7},{7,6},{8,9},{9,8},{10,11... | collective-permute-start | bytes 1585160 | tf_op jit(solution)/shard_map/ppermute | solution.py:451
  48.0 15.7 %collective-permute-start.9 = (bf16[512,128]{1,0:T(8,128)(2,1)S(1)}, bf16[512,128]{1,0:T(8,128)(2,1)S(1)}, u32[]{:S(2)}, u32[]{:S(2)}) collective-permute-start(bf16[512,128]{1,0:T(8,128)(2,1)S(1)} %get-tuple-element.73), channel_id=1, source_target_pairs={{0,2},{1,3},{2,4},{3,5},{4,6},{5,7},{6,0},{7,1},{8,10},{9,11},{10,... | collective-permute-start | bytes 393224 | tf_op jit(solution)/shard_map/ppermute | solution.py:448
  49.2 14.6 %collective-permute-start.10 = (bf16[512,128]{1,0:T(8,128)(2,1)S(1)}, bf16[512,128]{1,0:T(8,128)(2,1)S(1)}, u32[]{:S(2)}, u32[]{:S(2)}) collective-permute-start(bf16[512,128]{1,0:T(8,128)(2,1)S(1)} %get-tuple-element.74), channel_id=1, source_target_pairs={{0,4},{1,5},{2,6},{3,7},{4,0},{5,1},{6,2},{7,3},{8,12},{9,13},{10,... | collective-permute-start | bytes 393224 | tf_op jit(solution)/shard_map/ppermute | solution.py:448
  50.5 13.2 %collective-permute-start.11 = (bf16[512,128]{1,0:T(8,128)(2,1)S(1)}, bf16[512,128]{1,0:T(8,128)(2,1)S(1)}, u32[]{:S(2)}, u32[]{:S(2)}) collective-permute-start(bf16[512,128]{1,0:T(8,128)(2,1)S(1)} %get-tuple-element.75), channel_id=1, source_target_pairs={{0,6},{1,7},{2,0},{3,1},{4,2},{5,3},{6,4},{7,5},{8,14},{9,15},{10,... | collective-permute-start | bytes 393224 | tf_op jit(solution)/shard_map/ppermute | solution.py:448
  54.0 15.2 %collective-permute-start.13 = (bf16[1024,128]{1,0:T(8,128)(2,1)S(1)}, bf16[1024,128]{1,0:T(8,128)(2,1)S(1)}, u32[]{:S(2)}, u32[]{:S(2)}) collective-permute-start(bf16[1024,128]{1,0:T(8,128)(2,1)S(1)} %get-tuple-element.69._after), channel_id=1, source_target_pairs={{0,1},{1,0},{2,3},{3,2},{4,5},{5,4},{6,7},{7,6},{8,9},{9,8},{10,11... | collective-permute-start | bytes 786440 | tf_op jit(solution)/shard_map/ppermute | solution.py:451
  63.7 3.5 %copy-start.3 = (bf16[3,512,256]{2,1,0:T(8,128)(2,1)S(1)}, bf16[3,512,256]{2,1,0:T(8,128)(2,1)}, u32[]{:S(2)}) copy-start(bf16[3,512,256]{2,1,0:T(8,128)(2,1)} %get-tuple-element.80.own) | copy-start | bytes 2359300
  65.2 7.9 %collective-permute-start.12 = (bf16[1024,128]{1,0:T(8,128)(2,1)S(1)}, bf16[1024,128]{1,0:T(8,128)(2,1)S(1)}, u32[]{:S(2)}, u32[]{:S(2)}) collective-permute-start(bf16[1024,128]{1,0:T(8,128)(2,1)S(1)} %get-tuple-element.77._after), channel_id=1, source_target_pairs={{0,1},{1,0},{2,3},{3,2},{4,5},{5,4},{6,7},{7,6},{8,9},{9,8},{10,11... | collective-permute-start | bytes 786440 | tf_op jit(solution)/shard_map/ppermute | solution.py:451
  65.5 16.1 %collective-permute-start.14 = (bf16[512,256]{1,0:T(8,128)(2,1)S(1)}, bf16[512,256]{1,0:T(8,128)(2,1)S(1)}, u32[]{:S(2)}, u32[]{:S(2)}) collective-permute-start(bf16[512,256]{1,0:T(8,128)(2,1)S(1)} %get-tuple-element.87), channel_id=1, source_target_pairs={{0,1},{1,0},{2,3},{3,2},{4,5},{5,4},{6,7},{7,6},{8,9},{9,8},{10,11... | collective-permute-start | bytes 786440 | tf_op jit(solution)/shard_map/ppermute | solution.py:451
  67.9 13.7 %collective-permute-start.15 = (bf16[2,512,256]{2,1,0:T(8,128)(2,1)S(1)}, bf16[2,512,256]{2,1,0:T(8,128)(2,1)S(1)}, u32[]{:S(2)}, u32[]{:S(2)}) collective-permute-start(bf16[2,512,256]{2,1,0:T(8,128)(2,1)S(1)} %edge.1._after), channel_id=1, source_target_pairs={{0,2},{1,3},{2,4},{3,5},{4,6},{5,7},{8,10},{9,11},{10,12},{11,13},... | collective-permute-start | bytes 1572872 | tf_op jit(solution)/shard_map/ppermute | solution.py:552
  79.5 11.2 %collective-permute-start.16 = (bf16[1,1024,128]{2,1,0:T(8,128)(2,1)S(1)}, bf16[1,1024,128]{2,1,0:T(8,128)(2,1)S(1)}, u32[]{:S(2)}, u32[]{:S(2)}) collective-permute-start(bf16[1,1024,128]{2,1,0:T(8,128)(2,1)S(1)} %get-tuple-element.85._after), channel_id=1, source_target_pairs={{0,1},{1,0},{2,3},{3,2},{4,5},{5,4},{6,7},{7,6},{8,9},{9,8},{10,11... | collective-permute-start | bytes 786440 | tf_op jit(solution)/shard_map/ppermute | solution.py:451
  80.1 14.4 %collective-permute-start.17 = (bf16[2,1024,128]{2,1,0:T(8,128)(2,1)S(1)}, bf16[2,1024,128]{2,1,0:T(8,128)(2,1)S(1)}, u32[]{:S(2)}, u32[]{:S(2)}) collective-permute-start(bf16[2,1024,128]{2,1,0:T(8,128)(2,1)S(1)} %get-tuple-element.93), channel_id=1, source_target_pairs={{0,1},{1,0},{2,3},{3,2},{4,5},{5,4},{6,7},{7,6},{8,9},{9,8},{10,11... | collective-permute-start | bytes 1572872 | tf_op jit(solution)/shard_map/ppermute | solution.py:451
  89.4 11.1 %collective-permute-start.18 = (bf16[2,512,256]{2,1,0:T(8,128)(2,1)S(1)}, bf16[2,512,256]{2,1,0:T(8,128)(2,1)S(1)}, u32[]{:S(2)}, u32[]{:S(2)}) collective-permute-start(bf16[2,512,256]{2,1,0:T(8,128)(2,1)S(1)} %get-tuple-element.88._after), channel_id=1, source_target_pairs={{2,0},{3,1},{4,2},{5,3},{6,4},{7,5},{10,8},{11,9},{12,10},{13,11},... | collective-permute-start | bytes 1572872 | tf_op jit(solution)/shard_map/ppermute | solution.py:620
  101.3 34.6 %collective-permute-start.25 = (bf16[3,512,256]{2,1,0:T(8,128)(2,1)S(1)}, bf16[3,512,256]{2,1,0:T(8,128)(2,1)S(1)}, u32[]{:S(2)}, u32[]{:S(2)}) collective-permute-start(bf16[3,512,256]{2,1,0:T(8,128)(2,1)S(1)} %get-tuple-element.98._after), channel_id=1, source_target_pairs={{0,1},{1,0},{2,3},{3,2},{4,5},{5,4},{6,7},{7,6},{8,9},{9,8},{10,11... | collective-permute-start | bytes 2359304 | tf_op jit(solution)/shard_map/ppermute | solution.py:451
  103.2 5.9 %collective-permute-start.19 = (bf16[1,512,128]{2,1,0:T(8,128)(2,1)S(1)}, bf16[1,512,128]{2,1,0:T(8,128)(2,1)S(1)}, u32[]{:S(2)}, u32[]{:S(2)}) collective-permute-start(bf16[1,512,128]{2,1,0:T(8,128)(2,1)S(1)} %get-tuple-element.99), channel_id=1, source_target_pairs={{0,6},{1,7},{2,0},{3,1},{4,2},{5,3},{6,4},{7,5},{8,14},{9,15},{10,... | collective-permute-start | bytes 393224 | tf_op jit(solution)/shard_map/ppermute | solution.py:448
  103.7 23.4 %collective-permute-start.20 = (bf16[1,512,128]{2,1,0:T(8,128)(2,1)S(1)}, bf16[1,512,128]{2,1,0:T(8,128)(2,1)S(1)}, u32[]{:S(2)}, u32[]{:S(2)}) collective-permute-start(bf16[1,512,128]{2,1,0:T(8,128)(2,1)S(1)} %get-tuple-element.100), channel_id=1, source_target_pairs={{0,4},{1,5},{2,6},{3,7},{4,0},{5,1},{6,2},{7,3},{8,12},{9,13},{10,... | collective-permute-start | bytes 393224 | tf_op jit(solution)/shard_map/ppermute | solution.py:448
  106.4 28.2 %collective-permute-start.22 = (bf16[2,512,128]{2,1,0:T(8,128)(2,1)S(1)}, bf16[2,512,128]{2,1,0:T(8,128)(2,1)S(1)}, u32[]{:S(2)}, u32[]{:S(2)}) collective-permute-start(bf16[2,512,128]{2,1,0:T(8,128)(2,1)S(1)} %get-tuple-element.102), channel_id=1, source_target_pairs={{0,6},{1,7},{2,0},{3,1},{4,2},{5,3},{6,4},{7,5},{8,14},{9,15},{10,... | collective-permute-start | bytes 786440 | tf_op jit(solution)/shard_map/ppermute | solution.py:448
  107.6 28.2 %collective-permute-start.23 = (bf16[2,512,128]{2,1,0:T(8,128)(2,1)S(1)}, bf16[2,512,128]{2,1,0:T(8,128)(2,1)S(1)}, u32[]{:S(2)}, u32[]{:S(2)}) collective-permute-start(bf16[2,512,128]{2,1,0:T(8,128)(2,1)S(1)} %get-tuple-element.103), channel_id=1, source_target_pairs={{0,4},{1,5},{2,6},{3,7},{4,0},{5,1},{6,2},{7,3},{8,12},{9,13},{10,... | collective-permute-start | bytes 786440 | tf_op jit(solution)/shard_map/ppermute | solution.py:448
  109.2 26.7 %collective-permute-start.24 = (bf16[2,512,128]{2,1,0:T(8,128)(2,1)S(1)}, bf16[2,512,128]{2,1,0:T(8,128)(2,1)S(1)}, u32[]{:S(2)}, u32[]{:S(2)}) collective-permute-start(bf16[2,512,128]{2,1,0:T(8,128)(2,1)S(1)} %get-tuple-element.104), channel_id=1, source_target_pairs={{0,2},{1,3},{2,4},{3,5},{4,6},{5,7},{6,0},{7,1},{8,10},{9,11},{10,... | collective-permute-start | bytes 786440 | tf_op jit(solution)/shard_map/ppermute | solution.py:448
  127.1 6.9 %collective-permute-start.21 = (bf16[1,512,128]{2,1,0:T(8,128)(2,1)S(1)}, bf16[1,512,128]{2,1,0:T(8,128)(2,1)S(1)}, u32[]{:S(2)}, u32[]{:S(2)}) collective-permute-start(bf16[1,512,128]{2,1,0:T(8,128)(2,1)S(1)} %get-tuple-element.101), channel_id=1, source_target_pairs={{0,2},{1,3},{2,4},{3,5},{4,6},{5,7},{6,0},{7,1},{8,10},{9,11},{10,... | collective-permute-start | bytes 393224 | tf_op jit(solution)/shard_map/ppermute | solution.py:448

commit v2 on v1

--- a/solution.py
+++ b/solution.py
@@ -111,16 +111,6 @@
         @pl.when(step - HR // 2 != place[1])
         def _():
             send_ref[...] = part
-
-
-def edge_kernel(place, _after, own, got, out):
-    @pl.when(place[1] == 1)
-    def _():
-        out[...] = own[1:]
-
-    @pl.when(place[1] == 0)
-    def _():
-        out[...] = got[1:]
 
 
 def pack_kernel(unit, place, _after, x0, x1, x2, x3, sorted_ref, send_ref, slot_row, slot_col, kept_ref):
@@ -176,10 +166,29 @@
     send_ref[2 * half :, :] = info.astype(BF16)
 
 
-def pack_one_kernel(unit, kept_ref, _after, slot_row, x0, x1, x2, x3, sorted_ref, send_ref):
-    tok = x0.shape[0]
+def pack_value_kernel(unit, kept_ref, _after, slot_row, x0, x1, x2, x3, local_ref, sorted_ref, send_ref):
+    pack_one(unit, kept_ref, slot_row, (x0, x1, x2, x3), sorted_ref, send_ref)
+    tok = local_ref.shape[0]
+    for h in range(HL // 2):
+        at = CS // 2 + h * tok
+        send_ref[at : at + tok, :] = local_ref[:, h * HD : (h + 1) * HD]
+
+
+def pack_grad_kernel(
+    unit, place, kept_ref, _after, slot_row, x0, x1, x2, x3, own, got, sorted_ref, send_ref, edge_ref
+):
+    pack_one(unit, kept_ref, slot_row, (x0, x1, x2, x3), sorted_ref, send_ref)
+    for side, block in ((1, own), (0, got)):
+
+        @pl.when(place[1] == side)
+        def _(block=block):
+            edge_ref[...] = block[1:]
+
+
+def pack_one(unit, kept_ref, slot_row, blocks, sorted_ref, send_ref):
+    tok = sorted_ref.shape[1]
     row_index = lax.broadcasted_iota(jnp.int32, (tok, tok), 0).astype(F32)
-    for d, x in enumerate((x0, x1, x2, x3)):
+    for d, x in enumerate(blocks):
         move = (row_index == slot_row[d : d + 1, :]).astype(BF16)
         sorted_ref[d] = dot(move, x[...]).astype(BF16)
     offset = jnp.int32(0)
@@ -262,14 +271,30 @@
             p_ref[i * QB : (i + 1) * QB, j * QB : (j + 1) * QB] = (s_ref[i * QB : (i + 1) * QB, :] * scale).astype(BF16)
 
 
-def mix_kernel(unit, place, kept_ref, got_ref, _after, sorted_ref, came_ref, p_ref, v_ref, ot_ref, vt):
-    def own(d, u, to):
+def mix_kernel(
+    unit, place, kept_ref, got_ref, _after, sorted_ref, came_ref, p_ref, own, got, g_own, v_ref, ot_ref, edge_ref, vt
+):
+    tok = own.shape[1]
+
+    @pl.when(place[1] == 0)
+    def _():
+        edge_ref[0] = own[0]
+        edge_ref[1] = g_own[...]
+
+    @pl.when(place[1] == 1)
+    def _():
+        edge_ref[0] = got[0]
+        for h in range(HL // 2):
+            at = CS // 2 + h * tok
+            edge_ref[1, :, h * HD : (h + 1) * HD] = came_ref[at : at + tok, :]
+
+    def kept(d, u, to):
         v_ref[rows(to * unit, unit), :] = sorted_ref[d, rows(u * unit, unit), :]
 
-    def got(at, to):
+    def came(at, to):
         v_ref[rows(to * unit, unit), :] = came_ref[rows(at * unit, unit), :]
 
-    each_unit(sorted_ref.shape[1] // unit, place, kept_ref, got_ref, own, got)
+    each_unit(sorted_ref.shape[1] // unit, place, kept_ref, got_ref, kept, came)
     vt[...] = v_ref[...].astype(F32).T.astype(BF16)
     for j in range(CS // QB):
         end = (j + 1) * QB
@@ -317,33 +342,37 @@
     each_unit(tok // unit, place, kept_ref, got_ref, own_out, got_out)
 
 
-def unsort_kernel(unit, kept_ref, _after, slot_col, own_ref, back_ref, y0, y1, y2, y3, full):
+def unsort_kernel(unit, distances, kept_ref, _after, _after_edge, slot_col, own_ref, back_ref, *refs):
+    *outs, full = refs
     tok = own_ref.shape[2]
+    count = own_ref.shape[1]
     col_index = lax.broadcasted_iota(jnp.int32, (tok, tok), 1).astype(F32)
     offset = jnp.int32(0)
-    for d, y in enumerate((y0, y1, y2, y3)):
+    for d in range(HR):
         kept = kept_ref[d]
-
-        def own(u, carry, d=d):
-            for i in range(full.shape[0]):
-                full[i, rows(u * unit, unit), :] = own_ref[d, i, rows(u * unit, unit), :]
-            return carry
-
-        def got(u, carry, offset=offset, kept=kept):
-            for i in range(full.shape[0]):
-                full[i, rows(u * unit, unit), :] = back_ref[i, rows((offset + u - kept) * unit, unit), :]
-            return carry
-
-        lax.fori_loop(0, kept, own, 0)
-        lax.fori_loop(kept, tok // unit, got, 0)
+        if d in distances:
+            n = distances.index(d)
+
+            def own(u, carry, d=d, n=n):
+                for i in range(count):
+                    full[n, i, rows(u * unit, unit), :] = own_ref[d, i, rows(u * unit, unit), :]
+                return carry
+
+            def got(u, carry, n=n, offset=offset, kept=kept):
+                for i in range(count):
+                    full[n, i, rows(u * unit, unit), :] = back_ref[i, rows((offset + u - kept) * unit, unit), :]
+                return carry
+
+            lax.fori_loop(0, kept, own, 0)
+            lax.fori_loop(kept, tok // unit, got, 0)
+            move = (col_index == slot_col[:, d : d + 1]).astype(BF16)
+            for i in range(count):
+                outs[n][i] = dot(move, full[n, i]).astype(BF16)
         offset = offset + tok // unit - kept
-        move = (col_index == slot_col[:, d : d + 1]).astype(BF16)
-        for i in range(full.shape[0]):
-            y[i] = dot(move, full[i]).astype(BF16)
 
 
 def window_kernel(
-    place, _after, own, got, g_own, g_got, edge, dq_ref, early_ref, late_ref, carry_ref, *scratch
+    place, _after, own, got, g_own, g_came, edge, dq_ref, early_ref, late_ref, stats_ref, *scratch
 ):
     tok = own.shape[1]
     pair = 2 * tok
@@ -356,9 +385,10 @@
     for h in range(HL // 2):
         part = slice(h * HD, (h + 1) * HD)
         queries, grads, keys, values, kt, dk, dv = (ref.at[h] for ref in scratch)
-        for at, block, g_block in ((own_at, own, g_own), (got_at, got, g_got)):
+        g_got = g_came[CS // 2 + h * tok : CS // 2 + (h + 1) * tok, :]
+        for at, block, g_block in ((own_at, own, g_own[:, part]), (got_at, got, g_got)):
             queries[rows(at, tok), :] = block[0, :, part]
-            grads[rows(at, tok), :] = g_block[:, part]
+            grads[rows(at, tok), :] = g_block
             keys[rows(at + WIN, tok), :] = block[1, :, part]
             values[rows(at + WIN, tok), :] = block[2, :, part]
         keys[:WIN, :] = edge[0, :, part]
@@ -376,31 +406,54 @@
                 s = jnp.concatenate([jnp.where(started, s[: WIN - lo], -1e30), s[WIN - lo :]], axis=0)
             top = jnp.max(s, axis=0, keepdims=True)
             w = jnp.exp(s - top)
-            p = w * (1.0 / jnp.sum(w, axis=0, keepdims=True))
+            scale = 1.0 / jnp.sum(w, axis=0, keepdims=True)
+            p = w * scale
             dp = dot_nt(values[lo:hi, :], g)
             delta = jnp.sum(p * dp, axis=0, keepdims=True)
             pb = p.astype(BF16)
             ds = (p * (dp - delta)).astype(BF16)
             side, at = divmod(j * QB, tok)
             dq_ref[side, at : at + QB, part] = (dot(kt[:, lo:hi], ds).T * factor).astype(BF16)
-            part_k = dot(ds, q) * factor
-            part_v = dot(pb, g)
-            if j == 0:
-                dk[lo:hi, :] = part_k
-                dv[lo:hi, :] = part_v
-            else:
-                dk[lo : hi - QB, :] = dk[lo : hi - QB, :] + part_k[:-QB]
-                dv[lo : hi - QB, :] = dv[lo : hi - QB, :] + part_v[:-QB]
-                dk[hi - QB : hi, :] = part_k[-QB:]
-                dv[hi - QB : hi, :] = part_v[-QB:]
+            if side == 0:
+                for n, line in enumerate((top, scale, delta)):
+                    stats_ref[3 * h + n : 3 * h + n + 1, at : at + QB] = line
+            skip = max(0, WIN - lo)
+            low = max(lo, WIN) - WIN
+            part_k = dot(ds[skip:], q) * factor
+            part_v = dot(pb[skip:], g)
+            end = hi - WIN
+            if end - QB > low:
+                dk[low : end - QB, :] = dk[low : end - QB, :] + part_k[:-QB]
+                dv[low : end - QB, :] = dv[low : end - QB, :] + part_v[:-QB]
+            dk[end - QB : end, :] = part_k[-QB:]
+            dv[end - QB : end, :] = part_v[-QB:]
         for i, total in enumerate((dk, dv)):
-            carry_ref[i, :, part] = total[:WIN, :].astype(BF16)
-            early_ref[i, :, part] = total[WIN : WIN + tok, :].astype(BF16)
-            late_ref[i, :, part] = total[WIN + tok :, :]
-
-
-def settle_kernel(place, _after, dq_ref, early_ref, late_ref, carry_ref, own, send):
-    late = (late_ref[...] + carry_ref[...].astype(F32)).astype(BF16)
+            early_ref[i, :, part] = total[:tok, :].astype(BF16)
+            late_ref[i, :, part] = total[tok:, :]
+    stats_ref[6:, :] = jnp.zeros((2, tok), F32)
+
+
+def settle_kernel(place, _after, dq_ref, early_ref, late_ref, edge, ahead, stats, own, send, late):
+    tok = edge.shape[1]
+    factor = HD**-0.5
+    r = lax.broadcasted_iota(jnp.int32, (QB, QB), 0)
+    c = lax.broadcasted_iota(jnp.int32, (QB, QB), 1)
+    for h in range(HL // 2):
+        part = slice(h * HD, (h + 1) * HD)
+        for j in range(tok // QB):
+            at = slice(j * QB, (j + 1) * QB)
+            q, g = ahead[0, at, part], ahead[1, at, part]
+            top, scale, delta = (stats[3 * h + n : 3 * h + n + 1, at] for n in range(3))
+            s = dot_nt(edge[0, j * QB :, part], q) * factor
+            p = jnp.exp(s - top) * scale
+            first = jnp.where(r > c, p[:QB], 0.0)
+            p = first if j == tok // QB - 1 else jnp.concatenate([first, p[QB:]], axis=0)
+            ds = p * (dot_nt(edge[1, j * QB :, part], g) - delta)
+            add_k = dot(ds.astype(BF16), q) * factor
+            add_v = dot(p.astype(BF16), g)
+            for i, add in enumerate((add_k, add_v)):
+                base = late_ref[i, :, part] if j == 0 else late[h, i, j * QB :, :]
+                late[h, i, j * QB :, :] = base + add
     for side, (near, far) in enumerate(((own, send), (send, own))):
 
         @pl.when(place[1] == side)
@@ -408,7 +461,9 @@
             near[0] = dq_ref[0]
             near[1:] = early_ref[...]
             far[0] = dq_ref[1]
-            far[1:] = late
+            for h in range(HL // 2):
+                for i in range(2):
+                    far[1 + i, :, h * HD : (h + 1) * HD] = late[h, i].astype(BF16)
 
 
 def join_value_kernel(place, _after, v0, v1, v2, v3, out):
@@ -424,10 +479,11 @@
         for i in range(2):
             outs[i][:, at] = y[i]
     width = HL * HD // 2
-    for block, side in ((own, place[1]), (got, 1 - place[1])):
+    for n in range(2):
+        side = place[1] if n == 0 else 1 - place[1]
         at = pl.ds(pl.multiple_of(HR * HD + side * width, width), width)
         for i in range(3):
-            outs[i][:, at] = block[i]
+            outs[i][:, at] = own[i] if n == 0 else got[i]
 
 
 def struct(*shape, dtype=BF16):
@@ -512,18 +568,15 @@
     )(where, send, local_got, boundary, out_weight[0])
     g_arrived = [g_sent[0]] + [among_groups(g_sent[d], d) for d in range(1, HR)]
 
-    def pack_one(after, blocks, name):
-        return pl.pallas_call(
-            functools.partial(pack_one_kernel, unit),
-            out_shape=[struct(HR, tok, HD), struct(half, HD)],
-            in_specs=smem() + vmem(6),
-            out_specs=vmem(2),
-            compiler_params=params(20),
-            cost_estimate=takes(1.4),
-            name=name,
-        )(kept, after, slot_row, *blocks)
-
-    v_ordered, v_out = pack_one(g_sent[0], v_arrived, "pack_value")
+    v_ordered, v_out = pl.pallas_call(
+        functools.partial(pack_value_kernel, unit),
+        out_shape=[struct(HR, tok, HD), struct(half + HL // 2 * tok, HD)],
+        in_specs=smem() + vmem(7),
+        out_specs=vmem(2),
+        compiler_params=params(20),
+        cost_estimate=takes(1.6),
+        name="pack_value",
+    )(kept, g_sent[0], slot_row, *v_arrived, g_send)
     v_came = swap(v_out)
 
     got, q, k, kt, p = pl.pallas_call(
@@ -537,31 +590,31 @@
         name="probs",
     )(where, kept, v_out, ordered, came)
 
-    g_ordered, g_out = pack_one(kt, g_arrived, "pack_grad")
+    g_ordered, g_out, edge = pl.pallas_call(
+        functools.partial(pack_grad_kernel, unit),
+        out_shape=[struct(HR, tok, HD), struct(half, HD), struct(2, tok, width)],
+        in_specs=smem(2) + vmem(8),
+        out_specs=vmem(3),
+        compiler_params=params(20),
+        cost_estimate=takes(1.6),
+        name="pack_grad",
+    )(where, kept, kt, slot_row, *g_arrived, local_own, local_got)
     g_came = swap(g_out)
-
-    edge = pl.pallas_call(
-        edge_kernel,
-        out_shape=struct(2, tok, width),
-        in_specs=smem() + vmem(3),
-        out_specs=vmem()[0],
-        compiler_params=params(16),
-        cost_estimate=takes(0.6),
-        name="edge",
-    )(where, g_out, local_own, local_got)
-    edge_got = lax.ppermute(edge, "seq", [(i, i + 2) for i in range(devices - 2)])
-    g_got = swap(g_send)
-
-    v, ot = pl.pallas_call(
+    ahead = [(i, i + 2) for i in range(devices - 2)]
+    behind = [(i + 2, i) for i in range(devices - 2)]
+    edge_got = lax.ppermute(edge, "seq", ahead)
+
+    v, ot, query_edge = pl.pallas_call(
         functools.partial(mix_kernel, unit),
-        out_shape=[struct(CS, HD), struct(HD, CS, dtype=F32)],
-        in_specs=smem(3) + vmem(4),
-        out_specs=vmem(2),
+        out_shape=[struct(CS, HD), struct(HD, CS, dtype=F32), struct(2, tok, width)],
+        in_specs=smem(3) + vmem(7),
+        out_specs=vmem(3),
         scratch_shapes=[pltpu.VMEM((HD, CS), BF16)],
         compiler_params=params(20),
         cost_estimate=takes(1.7),
         name="mix",
-    )(where, kept, got, edge, v_ordered, v_came, p)
+    )(where, kept, got, edge, v_ordered, v_came, p, local_own, local_got, g_own)
+    query_edge_got = lax.ppermute(query_edge, "seq", behind)
 
     own_v, back_v, own, back = pl.pallas_call(
         functools.partial(grads_kernel, unit),
@@ -578,29 +631,28 @@
         name="grads",
     )(where, kept, got, g_ordered, g_came, q, k, v, kt, ot, p)
 
-    def bring_home(after, own, back, name):
+    def unsort(distances, after, after_edge, own, returned, name):
         count = own.shape[1]
-        returned = swap(back)
-        natural = pl.pallas_call(
-            functools.partial(unsort_kernel, unit),
-            out_shape=[struct(count, tok, HD)] * HR,
-            in_specs=smem() + vmem(4),
-            out_specs=vmem(4),
-            scratch_shapes=[pltpu.VMEM((count, tok, HD), BF16)],
-            compiler_params=params(32),
-        cost_estimate=takes(2),
+        return pl.pallas_call(
+            functools.partial(unsort_kernel, unit, distances),
+            out_shape=[struct(count, tok, HD)] * len(distances),
+            in_specs=smem() + vmem(5),
+            out_specs=vmem(len(distances)),
+            scratch_shapes=[pltpu.VMEM((len(distances), count, tok, HD), BF16)],
+            compiler_params=params(20),
+            cost_estimate=takes({'unsort_value':2.6,'unsort_first':0.1,'unsort_last':1.4}[name]),
             name=name,
-        )(kept, after, slot_col, own, returned)
-        return [natural[0]] + [among_groups(natural[d], -d) for d in range(1, HR)]
-
+        )(kept, after, after_edge, slot_col, own, returned)
+
+    returned_v, returned = swap(back_v), swap(back)
     pair = 2 * tok
-    dq_local, early, late, carry = pl.pallas_call(
+    dq_local, early, late, stats = pl.pallas_call(
         window_kernel,
         out_shape=[
             struct(2, tok, width),
             struct(2, tok, width),
             struct(2, tok, width, dtype=F32),
-            struct(2, tok, width),
+            struct(8, tok, dtype=F32),
         ],
         in_specs=smem() + vmem(6),
         out_specs=vmem(4),
@@ -610,25 +662,27 @@
             pltpu.VMEM((HL // 2, pair + WIN, HD), BF16),
             pltpu.VMEM((HL // 2, pair + WIN, HD), BF16),
             pltpu.VMEM((HL // 2, HD, pair + WIN), BF16),
-            pltpu.VMEM((HL // 2, pair + WIN, HD), F32),
-            pltpu.VMEM((HL // 2, pair + WIN, HD), F32),
+            pltpu.VMEM((HL // 2, pair, HD), F32),
+            pltpu.VMEM((HL // 2, pair, HD), F32),
         ],
         compiler_params=params(24),
-        cost_estimate=takes(7.8),
+        cost_estimate=takes(4),
         name="window",
-    )(where, back_v, local_own, local_got, g_own, g_got, edge_got)
-    carry_got = lax.ppermute(carry, "seq", [(i + 2, i) for i in range(devices - 2)])
-    home_v = bring_home(carry, own_v, back_v, "unsort_value")
-    home = bring_home(home_v[0], own, back, "unsort_query_key")
+    )(where, back_v, local_own, local_got, g_own, v_came, edge_got)
+    stats_got = lax.ppermute(stats, "seq", behind)
+    natural_v = unsort((0, 1, 2, 3), stats, query_edge_got, own_v, returned_v, "unsort_value")
+    home_v = [natural_v[0]] + [among_groups(natural_v[d], -d) for d in range(1, HR)]
+    first_natural = unsort((0, 1, 2), natural_v[0], natural_v[0], own, returned, "unsort_first")
     settled_own, settled_send = pl.pallas_call(
         settle_kernel,
         out_shape=[struct(3, tok, width)] * 2,
-        in_specs=smem() + vmem(5),
+        in_specs=smem() + vmem(7),
         out_specs=vmem(2),
-        compiler_params=params(16),
-        cost_estimate=takes(0.8),
+        scratch_shapes=[pltpu.VMEM((HL // 2, 2, tok, HD), F32)],
+        compiler_params=params(20),
+        cost_estimate=takes(0.1),
         name="settle",
-    )(where, home[0], dq_local, early, late, carry_got)
+    )(where, first_natural[0], dq_local, early, late, edge, query_edge_got, stats_got)
     settled_got = swap(settled_send)
     value_left = pl.pallas_call(
         join_value_kernel,
@@ -636,9 +690,12 @@
         in_specs=smem() + vmem(5),
         out_specs=vmem()[0],
         compiler_params=params(16),
-        cost_estimate=takes(0.7),
+        cost_estimate=takes(12),
         name="join_value",
     )(where, settled_send, *home_v)
+    last_natural = unsort((3,), value_left, value_left, own, returned, "unsort_last")
+    natural = [*first_natural, *last_natural]
+    home = [natural[0]] + [among_groups(natural[d], -d) for d in range(1, HR)]
 
     outs = pl.pallas_call(
         join_kernel,

time: 139 us -> 134 us (0.964)
  starting transfers between devices: 46 us -> 38.8 us
    ppermute x15, starting transfers between devices: 31.7 us -> 25.4 us  [among_groups(): return lax.ppermute(block, 'seq', route)]
    ppermute x8 -> x7, starting transfers between devices: 9.21 us -> 7.02 us  [swap(): return lax.ppermute(block, 'seq', [(i, i ^ 1) for i in range(devices)])]
    ppermute x8 -> x7, waiting for transfers between devices: 7.14 us -> 8.99 us  [swap(): return lax.ppermute(block, 'seq', [(i, i ^ 1) for i in range(devices)])]
    ppermute x2 -> x3, starting transfers between devices: 2.64 us -> 3.94 us  [the longest x1 1.37 us: pair_body(): edge_got = lax.ppermute(edge, 'seq', ahead)]
    ppermute x2 -> x3, waiting for transfers between devices: 3.25 us -> 2.38 us  [the longest x1 2.38 us: pair_body(): stats_got = lax.ppermute(stats, 'seq', behind)]
  transfers between devices with their start and end apart: 26 -> 26, of which waited for: 10 -> 9; matrix products, arithmetic and copies ran while one was open for 0% -> 0% of each run, Pallas kernels for 30% -> 32%
where the time goes in v2:
time: 134 us; the launch traced here: 133 us
  waiting for transfers between devices  46.2 us (34%)
  Pallas kernels  45.9 us (34%)
  starting transfers between devices  38.8 us (29%)
    ppermute x15, waiting for transfers between devices, among_groups(): return lax.ppermute(block, 'seq', route)  34.9 us
    ppermute x15, starting transfers between devices, among_groups(): return lax.ppermute(block, 'seq', route)  25.4 us
    ppermute x7, waiting for transfers between devices, swap(): return lax.ppermute(block, 'seq', [(i, i ^ 1) for i in range(devices)])  8.99 us
    pallas_call x1, Pallas kernels, pair_body(): pl.pallas_call(window_kernel, out_shape=[struct(2, tok, width), struct(2,...  7.36 us
    ppermute x7, starting transfers between devices, swap(): return lax.ppermute(block, 'seq', [(i, i ^ 1) for i in range(devices)])  7.02 us
    pallas_call x1, Pallas kernels, pair_body(): pl.pallas_call(functools.partial(grads_kernel, unit), out_shape=[struct(H...  6.41 us
    pallas_call x3, Pallas kernels, unsort(): pl.pallas_call(functools.partial(unsort_kernel, unit, distances), out_sha...  6.01 us
    pallas_call x1, Pallas kernels, pair_body(): pl.pallas_call(functools.partial(probs_kernel, unit), out_shape=[struct(H...  5.11 us
  transfers between devices with their start and end apart: 26, of which 9 were waited for; matrix products, arithmetic and copies ran while one was open for 0% of the time, Pallas kernels for 32%

profile of v2, /device:TPU:0, one launch (start us, length us, event | category | flops | bytes accessed | tf_op | source)
XLA Modules:
  0.0 133.5 jit_solution(6657529976341315367)
XLA Ops:
  0.6 2.4 %collective-permute-start.4 = (bf16[1,512,2048]{2,1,0:T(8,128)(2,1)}, bf16[1,512,2048]{2,1,0:T(8,128)(2,1)S(1)}, u32[]{:S(2)}, u32[]{:S(2)}) collective-permute-start(bf16[1,512,2048]{2,1,0:T(8,128)(2,1)} %param.9), channel_id=1, source_target_pairs={{8,0},{16,8},{24,16},{0,24},{9,1},{17,9},{25,17},{1,25},{10,2},{18... | collective-permute-start | bytes 6291464 | tf_op jit(solution)/shard_map/ppermute | solution.py:715
  3.7 4.1 %split.1 = (bf16[1040,128]{1,0:T(8,128)(2,1)}, bf16[1040,128]{1,0:T(8,128)(2,1)}, bf16[1040,128]{1,0:T(8,128)(2,1)}, bf16[1040,128]{1,0:T(8,128)(2,1)}, bf16[3,5...) custom-call(s32[2]{0:T(128)} %pad_add_fusion.place, s32[4,512]{1,0:T(4,128)} %bitcast.17, bf16[512,1024]{1,0:T(8,128)(2,1)} %bitcast.15, ...), custom_call_target="tpu_custom_call" | custom-call | flops 2200000000 | bytes 7000000 | tf_op jit(solution)/shard_map/split/pallas_call | solution.py:512
  7.8 1.6 %collective-permute-start.3 = (bf16[3,512,256]{2,1,0:T(8,128)(2,1)}, bf16[3,512,256]{2,1,0:T(8,128)(2,1)S(1)}, u32[]{:S(2)}, u32[]{:S(2)}) collective-permute-start(bf16[3,512,256]{2,1,0:T(8,128)(2,1)} %get-tuple-element.64), channel_id=1, source_target_pairs={{0,1},{1,0},{2,3},{3,2},{4,5},{5,4},{6,7},{7,6},{8,9},{9,8},{10,11... | collective-permute-start | bytes 2359304 | tf_op jit(solution)/shard_map/ppermute | solution.py:507
  9.4 1.6 %collective-permute-start = (bf16[1040,128]{1,0:T(8,128)(2,1)}, bf16[1040,128]{1,0:T(8,128)(2,1)S(1)}, u32[]{:S(2)}, u32[]{:S(2)}) collective-permute-start(bf16[1040,128]{1,0:T(8,128)(2,1)} %get-tuple-element.57), channel_id=1, source_target_pairs={{0,2},{1,3},{2,4},{3,5},{4,6},{5,7},{6,0},{7,1},{8,10},{9,11},{10,... | collective-permute-start | bytes 798728 | tf_op jit(solution)/shard_map/ppermute | solution.py:504
  11.0 2.6 %collective-permute-start.1 = (bf16[1040,128]{1,0:T(8,128)(2,1)}, bf16[1040,128]{1,0:T(8,128)(2,1)S(1)}, u32[]{:S(2)}, u32[]{:S(2)}) collective-permute-start(bf16[1040,128]{1,0:T(8,128)(2,1)} %get-tuple-element.58), channel_id=1, source_target_pairs={{0,4},{1,5},{2,6},{3,7},{4,0},{5,1},{6,2},{7,3},{8,12},{9,13},{10,... | collective-permute-start | bytes 798728 | tf_op jit(solution)/shard_map/ppermute | solution.py:504
  14.9 6.0 %collective-permute-done._after1.x1 = bf16[1040,128]{1,0:T(8,128)(2,1)S(1)} collective-permute-done((bf16[1040,128]{1,0:T(8,128)(2,1)}, bf16[1040,128]{1,0:T(8,128)(2,1)S(1)}, u32[]{:S(2)}, u32[]{:S(2)}) %collective-permute-start) | collective-permute-done | bytes 266272 | tf_op jit(solution)/shard_map/ppermute | solution.py:504
  20.9 9.7 %collective-permute-done.1._after2.x2 = bf16[1040,128]{1,0:T(8,128)(2,1)S(1)} collective-permute-done((bf16[1040,128]{1,0:T(8,128)(2,1)}, bf16[1040,128]{1,0:T(8,128)(2,1)S(1)}, u32[]{:S(2)}, u32[]{:S(2)}) %collective-permute-start.1) | collective-permute-done | bytes 266272 | tf_op jit(solution)/shard_map/ppermute | solution.py:504
  31.3 6.2 %collective-permute-start.5 = (bf16[512,128]{1,0:T(8,128)(2,1)S(1)}, bf16[512,128]{1,0:T(8,128)(2,1)S(1)}, u32[]{:S(2)}, u32[]{:S(2)}) collective-permute-start(bf16[512,128]{1,0:T(8,128)(2,1)S(1)} %get-tuple-element.67), channel_id=1, source_target_pairs={{0,2},{1,3},{2,4},{3,5},{4,6},{5,7},{6,0},{7,1},{8,10},{9,11},{10,... | collective-permute-start | bytes 393224 | tf_op jit(solution)/shard_map/ppermute | solution.py:504
  37.5 1.6 %collective-permute-start.6 = (bf16[512,128]{1,0:T(8,128)(2,1)S(1)}, bf16[512,128]{1,0:T(8,128)(2,1)S(1)}, u32[]{:S(2)}, u32[]{:S(2)}) collective-permute-start(bf16[512,128]{1,0:T(8,128)(2,1)S(1)} %get-tuple-element.68), channel_id=1, source_target_pairs={{0,4},{1,5},{2,6},{3,7},{4,0},{5,1},{6,2},{7,3},{8,12},{9,13},{10,... | collective-permute-start | bytes 393224 | tf_op jit(solution)/shard_map/ppermute | solution.py:504
  40.9 2.6 %pack.1 = (bf16[4,2,512,128]{3,2,1,0:T(8,128)(2,1)S(1)}, bf16[2064,128]{1,0:T(8,128)(2,1)S(1)}, f32[8,512]{1,0:T(8,128)S(1)}, f32[512,128]{1,0:T(8,128)S(1)}, s32[4]{0:T(128)S(1)}) custom-call(s32[2]{0:T(128)S(1)} %copy-done.1, bf16[512,128]{1,0:T(8,128)(2,1)S(1)} %get-tuple-element.60._after.x0, bf16[1040,128]{1,0:T(8,128)(2,1)S(1)} %copy-done.4, ...), custom_call_target="tpu_custom_call" | custom-call | flops 2860000000 | bytes 9100000 | tf_op jit(solution)/shard_map/pack/pallas_call | solution.py:535
  44.1 3.8 %project.1 = (bf16[512,128]{1,0:T(8,128)(2,1)S(1)}, bf16[512,128]{1,0:T(8,128)(2,1)S(1)}, bf16[512,128]{1,0:T(8,128)(2,1)S(1)}, bf16[512,128]{1,0:T(8,128)(2,1)S...) custom-call(s32[2]{0:T(128)S(1)} %copy-done.1, bf16[2064,128]{1,0:T(8,128)(2,1)S(1)} %get-tuple-element.63._after, ...), custom_call_target="tpu_custom_call" | custom-call | flops 4180000000 | bytes 13300000 | tf_op jit(solution)/shard_map/project/pallas_call | solution.py:552
  48.7 2.9 %collective-permute-start.11 = (bf16[512,128]{1,0:T(8,128)(2,1)S(1)}, bf16[512,128]{1,0:T(8,128)(2,1)S(1)}, u32[]{:S(2)}, u32[]{:S(2)}) collective-permute-start(bf16[512,128]{1,0:T(8,128)(2,1)S(1)} %get-tuple-element.77), channel_id=1, source_target_pairs={{0,6},{1,7},{2,0},{3,1},{4,2},{5,3},{6,4},{7,5},{8,14},{9,15},{10,... | collective-permute-start | bytes 393224 | tf_op jit(solution)/shard_map/ppermute | solution.py:504
  51.6 1.4 %pack_value.1 = (bf16[4,512,128]{2,1,0:T(8,128)(2,1)S(1)}, bf16[2048,128]{1,0:T(8,128)(2,1)S(1)}) custom-call(s32[4]{0:T(128)S(1)} %get-tuple-element.62.kept_ref, bf16[512,128]{1,0:T(8,128)(2,1)S(1)} %get-tuple-element.65._after.x0, f32[8,512]{1,0:T(8,128)S(1)} %get-tuple-element.66.slot_row, bf16[512,128]{1,0:T(8,128)(2,1)S(1)} %get-tuple-element.60._after.x0, ...), custom_call_target="tpu_custom_call" | custom-call | flops 1760000000 | bytes 5600000 | tf_op jit(solution)/shard_map/pack_value/pallas_call | solution.py:571
  53.0 1.6 %collective-permute-start.13 = (bf16[2048,128]{1,0:T(8,128)(2,1)S(1)}, bf16[2048,128]{1,0:T(8,128)(2,1)S(1)}, u32[]{:S(2)}, u32[]{:S(2)}) collective-permute-start(bf16[2048,128]{1,0:T(8,128)(2,1)S(1)} %get-tuple-element.71._after), channel_id=1, source_target_pairs={{0,1},{1,0},{2,3},{3,2},{4,5},{5,4},{6,7},{7,6},{8,9},{9,8},{10,11... | collective-permute-start | bytes 1572872 | tf_op jit(solution)/shard_map/ppermute | solution.py:507
  54.6 4.0 %collective-permute-done.8.came_ref = bf16[2064,128]{1,0:T(8,128)(2,1)S(1)} collective-permute-done((bf16[2064,128]{1,0:T(8,128)(2,1)S(1)}, bf16[2064,128]{1,0:T(8,128)(2,1)S(1)}, u32[]{:S(2)}, u32[]{:S(2)}) %collective-permute-start.8) | collective-permute-done | bytes 528416 | tf_op jit(solution)/shard_map/ppermute | solution.py:507
  58.6 5.1 %probs.1 = (s32[4]{0:T(128)S(1)}, bf16[2048,128]{1,0:T(8,128)(2,1)S(1)}, bf16[2048,128]{1,0:T(8,128)(2,1)S(1)}, bf16[128,2048]{1,0:T(8,128)(2,1)S(1)}, bf16[2048,2048]{1,0:T(8,128)(2,1)S(1)}) custom-call(s32[2]{0:T(128)S(1)} %copy-done.1, s32[4]{0:T(128)S(1)} %get-tuple-element.62.kept_ref, bf16[2048,128]{1,0:T(8,128)(2,1)S(1)} %get-tuple-element.71._after, ...), custom_call_target="tpu_custom_call" | custom-call | flops 5500000256 | bytes 17500000 | tf_op jit(solution)/shard_map/probs/pallas_call | solution.py:582
  63.7 1.4 %pack_grad.1 = (bf16[4,512,128]{2,1,0:T(8,128)(2,1)S(1)}, bf16[1024,128]{1,0:T(8,128)(2,1)S(1)}, bf16[2,512,256]{2,1,0:T(8,128)(2,1)S(1)}) custom-call(s32[2]{0:T(128)S(1)} %copy-done.1, s32[4]{0:T(128)S(1)} %get-tuple-element.62.kept_ref, bf16[128,2048]{1,0:T(8,128)(2,1)S(1)} %get-tuple-element.74._after.kt_ref, f32[8,512]{1,0:T(8,128)S(1)} %get-tuple-element.66.slot_row, ...), custom_call_target="tpu_custom_call" | custom-call | flops 1760000000 | bytes 5600000 | tf_op jit(solution)/shard_map/pack_grad/pallas_call | solution.py:593
  65.7 1.4 %collective-permute-start.14 = (bf16[2,512,256]{2,1,0:T(8,128)(2,1)S(1)}, bf16[2,512,256]{2,1,0:T(8,128)(2,1)S(1)}, u32[]{:S(2)}, u32[]{:S(2)}) collective-permute-start(bf16[2,512,256]{2,1,0:T(8,128)(2,1)S(1)} %get-tuple-element.83._after.edge), channel_id=1, source_target_pairs={{0,2},{1,3},{2,4},{3,5},{4,6},{5,7},{8,10},{9,11},{10,12},{11,13},... | collective-permute-start | bytes 1572872 | tf_op jit(solution)/shard_map/ppermute | solution.py:605
  67.1 2.7 %collective-permute-done.13.came_ref.g_came = bf16[2048,128]{1,0:T(8,128)(2,1)S(1)} collective-permute-done((bf16[2048,128]{1,0:T(8,128)(2,1)S(1)}, bf16[2048,128]{1,0:T(8,128)(2,1)S(1)}, u32[]{:S(2)}, u32[]{:S(2)}) %collective-permute-start.13) | collective-permute-done | bytes 524320 | tf_op jit(solution)/shard_map/ppermute | solution.py:507
  69.8 1.7 %mix.1 = (bf16[2048,128]{1,0:T(8,128)(2,1)S(1)}, f32[128,2048]{1,0:T(8,128)S(1)}, bf16[2,512,256]{2,1,0:T(8,128)(2,1)S(1)}) custom-call(s32[2]{0:T(128)S(1)} %copy-done.1, s32[4]{0:T(128)S(1)} %get-tuple-element.62.kept_ref, s32[4]{0:T(128)S(1)} %get-tuple-element.73.got_ref, bf16[2,512,256]{2,1,0:T(8,128)(2,1)S(1)} %get-tuple-element.83._after.edge, ...), custom_call_target="tpu_custom_call" | custom-call | flops 1870000000 | bytes 5950000 | tf_op jit(solution)/shard_map/mix/pallas_call | solution.py:607
  73.8 6.4 %grads.1 = (bf16[4,1,512,128]{3,2,1,0:T(8,128)(2,1)S(1)}, bf16[1,1024,128]{2,1,0:T(8,128)(2,1)S(1)}, bf16[4,2,512,128]{3,2,1,0:T(8,128)(2,1)S(1)}, bf16[2,1024,128]{2,1,0:T(8,128)(2,1)S(1)}) custom-call(s32[2]{0:T(128)S(1)} %copy-done.1, s32[4]{0:T(128)S(1)} %get-tuple-element.62.kept_ref, s32[4]{0:T(128)S(1)} %get-tuple-element.73.got_ref, ...), custom_call_target="tpu_custom_call" | custom-call | flops 6929999872 | bytes 22050000 | tf_op jit(solution)/shard_map/grads/pallas_call | solution.py:619
  80.8 1.5 %collective-permute-start.17 = (bf16[2,1024,128]{2,1,0:T(8,128)(2,1)S(1)}, bf16[2,1024,128]{2,1,0:T(8,128)(2,1)S(1)}, u32[]{:S(2)}, u32[]{:S(2)}) collective-permute-start(bf16[2,1024,128]{2,1,0:T(8,128)(2,1)S(1)} %get-tuple-element.96), channel_id=1, source_target_pairs={{0,1},{1,0},{2,3},{3,2},{4,5},{5,4},{6,7},{7,6},{8,9},{9,8},{10,11... | collective-permute-start | bytes 1572872 | tf_op jit(solution)/shard_map/ppermute | solution.py:507
  82.4 7.4 %window.1 = (bf16[2,512,256]{2,1,0:T(8,128)(2,1)S(1)}, bf16[2,512,256]{2,1,0:T(8,128)(2,1)S(1)}, f32[2,512,256]{2,1,0:T(8,128)S(1)}, f32[8,512]{1,0:T(8,128)S(1)}) custom-call(s32[2]{0:T(128)S(1)} %copy-done.1, bf16[1,1024,128]{2,1,0:T(8,128)(2,1)S(1)} %get-tuple-element.89._after, bf16[3,512,256]{2,1,0:T(8,128)(2,1)S(1)} %copy-done, ...), custom_call_target="tpu_custom_call" | custom-call | flops 4400000000 | bytes 14000000 | tf_op jit(solution)/shard_map/window/pallas_call | solution.py:649
  89.7 2.8 %unsort_value.1 = (bf16[1,512,128]{2,1,0:T(8,128)(2,1)S(1)}, bf16[1,512,128]{2,1,0:T(8,128)(2,1)S(1)}, bf16[1,512,128]{2,1,0:T(8,128)(2,1)S(1)}, bf16[1,512,128]{2,1,0:T(8,128)(2,1)S(1)}) custom-call(s32[4]{0:T(128)S(1)} %get-tuple-element.62.kept_ref, f32[8,512]{1,0:T(8,128)S(1)} %get-tuple-element.90._after, ...), custom_call_target="tpu_custom_call" | custom-call | flops 2860000000 | bytes 9100000 | tf_op jit(solution)/shard_map/unsort_value/pallas_call | solution.py:636
  92.5 1.7 %collective-permute-start.19 = (bf16[1,512,128]{2,1,0:T(8,128)(2,1)S(1)}, bf16[1,512,128]{2,1,0:T(8,128)(2,1)S(1)}, u32[]{:S(2)}, u32[]{:S(2)}) collective-permute-start(bf16[1,512,128]{2,1,0:T(8,128)(2,1)S(1)} %get-tuple-element.102), channel_id=1, source_target_pairs={{0,6},{1,7},{2,0},{3,1},{4,2},{5,3},{6,4},{7,5},{8,14},{9,15},{10,... | collective-permute-start | bytes 393224 | tf_op jit(solution)/shard_map/ppermute | solution.py:504
  94.3 1.5 %collective-permute-start.20 = (bf16[1,512,128]{2,1,0:T(8,128)(2,1)S(1)}, bf16[1,512,128]{2,1,0:T(8,128)(2,1)S(1)}, u32[]{:S(2)}, u32[]{:S(2)}) collective-permute-start(bf16[1,512,128]{2,1,0:T(8,128)(2,1)S(1)} %get-tuple-element.103), channel_id=1, source_target_pairs={{0,4},{1,5},{2,6},{3,7},{4,0},{5,1},{6,2},{7,3},{8,12},{9,13},{10,... | collective-permute-start | bytes 393224 | tf_op jit(solution)/shard_map/ppermute | solution.py:504
  98.3 2.2 %unsort_first.1 = (bf16[2,512,128]{2,1,0:T(8,128)(2,1)S(1)}, bf16[2,512,128]{2,1,0:T(8,128)(2,1)S(1)}, bf16[2,512,128]{2,1,0:T(8,128)(2,1)S(1)}) custom-call(s32[4]{0:T(128)S(1)} %get-tuple-element.62.kept_ref, bf16[1,512,128]{2,1,0:T(8,128)(2,1)S(1)} %get-tuple-element.94._after._after_edge.v0, ...), custom_call_target="tpu_custom_call" | custom-call | flops 110000000 | bytes 350000 | tf_op jit(solution)/shard_map/unsort_first/pallas_call | solution.py:636
  100.5 2.4 %collective-permute-done.18.stats = f32[8,512]{1,0:T(8,128)S(1)} collective-permute-done((f32[8,512]{1,0:T(8,128)S(1)}, f32[8,512]{1,0:T(8,128)S(1)}, u32[]{:S(2)}, u32[]{:S(2)}) %collective-permute-start.18) | collective-permute-done | bytes 16416 | tf_op jit(solution)/shard_map/ppermute | solution.py:672
  102.8 1.9 %settle.1 = (bf16[3,512,256]{2,1,0:T(8,128)(2,1)S(1)}, bf16[3,512,256]{2,1,0:T(8,128)(2,1)S(1)}) custom-call(s32[2]{0:T(128)S(1)} %copy-done.1, bf16[2,512,128]{2,1,0:T(8,128)(2,1)S(1)} %get-tuple-element.97._after.y0, bf16[2,512,256]{2,1,0:T(8,128)(2,1)S(1)} %get-tuple-element.98.dq_ref, bf16[2,512,256]{2,1,0:T(8,128)(2,1)S(1)} %get-tuple-element.99.early_ref, ...), custom_call_target="tpu_custom_call" | custom-call | flops 110000000 | bytes 350000 | tf_op jit(solution)/shard_map/settle/pallas_call | solution.py:676
  106.0 3.7 %collective-permute-start.23 = (bf16[2,512,128]{2,1,0:T(8,128)(2,1)S(1)}, bf16[2,512,128]{2,1,0:T(8,128)(2,1)S(1)}, u32[]{:S(2)}, u32[]{:S(2)}) collective-permute-start(bf16[2,512,128]{2,1,0:T(8,128)(2,1)S(1)} %get-tuple-element.106), channel_id=1, source_target_pairs={{0,4},{1,5},{2,6},{3,7},{4,0},{5,1},{6,2},{7,3},{8,12},{9,13},{10,... | collective-permute-start | bytes 786440 | tf_op jit(solution)/shard_map/ppermute | solution.py:504
  112.6 18.0 %collective-permute-done.23.y2 = bf16[2,512,128]{2,1,0:T(8,128)(2,1)S(1)} collective-permute-done((bf16[2,512,128]{2,1,0:T(8,128)(2,1)S(1)}, bf16[2,512,128]{2,1,0:T(8,128)(2,1)S(1)}, u32[]{:S(2)}, u32[]{:S(2)}) %collective-permute-start.23) | collective-permute-done | bytes 262176 | tf_op jit(solution)/shard_map/ppermute | solution.py:504
  130.7 2.8 %join.1 = (bf16[512,1024]{1,0:T(8,128)(2,1)}, bf16[512,1024]{1,0:T(8,128)(2,1)}, bf16[512,1024]{1,0:T(8,128)(2,1)}) custom-call(s32[2]{0:T(128)S(1)} %copy-done.1, bf16[512,512]{1,0:T(8,128)(2,1)S(1)} %join_value.1._after._after_edge.value_ref, bf16[2,512,128]{2,1,0:T(8,128)(2,1)S(1)} %get-tuple-element.97._after.y0, ...), custom_call_target="tpu_custom_call" | custom-call | flops 3080000000 | bytes 9800000 | tf_op jit(solution)/shard_map/join/pallas_call | solution.py:700
  (47 shorter events, 16.1 us)
Async XLA Ops:
  0.6 30.0 %copy-start.3 = (bf16[1,512,1024]{2,1,0:T(8,128)(2,1)S(1)}, bf16[1,512,1024]{2,1,0:T(8,128)(2,1)}, u32[]{:S(2)}) copy-start(bf16[1,512,1024]{2,1,0:T(8,128)(2,1)} %param.8) | copy-start | bytes 3145732
  0.6 43.5 %collective-permute-start.4 = (bf16[1,512,2048]{2,1,0:T(8,128)(2,1)}, bf16[1,512,2048]{2,1,0:T(8,128)(2,1)S(1)}, u32[]{:S(2)}, u32[]{:S(2)}) collective-permute-start(bf16[1,512,2048]{2,1,0:T(8,128)(2,1)} %param.9), channel_id=1, source_target_pairs={{8,0},{16,8},{24,16},{0,24},{9,1},{17,9},{25,17},{1,25},{10,2},{18... | collective-permute-start | bytes 6291464 | tf_op jit(solution)/shard_map/ppermute | solution.py:715
  3.7 26.9 %copy-start.1 = (s32[2]{0:T(128)S(1)}, s32[2]{0:T(128)}, u32[]{:S(2)}) copy-start(s32[2]{0:T(128)} %pad_add_fusion.place) | copy-start | bytes 28
  7.8 35.8 %collective-permute-start.3 = (bf16[3,512,256]{2,1,0:T(8,128)(2,1)}, bf16[3,512,256]{2,1,0:T(8,128)(2,1)S(1)}, u32[]{:S(2)}, u32[]{:S(2)}) collective-permute-start(bf16[3,512,256]{2,1,0:T(8,128)(2,1)} %get-tuple-element.64), channel_id=1, source_target_pairs={{0,1},{1,0},{2,3},{3,2},{4,5},{5,4},{6,7},{7,6},{8,9},{9,8},{10,11... | collective-permute-start | bytes 2359304 | tf_op jit(solution)/shard_map/ppermute | solution.py:507
  9.4 11.5 %collective-permute-start = (bf16[1040,128]{1,0:T(8,128)(2,1)}, bf16[1040,128]{1,0:T(8,128)(2,1)S(1)}, u32[]{:S(2)}, u32[]{:S(2)}) collective-permute-start(bf16[1040,128]{1,0:T(8,128)(2,1)} %get-tuple-element.57), channel_id=1, source_target_pairs={{0,2},{1,3},{2,4},{3,5},{4,6},{5,7},{6,0},{7,1},{8,10},{9,11},{10,... | collective-permute-start | bytes 798728 | tf_op jit(solution)/shard_map/ppermute | solution.py:504
  11.0 19.6 %collective-permute-start.1 = (bf16[1040,128]{1,0:T(8,128)(2,1)}, bf16[1040,128]{1,0:T(8,128)(2,1)S(1)}, u32[]{:S(2)}, u32[]{:S(2)}) collective-permute-start(bf16[1040,128]{1,0:T(8,128)(2,1)} %get-tuple-element.58), channel_id=1, source_target_pairs={{0,4},{1,5},{2,6},{3,7},{4,0},{5,1},{6,2},{7,3},{8,12},{9,13},{10,... | collective-permute-start | bytes 798728 | tf_op jit(solution)/shard_map/ppermute | solution.py:504
  13.6 17.1 %collective-permute-start.2 = (bf16[1040,128]{1,0:T(8,128)(2,1)}, bf16[1040,128]{1,0:T(8,128)(2,1)S(1)}, u32[]{:S(2)}, u32[]{:S(2)}) collective-permute-start(bf16[1040,128]{1,0:T(8,128)(2,1)} %get-tuple-element.59), channel_id=1, source_target_pairs={{0,6},{1,7},{2,0},{3,1},{4,2},{5,3},{6,4},{7,5},{8,14},{9,15},{10,... | collective-permute-start | bytes 798728 | tf_op jit(solution)/shard_map/ppermute | solution.py:504
  31.3 17.4 %collective-permute-start.5 = (bf16[512,128]{1,0:T(8,128)(2,1)S(1)}, bf16[512,128]{1,0:T(8,128)(2,1)S(1)}, u32[]{:S(2)}, u32[]{:S(2)}) collective-permute-start(bf16[512,128]{1,0:T(8,128)(2,1)S(1)} %get-tuple-element.67), channel_id=1, source_target_pairs={{0,2},{1,3},{2,4},{3,5},{4,6},{5,7},{6,0},{7,1},{8,10},{9,11},{10,... | collective-permute-start | bytes 393224 | tf_op jit(solution)/shard_map/ppermute | solution.py:504
  37.5 14.1 %collective-permute-start.6 = (bf16[512,128]{1,0:T(8,128)(2,1)S(1)}, bf16[512,128]{1,0:T(8,128)(2,1)S(1)}, u32[]{:S(2)}, u32[]{:S(2)}) collective-permute-start(bf16[512,128]{1,0:T(8,128)(2,1)S(1)} %get-tuple-element.68), channel_id=1, source_target_pairs={{0,4},{1,5},{2,6},{3,7},{4,0},{5,1},{6,2},{7,3},{8,12},{9,13},{10,... | collective-permute-start | bytes 393224 | tf_op jit(solution)/shard_map/ppermute | solution.py:504
  39.1 12.5 %collective-permute-start.7 = (bf16[512,128]{1,0:T(8,128)(2,1)S(1)}, bf16[512,128]{1,0:T(8,128)(2,1)S(1)}, u32[]{:S(2)}, u32[]{:S(2)}) collective-permute-start(bf16[512,128]{1,0:T(8,128)(2,1)S(1)} %get-tuple-element.69), channel_id=1, source_target_pairs={{0,6},{1,7},{2,0},{3,1},{4,2},{5,3},{6,4},{7,5},{8,14},{9,15},{10,... | collective-permute-start | bytes 393224 | tf_op jit(solution)/shard_map/ppermute | solution.py:504
  40.0 1.0 copy-start.4
  40.9 3.2 %copy-start.2 = (bf16[1,1024,2048]{2,1,0:T(8,128)(2,1)S(1)}, bf16[1,1024,2048]{2,1,0:T(8,128)(2,1)}, u32[]{:S(2)}) copy-start(bf16[1,1024,2048]{2,1,0:T(8,128)(2,1)} %param.10) | copy-start | bytes 12582916
  43.6 15.0 %collective-permute-start.8 = (bf16[2064,128]{1,0:T(8,128)(2,1)S(1)}, bf16[2064,128]{1,0:T(8,128)(2,1)S(1)}, u32[]{:S(2)}, u32[]{:S(2)}) collective-permute-start(bf16[2064,128]{1,0:T(8,128)(2,1)S(1)} %get-tuple-element.63._after), channel_id=1, source_target_pairs={{0,1},{1,0},{2,3},{3,2},{4,5},{5,4},{6,7},{7,6},{8,9},{9,8},{10,11... | collective-permute-start | bytes 1585160 | tf_op jit(solution)/shard_map/ppermute | solution.py:507
  48.0 15.7 %collective-permute-start.10 = (bf16[512,128]{1,0:T(8,128)(2,1)S(1)}, bf16[512,128]{1,0:T(8,128)(2,1)S(1)}, u32[]{:S(2)}, u32[]{:S(2)}) collective-permute-start(bf16[512,128]{1,0:T(8,128)(2,1)S(1)} %get-tuple-element.76), channel_id=1, source_target_pairs={{0,4},{1,5},{2,6},{3,7},{4,0},{5,1},{6,2},{7,3},{8,12},{9,13},{10,... | collective-permute-start | bytes 393224 | tf_op jit(solution)/shard_map/ppermute | solution.py:504
  48.7 15.0 %collective-permute-start.11 = (bf16[512,128]{1,0:T(8,128)(2,1)S(1)}, bf16[512,128]{1,0:T(8,128)(2,1)S(1)}, u32[]{:S(2)}, u32[]{:S(2)}) collective-permute-start(bf16[512,128]{1,0:T(8,128)(2,1)S(1)} %get-tuple-element.77), channel_id=1, source_target_pairs={{0,6},{1,7},{2,0},{3,1},{4,2},{5,3},{6,4},{7,5},{8,14},{9,15},{10,... | collective-permute-start | bytes 393224 | tf_op jit(solution)/shard_map/ppermute | solution.py:504
  51.6 12.1 %collective-permute-start.9 = (bf16[512,128]{1,0:T(8,128)(2,1)S(1)}, bf16[512,128]{1,0:T(8,128)(2,1)S(1)}, u32[]{:S(2)}, u32[]{:S(2)}) collective-permute-start(bf16[512,128]{1,0:T(8,128)(2,1)S(1)} %get-tuple-element.75), channel_id=1, source_target_pairs={{0,2},{1,3},{2,4},{3,5},{4,6},{5,7},{6,0},{7,1},{8,10},{9,11},{10,... | collective-permute-start | bytes 393224 | tf_op jit(solution)/shard_map/ppermute | solution.py:504
  53.0 16.8 %collective-permute-start.13 = (bf16[2048,128]{1,0:T(8,128)(2,1)S(1)}, bf16[2048,128]{1,0:T(8,128)(2,1)S(1)}, u32[]{:S(2)}, u32[]{:S(2)}) collective-permute-start(bf16[2048,128]{1,0:T(8,128)(2,1)S(1)} %get-tuple-element.71._after), channel_id=1, source_target_pairs={{0,1},{1,0},{2,3},{3,2},{4,5},{5,4},{6,7},{7,6},{8,9},{9,8},{10,11... | collective-permute-start | bytes 1572872 | tf_op jit(solution)/shard_map/ppermute | solution.py:507
  58.6 5.2 %copy-start = (bf16[3,512,256]{2,1,0:T(8,128)(2,1)S(1)}, bf16[3,512,256]{2,1,0:T(8,128)(2,1)}, u32[]{:S(2)}) copy-start(bf16[3,512,256]{2,1,0:T(8,128)(2,1)} %get-tuple-element.78.own) | copy-start | bytes 2359300
  65.1 8.7 %collective-permute-start.12 = (bf16[1024,128]{1,0:T(8,128)(2,1)S(1)}, bf16[1024,128]{1,0:T(8,128)(2,1)S(1)}, u32[]{:S(2)}, u32[]{:S(2)}) collective-permute-start(bf16[1024,128]{1,0:T(8,128)(2,1)S(1)} %get-tuple-element.80), channel_id=1, source_target_pairs={{0,1},{1,0},{2,3},{3,2},{4,5},{5,4},{6,7},{7,6},{8,9},{9,8},{10,11... | collective-permute-start | bytes 786440 | tf_op jit(solution)/shard_map/ppermute | solution.py:507
  65.7 16.6 %collective-permute-start.14 = (bf16[2,512,256]{2,1,0:T(8,128)(2,1)S(1)}, bf16[2,512,256]{2,1,0:T(8,128)(2,1)S(1)}, u32[]{:S(2)}, u32[]{:S(2)}) collective-permute-start(bf16[2,512,256]{2,1,0:T(8,128)(2,1)S(1)} %get-tuple-element.83._after.edge), channel_id=1, source_target_pairs={{0,2},{1,3},{2,4},{3,5},{4,6},{5,7},{8,10},{9,11},{10,12},{11,13},... | collective-permute-start | bytes 1572872 | tf_op jit(solution)/shard_map/ppermute | solution.py:605
  71.6 18.2 %collective-permute-start.15 = (bf16[2,512,256]{2,1,0:T(8,128)(2,1)S(1)}, bf16[2,512,256]{2,1,0:T(8,128)(2,1)S(1)}, u32[]{:S(2)}, u32[]{:S(2)}) collective-permute-start(bf16[2,512,256]{2,1,0:T(8,128)(2,1)S(1)} %get-tuple-element.91), channel_id=1, source_target_pairs={{2,0},{3,1},{4,2},{5,3},{6,4},{7,5},{10,8},{11,9},{12,10},{13,11},... | collective-permute-start | bytes 1572872 | tf_op jit(solution)/shard_map/ppermute | solution.py:617
  80.3 9.5 %collective-permute-start.16 = (bf16[1,1024,128]{2,1,0:T(8,128)(2,1)S(1)}, bf16[1,1024,128]{2,1,0:T(8,128)(2,1)S(1)}, u32[]{:S(2)}, u32[]{:S(2)}) collective-permute-start(bf16[1,1024,128]{2,1,0:T(8,128)(2,1)S(1)} %get-tuple-element.89._after), channel_id=1, source_target_pairs={{0,1},{1,0},{2,3},{3,2},{4,5},{5,4},{6,7},{7,6},{8,9},{9,8},{10,11... | collective-permute-start | bytes 786440 | tf_op jit(solution)/shard_map/ppermute | solution.py:507
  80.8 17.5 %collective-permute-start.17 = (bf16[2,1024,128]{2,1,0:T(8,128)(2,1)S(1)}, bf16[2,1024,128]{2,1,0:T(8,128)(2,1)S(1)}, u32[]{:S(2)}, u32[]{:S(2)}) collective-permute-start(bf16[2,1024,128]{2,1,0:T(8,128)(2,1)S(1)} %get-tuple-element.96), channel_id=1, source_target_pairs={{0,1},{1,0},{2,3},{3,2},{4,5},{5,4},{6,7},{7,6},{8,9},{9,8},{10,11... | collective-permute-start | bytes 1572872 | tf_op jit(solution)/shard_map/ppermute | solution.py:507
  92.5 13.4 %collective-permute-start.19 = (bf16[1,512,128]{2,1,0:T(8,128)(2,1)S(1)}, bf16[1,512,128]{2,1,0:T(8,128)(2,1)S(1)}, u32[]{:S(2)}, u32[]{:S(2)}) collective-permute-start(bf16[1,512,128]{2,1,0:T(8,128)(2,1)S(1)} %get-tuple-element.102), channel_id=1, source_target_pairs={{0,6},{1,7},{2,0},{3,1},{4,2},{5,3},{6,4},{7,5},{8,14},{9,15},{10,... | collective-permute-start | bytes 393224 | tf_op jit(solution)/shard_map/ppermute | solution.py:504
  94.3 15.4 %collective-permute-start.20 = (bf16[1,512,128]{2,1,0:T(8,128)(2,1)S(1)}, bf16[1,512,128]{2,1,0:T(8,128)(2,1)S(1)}, u32[]{:S(2)}, u32[]{:S(2)}) collective-permute-start(bf16[1,512,128]{2,1,0:T(8,128)(2,1)S(1)} %get-tuple-element.103), channel_id=1, source_target_pairs={{0,4},{1,5},{2,6},{3,7},{4,0},{5,1},{6,2},{7,3},{8,12},{9,13},{10,... | collective-permute-start | bytes 393224 | tf_op jit(solution)/shard_map/ppermute | solution.py:504
  95.7 14.0 %collective-permute-start.21 = (bf16[1,512,128]{2,1,0:T(8,128)(2,1)S(1)}, bf16[1,512,128]{2,1,0:T(8,128)(2,1)S(1)}, u32[]{:S(2)}, u32[]{:S(2)}) collective-permute-start(bf16[1,512,128]{2,1,0:T(8,128)(2,1)S(1)} %get-tuple-element.104), channel_id=1, source_target_pairs={{0,2},{1,3},{2,4},{3,5},{4,6},{5,7},{6,0},{7,1},{8,10},{9,11},{10,... | collective-permute-start | bytes 393224 | tf_op jit(solution)/shard_map/ppermute | solution.py:504
  95.7 7.1 %collective-permute-start.18 = (f32[8,512]{1,0:T(8,128)S(1)}, f32[8,512]{1,0:T(8,128)S(1)}, u32[]{:S(2)}, u32[]{:S(2)}) collective-permute-start(f32[8,512]{1,0:T(8,128)S(1)} %get-tuple-element.90._after), channel_id=1, source_target_pairs={{2,0},{3,1},{4,2},{5,3},{6,4},{7,5},{10,8},{11,9},{12,10},{13,11},... | collective-permute-start | bytes 49160 | tf_op jit(solution)/shard_map/ppermute | solution.py:672
  104.7 26.0 %collective-permute-start.25 = (bf16[3,512,256]{2,1,0:T(8,128)(2,1)S(1)}, bf16[3,512,256]{2,1,0:T(8,128)(2,1)S(1)}, u32[]{:S(2)}, u32[]{:S(2)}) collective-permute-start(bf16[3,512,256]{2,1,0:T(8,128)(2,1)S(1)} %get-tuple-element.101._after), channel_id=1, source_target_pairs={{0,1},{1,0},{2,3},{3,2},{4,5},{5,4},{6,7},{7,6},{8,9},{9,8},{10,11... | collective-permute-start | bytes 2359304 | tf_op jit(solution)/shard_map/ppermute | solution.py:507
  105.3 7.3 %collective-permute-start.22 = (bf16[2,512,128]{2,1,0:T(8,128)(2,1)S(1)}, bf16[2,512,128]{2,1,0:T(8,128)(2,1)S(1)}, u32[]{:S(2)}, u32[]{:S(2)}) collective-permute-start(bf16[2,512,128]{2,1,0:T(8,128)(2,1)S(1)} %get-tuple-element.105), channel_id=1, source_target_pairs={{0,6},{1,7},{2,0},{3,1},{4,2},{5,3},{6,4},{7,5},{8,14},{9,15},{10,... | collective-permute-start | bytes 786440 | tf_op jit(solution)/shard_map/ppermute | solution.py:504
  106.0 24.7 %collective-permute-start.23 = (bf16[2,512,128]{2,1,0:T(8,128)(2,1)S(1)}, bf16[2,512,128]{2,1,0:T(8,128)(2,1)S(1)}, u32[]{:S(2)}, u32[]{:S(2)}) collective-permute-start(bf16[2,512,128]{2,1,0:T(8,128)(2,1)S(1)} %get-tuple-element.106), channel_id=1, source_target_pairs={{0,4},{1,5},{2,6},{3,7},{4,0},{5,1},{6,2},{7,3},{8,12},{9,13},{10,... | collective-permute-start | bytes 786440 | tf_op jit(solution)/shard_map/ppermute | solution.py:504
  111.5 19.2 %collective-permute-start.24 = (bf16[2,512,128]{2,1,0:T(8,128)(2,1)S(1)}, bf16[2,512,128]{2,1,0:T(8,128)(2,1)S(1)}, u32[]{:S(2)}, u32[]{:S(2)}) collective-permute-start(bf16[2,512,128]{2,1,0:T(8,128)(2,1)S(1)} %unsort_last.1), channel_id=1, source_target_pairs={{0,2},{1,3},{2,4},{3,5},{4,6},{5,7},{6,0},{7,1},{8,10},{9,11},{10,... | collective-permute-start | bytes 786440 | tf_op jit(solution)/shard_map/ppermute | solution.py:504

commit v3 on v2

--- a/solution.py
+++ b/solution.py
@@ -66,7 +66,13 @@
 
 def split_kernel(place, labels, q_hbm, k_hbm, v_hbm, x0, x1, x2, x3, own, send, held, sems):
     tok = q_hbm.shape[0]
-    copies = [pltpu.make_async_copy(source, held.at[i], sems.at[i]) for i, source in enumerate((q_hbm, k_hbm, v_hbm))]
+    cuts = sems.shape[1]
+    size = tok // cuts
+    copies = []
+    for i, source in enumerate((q_hbm, k_hbm, v_hbm)):
+        for n in range(cuts):
+            at = slice(n * size, (n + 1) * size)
+            copies.append(pltpu.make_async_copy(source.at[at], held.at[i, at], sems.at[i, n]))
     start_all(copies)
     for d, x in enumerate((x0, x1, x2, x3)):
         line = labels[pl.ds(lax.rem(place[0] + d, HR), 1), :].astype(F32)
@@ -75,7 +81,7 @@
         x[2 * tok :, :] = jnp.concatenate(parts, axis=0).astype(BF16)
     width = HL * HD // 2
     for i in range(3):
-        copies[i].wait()
+        wait_all(copies[i * cuts : (i + 1) * cuts])
         for d, x in enumerate((x0, x1, x2, x3)):
             if i < 2:
                 x[i * tok : (i + 1) * tok, :] = held[i, :, head_columns(place, d)]
@@ -301,13 +307,9 @@
         ot_ref[:, j * QB : end] = dot(vt[:, :end], p_ref[:end, j * QB : end])
 
 
-def grads_kernel(
-    unit, place, kept_ref, got_ref, sorted_ref, came_ref, q_ref, k_ref, v_ref, kt_ref, ot_ref, p_ref,
-    own_v, back_v, own_ref, back_ref, g_ref, dqt, res,
-):
+def value_grads_kernel(unit, place, kept_ref, got_ref, _after, sorted_ref, came_ref, p_ref, g_ref, own_ref, back_ref, res):
     tok = sorted_ref.shape[1]
-    half = CS // 2
-    count = CS // QB
+
     def own(d, u, to):
         g_ref[rows(to * unit, unit), :] = sorted_ref[d, rows(u * unit, unit), :]
 
@@ -315,27 +317,38 @@
         g_ref[rows(to * unit, unit), :] = came_ref[rows(at * unit, unit), :]
 
     each_unit(tok // unit, place, kept_ref, got_ref, own, got)
+    for lo in range(0, CS, QB):
+        res[lo : lo + QB, :] = dot(p_ref[lo : lo + QB, lo:], g_ref[lo:, :]).astype(BF16)
+
+    def own_out(d, u, to):
+        own_ref[d, 0, rows(u * unit, unit), :] = res[rows(to * unit, unit), :]
+
+    def got_out(at, to):
+        back_ref[0, rows(at * unit, unit), :] = res[rows(to * unit, unit), :]
+
+    each_unit(tok // unit, place, kept_ref, got_ref, own_out, got_out)
+
+
+def grads_kernel(
+    unit, place, kept_ref, got_ref, _after, q_ref, k_ref, v_ref, kt_ref, ot_ref, p_ref, g_ref, own_ref, back_ref, dqt, res
+):
+    tok = own_ref.shape[2]
     delta = jnp.sum(g_ref[...].astype(F32).T * ot_ref[...], axis=0, keepdims=True)
     factor = HD**-0.5
-    for i in range(count):
-        lo, hi = i * QB, (i + 1) * QB
-        p = p_ref[lo:hi, lo:]
-        g = g_ref[lo:, :]
-        res[2, lo:hi, :] = dot(p, g).astype(BF16)
-        dp = dot_nt(v_ref[lo:hi, :], g)
-        ds = (p.astype(F32) * (dp - delta[:, lo:])).astype(BF16)
+    for lo in range(0, CS, QB):
+        hi = lo + QB
+        dp = dot_nt(v_ref[lo:hi, :], g_ref[lo:, :])
+        ds = (p_ref[lo:hi, lo:].astype(F32) * (dp - delta[:, lo:])).astype(BF16)
         res[1, lo:hi, :] = (dot(ds, q_ref[lo:, :]) * factor).astype(BF16)
         part = dot(kt_ref[:, lo:hi], ds)
-        dqt[:, lo:] = part if i == 0 else dqt[:, lo:] + part
+        dqt[:, lo:] = part if lo == 0 else dqt[:, lo:] + part
     res[0] = (dqt[...].T * factor).astype(BF16)
 
     def own_out(d, u, to):
-        own_v[d, 0, rows(u * unit, unit), :] = res[2, rows(to * unit, unit), :]
         for i in range(2):
             own_ref[d, i, rows(u * unit, unit), :] = res[i, rows(to * unit, unit), :]
 
     def got_out(at, to):
-        back_v[0, rows(at * unit, unit), :] = res[2, rows(to * unit, unit), :]
         for i in range(2):
             back_ref[i, rows(at * unit, unit), :] = res[i, rows(to * unit, unit), :]
 
@@ -372,7 +385,7 @@
 
 
 def window_kernel(
-    place, _after, own, got, g_own, g_came, edge, dq_ref, early_ref, late_ref, stats_ref, *scratch
+    place, _after, _after_edge, own, got, g_own, g_came, edge, dq_ref, early_ref, late_ref, stats_ref, *scratch
 ):
     tok = own.shape[1]
     pair = 2 * tok
@@ -514,7 +527,7 @@
         out_shape=[struct(2 * tok + 16, HD)] * HR + [struct(3, tok, width)] * 2,
         in_specs=smem() + vmem() + hbm * 3,
         out_specs=vmem(6),
-        scratch_shapes=[pltpu.VMEM((3, tok, query.shape[2]), BF16), pltpu.SemaphoreType.DMA((3,))],
+        scratch_shapes=[pltpu.VMEM((3, tok, query.shape[2]), BF16), pltpu.SemaphoreType.DMA((3, 4))],
         compiler_params=params(SPLIT_MIB),
         cost_estimate=takes(2),
         name="split",
@@ -543,7 +556,7 @@
         ],
         in_specs=smem() + vmem(5),
         out_specs=vmem(4) + smem(),
-        compiler_params=params(32),
+        compiler_params=params(20),
         cost_estimate=takes(2.6),
         name="pack",
     )(where, v_sent[0], *arrived)
@@ -562,7 +575,7 @@
         ],
         out_specs=[pl.BlockSpec((tok, HD), lambda n: (0, 0))] * HR
         + [pl.BlockSpec((tok, width), lambda n: (0, 0))] * 2,
-        compiler_params=params(32),
+        compiler_params=params(20),
         cost_estimate=takes(3.8),
         name="project",
     )(where, send, local_got, boundary, out_weight[0])
@@ -616,20 +629,26 @@
     )(where, kept, got, edge, v_ordered, v_came, p, local_own, local_got, g_own)
     query_edge_got = lax.ppermute(query_edge, "seq", behind)
 
-    own_v, back_v, own, back = pl.pallas_call(
+    g, own_v, back_v = pl.pallas_call(
+        functools.partial(value_grads_kernel, unit),
+        out_shape=[struct(CS, HD), struct(HR, 1, tok, HD), struct(1, half, HD)],
+        in_specs=smem(3) + vmem(4),
+        out_specs=vmem(3),
+        scratch_shapes=[pltpu.VMEM((CS, HD), BF16)],
+        compiler_params=params(16),
+        cost_estimate=takes(2.4),
+        name="value_grads",
+    )(where, kept, got, ot, g_ordered, g_came, p)
+    own, back = pl.pallas_call(
         functools.partial(grads_kernel, unit),
-        out_shape=[struct(HR, 1, tok, HD), struct(1, half, HD), struct(HR, 2, tok, HD), struct(2, half, HD)],
+        out_shape=[struct(HR, 2, tok, HD), struct(2, half, HD)],
         in_specs=smem(3) + vmem(8),
-        out_specs=vmem(4),
-        scratch_shapes=[
-            pltpu.VMEM((CS, HD), BF16),
-            pltpu.VMEM((HD, CS), F32),
-            pltpu.VMEM((3, CS, HD), BF16),
-        ],
+        out_specs=vmem(2),
+        scratch_shapes=[pltpu.VMEM((HD, CS), F32), pltpu.VMEM((2, CS, HD), BF16)],
         compiler_params=params(24),
-        cost_estimate=takes(6.3),
+        cost_estimate=takes(5),
         name="grads",
-    )(where, kept, got, g_ordered, g_came, q, k, v, kt, ot, p)
+    )(where, kept, got, back_v, q, k, v, kt, ot, p, g)
 
     def unsort(distances, after, after_edge, own, returned, name):
         count = own.shape[1]
@@ -646,6 +665,8 @@
 
     returned_v, returned = swap(back_v), swap(back)
     pair = 2 * tok
+    natural_v = unsort((0, 1, 2, 3), back, back, own_v, returned_v, "unsort_value")
+    home_v = [natural_v[0]] + [among_groups(natural_v[d], -d) for d in range(1, HR)]
     dq_local, early, late, stats = pl.pallas_call(
         window_kernel,
         out_shape=[
@@ -654,7 +675,7 @@
             struct(2, tok, width, dtype=F32),
             struct(8, tok, dtype=F32),
         ],
-        in_specs=smem() + vmem(6),
+        in_specs=smem() + vmem(7),
         out_specs=vmem(4),
         scratch_shapes=[
             pltpu.VMEM((HL // 2, pair, HD), BF16),
@@ -666,13 +687,11 @@
             pltpu.VMEM((HL // 2, pair, HD), F32),
         ],
         compiler_params=params(24),
-        cost_estimate=takes(4),
+        cost_estimate=takes(0.1),
         name="window",
-    )(where, back_v, local_own, local_got, g_own, v_came, edge_got)
+    )(where, natural_v[0], query_edge_got, local_own, local_got, g_own, v_came, edge_got)
     stats_got = lax.ppermute(stats, "seq", behind)
-    natural_v = unsort((0, 1, 2, 3), stats, query_edge_got, own_v, returned_v, "unsort_value")
-    home_v = [natural_v[0]] + [among_groups(natural_v[d], -d) for d in range(1, HR)]
-    first_natural = unsort((0, 1, 2), natural_v[0], natural_v[0], own, returned, "unsort_first")
+    first_natural = unsort((0, 1, 2), stats, stats, own, returned, "unsort_first")
     settled_own, settled_send = pl.pallas_call(
         settle_kernel,
         out_shape=[struct(3, tok, width)] * 2,
@@ -702,7 +721,7 @@
         out_shape=[struct(tok, (HR + HL) * HD)] * 3,
         in_specs=smem() + vmem(7),
         out_specs=vmem(3),
-        compiler_params=params(32),
+        compiler_params=params(20),
         cost_estimate=takes(2.8),
         name="join",
     )(where, value_left, *home, settled_own, settled_got)

time: 134 us -> 130 us (0.970)
  waiting for transfers between devices: 46.2 us -> 39.9 us
  starting transfers between devices: 38.8 us -> 40.4 us
    ppermute x15, waiting for transfers between devices: 34.9 us -> 29 us  [among_groups(): return lax.ppermute(block, 'seq', route)]
    pallas_call x0 -> x1, Pallas kernels: none -> 2.5 us  [pair_body(): pl.pallas_call(functools.partial(value_grads_kernel, unit), out_shape=[st...]
    ppermute x1, waiting for transfers between devices: 2.38 us -> 0.01 us  [pair_body(): stats_got = lax.ppermute(stats, 'seq', behind)]
    ppermute x1, waiting for transfers between devices: 0.01 us -> 1.86 us  [pair_body(): query_edge_got = lax.ppermute(query_edge, 'seq', behind)]
    pallas_call x1, Pallas kernels: 6.41 us -> 4.63 us  [pair_body(): pl.pallas_call(functools.partial(grads_kernel, unit), out_shape=[struct(H...]
  transfers between devices with their start and end apart: 26 -> 26, of which waited for: 9 -> 8; matrix products, arithmetic and copies ran while one was open for 0% -> 1% of each run, Pallas kernels for 32% -> 34%
where the time goes in v3:
time: 130 us
  Pallas kernels  46.7 us (36%)
  starting transfers between devices  40.4 us (31%)
  waiting for transfers between devices  39.9 us (31%)
    ppermute x15, waiting for transfers between devices, among_groups(): return lax.ppermute(block, 'seq', route)  29 us
    ppermute x15, starting transfers between devices, among_groups(): return lax.ppermute(block, 'seq', route)  26.2 us
    ppermute x7, waiting for transfers between devices, swap(): return lax.ppermute(block, 'seq', [(i, i ^ 1) for i in range(devices)])  9.05 us
    ppermute x7, starting transfers between devices, swap(): return lax.ppermute(block, 'seq', [(i, i ^ 1) for i in range(devices)])  7.66 us
    pallas_call x1, Pallas kernels, pair_body(): pl.pallas_call(window_kernel, out_shape=[struct(2, tok, width), struct(2,...  7.36 us
    pallas_call x3, Pallas kernels, unsort(): pl.pallas_call(functools.partial(unsort_kernel, unit, distances), out_sha...  6.02 us
    pallas_call x1, Pallas kernels, pair_body(): pl.pallas_call(functools.partial(probs_kernel, unit), out_shape=[struct(H...  5.11 us
    pallas_call x1, Pallas kernels, pair_body(): pl.pallas_call(functools.partial(grads_kernel, unit), out_shape=[struct(H...  4.63 us
  transfers between devices with their start and end apart: 26, of which 8 were waited for; matrix products, arithmetic and copies ran while one was open for 1% of the time, Pallas kernels for 34%

profile of v3, /device:TPU:0, one launch (start us, length us, event | category | flops | bytes accessed | tf_op | source)
XLA Modules:
  0.0 129.5 jit_solution(12779771476425645485)
XLA Ops:
  0.6 2.4 %collective-permute-start.4 = (bf16[1,512,2048]{2,1,0:T(8,128)(2,1)}, bf16[1,512,2048]{2,1,0:T(8,128)(2,1)S(1)}, u32[]{:S(2)}, u32[]{:S(2)}) collective-permute-start(bf16[1,512,2048]{2,1,0:T(8,128)(2,1)} %param.9), channel_id=1, source_target_pairs={{8,0},{16,8},{24,16},{0,24},{9,1},{17,9},{25,17},{1,25},{10,2},{18... | collective-permute-start | bytes 6291464 | tf_op jit(solution)/shard_map/ppermute | solution.py:734
  3.7 4.1 %split.1 = (bf16[1040,128]{1,0:T(8,128)(2,1)}, bf16[1040,128]{1,0:T(8,128)(2,1)}, bf16[1040,128]{1,0:T(8,128)(2,1)}, bf16[1040,128]{1,0:T(8,128)(2,1)}, bf16[3,5...) custom-call(s32[2]{0:T(128)} %pad_add_fusion.place, s32[4,512]{1,0:T(4,128)} %bitcast.17, bf16[512,1024]{1,0:T(8,128)(2,1)} %bitcast.15, ...), custom_call_target="tpu_custom_call" | custom-call | flops 2200000000 | bytes 7000000 | tf_op jit(solution)/shard_map/split/pallas_call | solution.py:525
  7.9 1.6 %collective-permute-start.3 = (bf16[3,512,256]{2,1,0:T(8,128)(2,1)}, bf16[3,512,256]{2,1,0:T(8,128)(2,1)S(1)}, u32[]{:S(2)}, u32[]{:S(2)}) collective-permute-start(bf16[3,512,256]{2,1,0:T(8,128)(2,1)} %get-tuple-element.65), channel_id=1, source_target_pairs={{0,1},{1,0},{2,3},{3,2},{4,5},{5,4},{6,7},{7,6},{8,9},{9,8},{10,11... | collective-permute-start | bytes 2359304 | tf_op jit(solution)/shard_map/ppermute | solution.py:520
  9.5 1.6 %collective-permute-start = (bf16[1040,128]{1,0:T(8,128)(2,1)}, bf16[1040,128]{1,0:T(8,128)(2,1)S(1)}, u32[]{:S(2)}, u32[]{:S(2)}) collective-permute-start(bf16[1040,128]{1,0:T(8,128)(2,1)} %get-tuple-element.58), channel_id=1, source_target_pairs={{0,2},{1,3},{2,4},{3,5},{4,6},{5,7},{6,0},{7,1},{8,10},{9,11},{10,... | collective-permute-start | bytes 798728 | tf_op jit(solution)/shard_map/ppermute | solution.py:517
  11.0 2.6 %collective-permute-start.1 = (bf16[1040,128]{1,0:T(8,128)(2,1)}, bf16[1040,128]{1,0:T(8,128)(2,1)S(1)}, u32[]{:S(2)}, u32[]{:S(2)}) collective-permute-start(bf16[1040,128]{1,0:T(8,128)(2,1)} %get-tuple-element.59), channel_id=1, source_target_pairs={{0,4},{1,5},{2,6},{3,7},{4,0},{5,1},{6,2},{7,3},{8,12},{9,13},{10,... | collective-permute-start | bytes 798728 | tf_op jit(solution)/shard_map/ppermute | solution.py:517
  15.0 6.0 %collective-permute-done._after1.x1 = bf16[1040,128]{1,0:T(8,128)(2,1)S(1)} collective-permute-done((bf16[1040,128]{1,0:T(8,128)(2,1)}, bf16[1040,128]{1,0:T(8,128)(2,1)S(1)}, u32[]{:S(2)}, u32[]{:S(2)}) %collective-permute-start) | collective-permute-done | bytes 266272 | tf_op jit(solution)/shard_map/ppermute | solution.py:517
  21.0 9.7 %collective-permute-done.1._after2.x2 = bf16[1040,128]{1,0:T(8,128)(2,1)S(1)} collective-permute-done((bf16[1040,128]{1,0:T(8,128)(2,1)}, bf16[1040,128]{1,0:T(8,128)(2,1)S(1)}, u32[]{:S(2)}, u32[]{:S(2)}) %collective-permute-start.1) | collective-permute-done | bytes 266272 | tf_op jit(solution)/shard_map/ppermute | solution.py:517
  31.4 6.2 %collective-permute-start.5 = (bf16[512,128]{1,0:T(8,128)(2,1)S(1)}, bf16[512,128]{1,0:T(8,128)(2,1)S(1)}, u32[]{:S(2)}, u32[]{:S(2)}) collective-permute-start(bf16[512,128]{1,0:T(8,128)(2,1)S(1)} %get-tuple-element.68), channel_id=1, source_target_pairs={{0,2},{1,3},{2,4},{3,5},{4,6},{5,7},{6,0},{7,1},{8,10},{9,11},{10,... | collective-permute-start | bytes 393224 | tf_op jit(solution)/shard_map/ppermute | solution.py:517
  37.6 1.6 %collective-permute-start.6 = (bf16[512,128]{1,0:T(8,128)(2,1)S(1)}, bf16[512,128]{1,0:T(8,128)(2,1)S(1)}, u32[]{:S(2)}, u32[]{:S(2)}) collective-permute-start(bf16[512,128]{1,0:T(8,128)(2,1)S(1)} %get-tuple-element.69), channel_id=1, source_target_pairs={{0,4},{1,5},{2,6},{3,7},{4,0},{5,1},{6,2},{7,3},{8,12},{9,13},{10,... | collective-permute-start | bytes 393224 | tf_op jit(solution)/shard_map/ppermute | solution.py:517
  41.0 2.6 %pack.1 = (bf16[4,2,512,128]{3,2,1,0:T(8,128)(2,1)S(1)}, bf16[2064,128]{1,0:T(8,128)(2,1)S(1)}, f32[8,512]{1,0:T(8,128)S(1)}, f32[512,128]{1,0:T(8,128)S(1)}, s32[4]{0:T(128)S(1)}) custom-call(s32[2]{0:T(128)S(1)} %copy-done.1, bf16[512,128]{1,0:T(8,128)(2,1)S(1)} %get-tuple-element.61._after.x0, bf16[1040,128]{1,0:T(8,128)(2,1)S(1)} %copy-done.4, ...), custom_call_target="tpu_custom_call" | custom-call | flops 2860000000 | bytes 9100000 | tf_op jit(solution)/shard_map/pack/pallas_call | solution.py:548
  44.2 3.8 %project.1 = (bf16[512,128]{1,0:T(8,128)(2,1)S(1)}, bf16[512,128]{1,0:T(8,128)(2,1)S(1)}, bf16[512,128]{1,0:T(8,128)(2,1)S(1)}, bf16[512,128]{1,0:T(8,128)(2,1)S...) custom-call(s32[2]{0:T(128)S(1)} %copy-done.1, bf16[2064,128]{1,0:T(8,128)(2,1)S(1)} %get-tuple-element.64._after, ...), custom_call_target="tpu_custom_call" | custom-call | flops 4180000000 | bytes 13300000 | tf_op jit(solution)/shard_map/project/pallas_call | solution.py:565
  48.8 2.9 %collective-permute-start.11 = (bf16[512,128]{1,0:T(8,128)(2,1)S(1)}, bf16[512,128]{1,0:T(8,128)(2,1)S(1)}, u32[]{:S(2)}, u32[]{:S(2)}) collective-permute-start(bf16[512,128]{1,0:T(8,128)(2,1)S(1)} %get-tuple-element.78), channel_id=1, source_target_pairs={{0,6},{1,7},{2,0},{3,1},{4,2},{5,3},{6,4},{7,5},{8,14},{9,15},{10,... | collective-permute-start | bytes 393224 | tf_op jit(solution)/shard_map/ppermute | solution.py:517
  53.1 1.6 %collective-permute-start.12 = (bf16[2048,128]{1,0:T(8,128)(2,1)S(1)}, bf16[2048,128]{1,0:T(8,128)(2,1)S(1)}, u32[]{:S(2)}, u32[]{:S(2)}) collective-permute-start(bf16[2048,128]{1,0:T(8,128)(2,1)S(1)} %get-tuple-element.72._after), channel_id=1, source_target_pairs={{0,1},{1,0},{2,3},{3,2},{4,5},{5,4},{6,7},{7,6},{8,9},{9,8},{10,11... | collective-permute-start | bytes 1572872 | tf_op jit(solution)/shard_map/ppermute | solution.py:520
  54.7 4.0 %collective-permute-done.8.came_ref = bf16[2064,128]{1,0:T(8,128)(2,1)S(1)} collective-permute-done((bf16[2064,128]{1,0:T(8,128)(2,1)S(1)}, bf16[2064,128]{1,0:T(8,128)(2,1)S(1)}, u32[]{:S(2)}, u32[]{:S(2)}) %collective-permute-start.8) | collective-permute-done | bytes 528416 | tf_op jit(solution)/shard_map/ppermute | solution.py:520
  58.7 5.1 %probs.1 = (s32[4]{0:T(128)S(1)}, bf16[2048,128]{1,0:T(8,128)(2,1)S(1)}, bf16[2048,128]{1,0:T(8,128)(2,1)S(1)}, bf16[128,2048]{1,0:T(8,128)(2,1)S(1)}, bf16[2048,2048]{1,0:T(8,128)(2,1)S(1)}) custom-call(s32[2]{0:T(128)S(1)} %copy-done.1, s32[4]{0:T(128)S(1)} %get-tuple-element.63.kept_ref, bf16[2048,128]{1,0:T(8,128)(2,1)S(1)} %get-tuple-element.72._after, ...), custom_call_target="tpu_custom_call" | custom-call | flops 5500000256 | bytes 17500000 | tf_op jit(solution)/shard_map/probs/pallas_call | solution.py:595
  67.2 2.7 %collective-permute-done.12.came_ref.g_came = bf16[2048,128]{1,0:T(8,128)(2,1)S(1)} collective-permute-done((bf16[2048,128]{1,0:T(8,128)(2,1)S(1)}, bf16[2048,128]{1,0:T(8,128)(2,1)S(1)}, u32[]{:S(2)}, u32[]{:S(2)}) %collective-permute-start.12) | collective-permute-done | bytes 524320 | tf_op jit(solution)/shard_map/ppermute | solution.py:520
  69.9 1.7 %mix.1 = (bf16[2048,128]{1,0:T(8,128)(2,1)S(1)}, f32[128,2048]{1,0:T(8,128)S(1)}, bf16[2,512,256]{2,1,0:T(8,128)(2,1)S(1)}) custom-call(s32[2]{0:T(128)S(1)} %copy-done.1, s32[4]{0:T(128)S(1)} %get-tuple-element.63.kept_ref, s32[4]{0:T(128)S(1)} %get-tuple-element.74.got_ref, bf16[2,512,256]{2,1,0:T(8,128)(2,1)S(1)} %get-tuple-element.80._after.edge, ...), custom_call_target="tpu_custom_call" | custom-call | flops 1870000000 | bytes 5950000 | tf_op jit(solution)/shard_map/mix/pallas_call | solution.py:620
  71.6 2.3 %collective-permute-done.13.came_ref = bf16[1024,128]{1,0:T(8,128)(2,1)S(1)} collective-permute-done((bf16[1024,128]{1,0:T(8,128)(2,1)S(1)}, bf16[1024,128]{1,0:T(8,128)(2,1)S(1)}, u32[]{:S(2)}, u32[]{:S(2)}) %collective-permute-start.13) | collective-permute-done | bytes 262176 | tf_op jit(solution)/shard_map/ppermute | solution.py:520
  74.0 2.5 %value_grads.1 = (bf16[2048,128]{1,0:T(8,128)(2,1)S(1)}, bf16[4,1,512,128]{3,2,1,0:T(8,128)(2,1)S(1)}, bf16[1,1024,128]{2,1,0:T(8,128)(2,1)S(1)}) custom-call(s32[2]{0:T(128)S(1)} %copy-done.1, s32[4]{0:T(128)S(1)} %get-tuple-element.63.kept_ref, s32[4]{0:T(128)S(1)} %get-tuple-element.74.got_ref, f32[128,2048]{1,0:T(8,128)S(1)} %get-tuple-element.84._after.ot_ref, ...), custom_call_target="tpu_custom_call" | custom-call | flops 2640000000 | bytes 8400000 | tf_op jit(solution)/shard_map/value_grads/pallas_call | solution.py:632
  77.0 1.5 %collective-permute-start.15 = (bf16[2,512,256]{2,1,0:T(8,128)(2,1)S(1)}, bf16[2,512,256]{2,1,0:T(8,128)(2,1)S(1)}, u32[]{:S(2)}, u32[]{:S(2)}) collective-permute-start(bf16[2,512,256]{2,1,0:T(8,128)(2,1)S(1)} %get-tuple-element.96), channel_id=1, source_target_pairs={{2,0},{3,1},{4,2},{5,3},{6,4},{7,5},{10,8},{11,9},{12,10},{13,11},... | collective-permute-start | bytes 1572872 | tf_op jit(solution)/shard_map/ppermute | solution.py:630
  78.5 4.6 %grads.1 = (bf16[4,2,512,128]{3,2,1,0:T(8,128)(2,1)S(1)}, bf16[2,1024,128]{2,1,0:T(8,128)(2,1)S(1)}) custom-call(s32[2]{0:T(128)S(1)} %copy-done.1, s32[4]{0:T(128)S(1)} %get-tuple-element.63.kept_ref, s32[4]{0:T(128)S(1)} %get-tuple-element.74.got_ref, bf16[1,1024,128]{2,1,0:T(8,128)(2,1)S(1)} %get-tuple-element.87._after, ...), custom_call_target="tpu_custom_call" | custom-call | flops 5500000256 | bytes 17500000 | tf_op jit(solution)/shard_map/grads/pallas_call | solution.py:642
  83.1 1.6 %collective-permute-start.17 = (bf16[2,1024,128]{2,1,0:T(8,128)(2,1)S(1)}, bf16[2,1024,128]{2,1,0:T(8,128)(2,1)S(1)}, u32[]{:S(2)}, u32[]{:S(2)}) collective-permute-start(bf16[2,1024,128]{2,1,0:T(8,128)(2,1)S(1)} %get-tuple-element.92._after._after_edge), channel_id=1, source_target_pairs={{0,1},{1,0},{2,3},{3,2},{4,5},{5,4},{6,7},{7,6},{8,9},{9,8},{10,11... | collective-permute-start | bytes 1572872 | tf_op jit(solution)/shard_map/ppermute | solution.py:520
  84.7 2.6 %unsort_value.1 = (bf16[1,512,128]{2,1,0:T(8,128)(2,1)S(1)}, bf16[1,512,128]{2,1,0:T(8,128)(2,1)S(1)}, bf16[1,512,128]{2,1,0:T(8,128)(2,1)S(1)}, bf16[1,512,128]{2,1,0:T(8,128)(2,1)S(1)}) custom-call(s32[4]{0:T(128)S(1)} %get-tuple-element.63.kept_ref, bf16[2,1024,128]{2,1,0:T(8,128)(2,1)S(1)} %get-tuple-element.92._after._after_edge, ...), custom_call_target="tpu_custom_call" | custom-call | flops 2860000000 | bytes 9100000 | tf_op jit(solution)/shard_map/unsort_value/pallas_call | solution.py:655
  87.3 2.7 %collective-permute-start.19 = (bf16[1,512,128]{2,1,0:T(8,128)(2,1)S(1)}, bf16[1,512,128]{2,1,0:T(8,128)(2,1)S(1)}, u32[]{:S(2)}, u32[]{:S(2)}) collective-permute-start(bf16[1,512,128]{2,1,0:T(8,128)(2,1)S(1)} %get-tuple-element.104), channel_id=1, source_target_pairs={{0,6},{1,7},{2,0},{3,1},{4,2},{5,3},{6,4},{7,5},{8,14},{9,15},{10,... | collective-permute-start | bytes 393224 | tf_op jit(solution)/shard_map/ppermute | solution.py:517
  90.0 1.5 %collective-permute-start.20 = (bf16[1,512,128]{2,1,0:T(8,128)(2,1)S(1)}, bf16[1,512,128]{2,1,0:T(8,128)(2,1)S(1)}, u32[]{:S(2)}, u32[]{:S(2)}) collective-permute-start(bf16[1,512,128]{2,1,0:T(8,128)(2,1)S(1)} %get-tuple-element.105), channel_id=1, source_target_pairs={{0,4},{1,5},{2,6},{3,7},{4,0},{5,1},{6,2},{7,3},{8,12},{9,13},{10,... | collective-permute-start | bytes 393224 | tf_op jit(solution)/shard_map/ppermute | solution.py:517
  91.5 1.9 %collective-permute-done.15._after_edge.ahead = bf16[2,512,256]{2,1,0:T(8,128)(2,1)S(1)} collective-permute-done((bf16[2,512,256]{2,1,0:T(8,128)(2,1)S(1)}, bf16[2,512,256]{2,1,0:T(8,128)(2,1)S(1)}, u32[]{:S(2)}, u32[]{:S(2)}) %collective-permute-start.15) | collective-permute-done | bytes 524320 | tf_op jit(solution)/shard_map/ppermute | solution.py:630
  93.3 7.4 %window.1 = (bf16[2,512,256]{2,1,0:T(8,128)(2,1)S(1)}, bf16[2,512,256]{2,1,0:T(8,128)(2,1)S(1)}, f32[2,512,256]{2,1,0:T(8,128)S(1)}, f32[8,512]{1,0:T(8,128)S(1)}) custom-call(s32[2]{0:T(128)S(1)} %copy-done.1, bf16[1,512,128]{2,1,0:T(8,128)(2,1)S(1)} %get-tuple-element.95._after.v0, bf16[2,512,256]{2,1,0:T(8,128)(2,1)S(1)} %collective-permute-done.15._after_edge.ahead, ...), custom_call_target="tpu_custom_call" | custom-call | flops 110000000 | bytes 350000 | tf_op jit(solution)/shard_map/window/pallas_call | solution.py:670
  102.0 2.4 %unsort_first.1 = (bf16[2,512,128]{2,1,0:T(8,128)(2,1)S(1)}, bf16[2,512,128]{2,1,0:T(8,128)(2,1)S(1)}, bf16[2,512,128]{2,1,0:T(8,128)(2,1)S(1)}) custom-call(s32[4]{0:T(128)S(1)} %get-tuple-element.63.kept_ref, f32[8,512]{1,0:T(8,128)S(1)} %get-tuple-element.97._after._after_edge, f32[8,512]{1,0:T(8,128)S(1)} %get-tuple-element.97._after._after_edge, ...), custom_call_target="tpu_custom_call" | custom-call | flops 110000000 | bytes 350000 | tf_op jit(solution)/shard_map/unsort_first/pallas_call | solution.py:655
  104.4 3.1 %collective-permute-start.22 = (bf16[2,512,128]{2,1,0:T(8,128)(2,1)S(1)}, bf16[2,512,128]{2,1,0:T(8,128)(2,1)S(1)}, u32[]{:S(2)}, u32[]{:S(2)}) collective-permute-start(bf16[2,512,128]{2,1,0:T(8,128)(2,1)S(1)} %get-tuple-element.107), channel_id=1, source_target_pairs={{0,6},{1,7},{2,0},{3,1},{4,2},{5,3},{6,4},{7,5},{8,14},{9,15},{10,... | collective-permute-start | bytes 786440 | tf_op jit(solution)/shard_map/ppermute | solution.py:517
  108.5 1.9 %settle.1 = (bf16[3,512,256]{2,1,0:T(8,128)(2,1)S(1)}, bf16[3,512,256]{2,1,0:T(8,128)(2,1)S(1)}) custom-call(s32[2]{0:T(128)S(1)} %copy-done.1, bf16[2,512,128]{2,1,0:T(8,128)(2,1)S(1)} %get-tuple-element.99._after.y0, bf16[2,512,256]{2,1,0:T(8,128)(2,1)S(1)} %get-tuple-element.100.dq_ref, bf16[2,512,256]{2,1,0:T(8,128)(2,1)S(1)} %get-tuple-element.101.early_ref, ...), custom_call_target="tpu_custom_call" | custom-call | flops 110000000 | bytes 350000 | tf_op jit(solution)/shard_map/settle/pallas_call | solution.py:695
  114.2 12.5 %collective-permute-done.23.y2 = bf16[2,512,128]{2,1,0:T(8,128)(2,1)S(1)} collective-permute-done((bf16[2,512,128]{2,1,0:T(8,128)(2,1)S(1)}, bf16[2,512,128]{2,1,0:T(8,128)(2,1)S(1)}, u32[]{:S(2)}, u32[]{:S(2)}) %collective-permute-start.23) | collective-permute-done | bytes 262176 | tf_op jit(solution)/shard_map/ppermute | solution.py:517
  126.8 2.8 %join.1 = (bf16[512,1024]{1,0:T(8,128)(2,1)}, bf16[512,1024]{1,0:T(8,128)(2,1)}, bf16[512,1024]{1,0:T(8,128)(2,1)}) custom-call(s32[2]{0:T(128)S(1)} %copy-done.1, bf16[512,512]{1,0:T(8,128)(2,1)S(1)} %join_value.1._after._after_edge.value_ref, bf16[2,512,128]{2,1,0:T(8,128)(2,1)S(1)} %get-tuple-element.99._after.y0, ...), custom_call_target="tpu_custom_call" | custom-call | flops 3080000000 | bytes 9800000 | tf_op jit(solution)/shard_map/join/pallas_call | solution.py:719
  (48 shorter events, 17.3 us)
Async XLA Ops:
  0.6 30.1 %copy-start.3 = (bf16[1,512,1024]{2,1,0:T(8,128)(2,1)S(1)}, bf16[1,512,1024]{2,1,0:T(8,128)(2,1)}, u32[]{:S(2)}) copy-start(bf16[1,512,1024]{2,1,0:T(8,128)(2,1)} %param.8) | copy-start | bytes 3145732
  0.6 43.6 %collective-permute-start.4 = (bf16[1,512,2048]{2,1,0:T(8,128)(2,1)}, bf16[1,512,2048]{2,1,0:T(8,128)(2,1)S(1)}, u32[]{:S(2)}, u32[]{:S(2)}) collective-permute-start(bf16[1,512,2048]{2,1,0:T(8,128)(2,1)} %param.9), channel_id=1, source_target_pairs={{8,0},{16,8},{24,16},{0,24},{9,1},{17,9},{25,17},{1,25},{10,2},{18... | collective-permute-start | bytes 6291464 | tf_op jit(solution)/shard_map/ppermute | solution.py:734
  3.7 27.0 %copy-start.1 = (s32[2]{0:T(128)S(1)}, s32[2]{0:T(128)}, u32[]{:S(2)}) copy-start(s32[2]{0:T(128)} %pad_add_fusion.place) | copy-start | bytes 28
  7.9 35.8 %collective-permute-start.3 = (bf16[3,512,256]{2,1,0:T(8,128)(2,1)}, bf16[3,512,256]{2,1,0:T(8,128)(2,1)S(1)}, u32[]{:S(2)}, u32[]{:S(2)}) collective-permute-start(bf16[3,512,256]{2,1,0:T(8,128)(2,1)} %get-tuple-element.65), channel_id=1, source_target_pairs={{0,1},{1,0},{2,3},{3,2},{4,5},{5,4},{6,7},{7,6},{8,9},{9,8},{10,11... | collective-permute-start | bytes 2359304 | tf_op jit(solution)/shard_map/ppermute | solution.py:520
  9.5 11.5 %collective-permute-start = (bf16[1040,128]{1,0:T(8,128)(2,1)}, bf16[1040,128]{1,0:T(8,128)(2,1)S(1)}, u32[]{:S(2)}, u32[]{:S(2)}) collective-permute-start(bf16[1040,128]{1,0:T(8,128)(2,1)} %get-tuple-element.58), channel_id=1, source_target_pairs={{0,2},{1,3},{2,4},{3,5},{4,6},{5,7},{6,0},{7,1},{8,10},{9,11},{10,... | collective-permute-start | bytes 798728 | tf_op jit(solution)/shard_map/ppermute | solution.py:517
  11.0 19.6 %collective-permute-start.1 = (bf16[1040,128]{1,0:T(8,128)(2,1)}, bf16[1040,128]{1,0:T(8,128)(2,1)S(1)}, u32[]{:S(2)}, u32[]{:S(2)}) collective-permute-start(bf16[1040,128]{1,0:T(8,128)(2,1)} %get-tuple-element.59), channel_id=1, source_target_pairs={{0,4},{1,5},{2,6},{3,7},{4,0},{5,1},{6,2},{7,3},{8,12},{9,13},{10,... | collective-permute-start | bytes 798728 | tf_op jit(solution)/shard_map/ppermute | solution.py:517
  13.6 17.1 %collective-permute-start.2 = (bf16[1040,128]{1,0:T(8,128)(2,1)}, bf16[1040,128]{1,0:T(8,128)(2,1)S(1)}, u32[]{:S(2)}, u32[]{:S(2)}) collective-permute-start(bf16[1040,128]{1,0:T(8,128)(2,1)} %get-tuple-element.60), channel_id=1, source_target_pairs={{0,6},{1,7},{2,0},{3,1},{4,2},{5,3},{6,4},{7,5},{8,14},{9,15},{10,... | collective-permute-start | bytes 798728 | tf_op jit(solution)/shard_map/ppermute | solution.py:517
  31.4 17.4 %collective-permute-start.5 = (bf16[512,128]{1,0:T(8,128)(2,1)S(1)}, bf16[512,128]{1,0:T(8,128)(2,1)S(1)}, u32[]{:S(2)}, u32[]{:S(2)}) collective-permute-start(bf16[512,128]{1,0:T(8,128)(2,1)S(1)} %get-tuple-element.68), channel_id=1, source_target_pairs={{0,2},{1,3},{2,4},{3,5},{4,6},{5,7},{6,0},{7,1},{8,10},{9,11},{10,... | collective-permute-start | bytes 393224 | tf_op jit(solution)/shard_map/ppermute | solution.py:517
  37.6 14.1 %collective-permute-start.6 = (bf16[512,128]{1,0:T(8,128)(2,1)S(1)}, bf16[512,128]{1,0:T(8,128)(2,1)S(1)}, u32[]{:S(2)}, u32[]{:S(2)}) collective-permute-start(bf16[512,128]{1,0:T(8,128)(2,1)S(1)} %get-tuple-element.69), channel_id=1, source_target_pairs={{0,4},{1,5},{2,6},{3,7},{4,0},{5,1},{6,2},{7,3},{8,12},{9,13},{10,... | collective-permute-start | bytes 393224 | tf_op jit(solution)/shard_map/ppermute | solution.py:517
  39.2 12.5 %collective-permute-start.7 = (bf16[512,128]{1,0:T(8,128)(2,1)S(1)}, bf16[512,128]{1,0:T(8,128)(2,1)S(1)}, u32[]{:S(2)}, u32[]{:S(2)}) collective-permute-start(bf16[512,128]{1,0:T(8,128)(2,1)S(1)} %get-tuple-element.70), channel_id=1, source_target_pairs={{0,6},{1,7},{2,0},{3,1},{4,2},{5,3},{6,4},{7,5},{8,14},{9,15},{10,... | collective-permute-start | bytes 393224 | tf_op jit(solution)/shard_map/ppermute | solution.py:517
  40.0 1.0 copy-start.4
  41.0 3.2 %copy-start.2 = (bf16[1,1024,2048]{2,1,0:T(8,128)(2,1)S(1)}, bf16[1,1024,2048]{2,1,0:T(8,128)(2,1)}, u32[]{:S(2)}) copy-start(bf16[1,1024,2048]{2,1,0:T(8,128)(2,1)} %param.10) | copy-start | bytes 12582916
  43.7 15.0 %collective-permute-start.8 = (bf16[2064,128]{1,0:T(8,128)(2,1)S(1)}, bf16[2064,128]{1,0:T(8,128)(2,1)S(1)}, u32[]{:S(2)}, u32[]{:S(2)}) collective-permute-start(bf16[2064,128]{1,0:T(8,128)(2,1)S(1)} %get-tuple-element.64._after), channel_id=1, source_target_pairs={{0,1},{1,0},{2,3},{3,2},{4,5},{5,4},{6,7},{7,6},{8,9},{9,8},{10,11... | collective-permute-start | bytes 1585160 | tf_op jit(solution)/shard_map/ppermute | solution.py:520
  48.1 15.7 %collective-permute-start.10 = (bf16[512,128]{1,0:T(8,128)(2,1)S(1)}, bf16[512,128]{1,0:T(8,128)(2,1)S(1)}, u32[]{:S(2)}, u32[]{:S(2)}) collective-permute-start(bf16[512,128]{1,0:T(8,128)(2,1)S(1)} %get-tuple-element.77), channel_id=1, source_target_pairs={{0,4},{1,5},{2,6},{3,7},{4,0},{5,1},{6,2},{7,3},{8,12},{9,13},{10,... | collective-permute-start | bytes 393224 | tf_op jit(solution)/shard_map/ppermute | solution.py:517
  48.8 15.0 %collective-permute-start.11 = (bf16[512,128]{1,0:T(8,128)(2,1)S(1)}, bf16[512,128]{1,0:T(8,128)(2,1)S(1)}, u32[]{:S(2)}, u32[]{:S(2)}) collective-permute-start(bf16[512,128]{1,0:T(8,128)(2,1)S(1)} %get-tuple-element.78), channel_id=1, source_target_pairs={{0,6},{1,7},{2,0},{3,1},{4,2},{5,3},{6,4},{7,5},{8,14},{9,15},{10,... | collective-permute-start | bytes 393224 | tf_op jit(solution)/shard_map/ppermute | solution.py:517
  51.7 12.1 %collective-permute-start.9 = (bf16[512,128]{1,0:T(8,128)(2,1)S(1)}, bf16[512,128]{1,0:T(8,128)(2,1)S(1)}, u32[]{:S(2)}, u32[]{:S(2)}) collective-permute-start(bf16[512,128]{1,0:T(8,128)(2,1)S(1)} %get-tuple-element.76), channel_id=1, source_target_pairs={{0,2},{1,3},{2,4},{3,5},{4,6},{5,7},{6,0},{7,1},{8,10},{9,11},{10,... | collective-permute-start | bytes 393224 | tf_op jit(solution)/shard_map/ppermute | solution.py:517
  53.1 16.8 %collective-permute-start.12 = (bf16[2048,128]{1,0:T(8,128)(2,1)S(1)}, bf16[2048,128]{1,0:T(8,128)(2,1)S(1)}, u32[]{:S(2)}, u32[]{:S(2)}) collective-permute-start(bf16[2048,128]{1,0:T(8,128)(2,1)S(1)} %get-tuple-element.72._after), channel_id=1, source_target_pairs={{0,1},{1,0},{2,3},{3,2},{4,5},{5,4},{6,7},{7,6},{8,9},{9,8},{10,11... | collective-permute-start | bytes 1572872 | tf_op jit(solution)/shard_map/ppermute | solution.py:520
  58.7 5.1 %copy-start = (bf16[3,512,256]{2,1,0:T(8,128)(2,1)S(1)}, bf16[3,512,256]{2,1,0:T(8,128)(2,1)}, u32[]{:S(2)}) copy-start(bf16[3,512,256]{2,1,0:T(8,128)(2,1)} %get-tuple-element.79.own) | copy-start | bytes 2359300
  65.2 8.7 %collective-permute-start.13 = (bf16[1024,128]{1,0:T(8,128)(2,1)S(1)}, bf16[1024,128]{1,0:T(8,128)(2,1)S(1)}, u32[]{:S(2)}, u32[]{:S(2)}) collective-permute-start(bf16[1024,128]{1,0:T(8,128)(2,1)S(1)} %get-tuple-element.86), channel_id=1, source_target_pairs={{0,1},{1,0},{2,3},{3,2},{4,5},{5,4},{6,7},{7,6},{8,9},{9,8},{10,11... | collective-permute-start | bytes 786440 | tf_op jit(solution)/shard_map/ppermute | solution.py:520
  65.8 25.6 %collective-permute-start.16 = (bf16[2,512,256]{2,1,0:T(8,128)(2,1)S(1)}, bf16[2,512,256]{2,1,0:T(8,128)(2,1)S(1)}, u32[]{:S(2)}, u32[]{:S(2)}) collective-permute-start(bf16[2,512,256]{2,1,0:T(8,128)(2,1)S(1)} %get-tuple-element.80._after.edge), channel_id=1, source_target_pairs={{0,2},{1,3},{2,4},{3,5},{4,6},{5,7},{8,10},{9,11},{10,12},{11,13},... | collective-permute-start | bytes 1572872 | tf_op jit(solution)/shard_map/ppermute | solution.py:618
  76.5 8.3 %collective-permute-start.14 = (bf16[1,1024,128]{2,1,0:T(8,128)(2,1)S(1)}, bf16[1,1024,128]{2,1,0:T(8,128)(2,1)S(1)}, u32[]{:S(2)}, u32[]{:S(2)}) collective-permute-start(bf16[1,1024,128]{2,1,0:T(8,128)(2,1)S(1)} %get-tuple-element.87._after), channel_id=1, source_target_pairs={{0,1},{1,0},{2,3},{3,2},{4,5},{5,4},{6,7},{7,6},{8,9},{9,8},{10,11... | collective-permute-start | bytes 786440 | tf_op jit(solution)/shard_map/ppermute | solution.py:520
  77.0 16.3 %collective-permute-start.15 = (bf16[2,512,256]{2,1,0:T(8,128)(2,1)S(1)}, bf16[2,512,256]{2,1,0:T(8,128)(2,1)S(1)}, u32[]{:S(2)}, u32[]{:S(2)}) collective-permute-start(bf16[2,512,256]{2,1,0:T(8,128)(2,1)S(1)} %get-tuple-element.96), channel_id=1, source_target_pairs={{2,0},{3,1},{4,2},{5,3},{6,4},{7,5},{10,8},{11,9},{12,10},{13,11},... | collective-permute-start | bytes 1572872 | tf_op jit(solution)/shard_map/ppermute | solution.py:630
  83.1 18.8 %collective-permute-start.17 = (bf16[2,1024,128]{2,1,0:T(8,128)(2,1)S(1)}, bf16[2,1024,128]{2,1,0:T(8,128)(2,1)S(1)}, u32[]{:S(2)}, u32[]{:S(2)}) collective-permute-start(bf16[2,1024,128]{2,1,0:T(8,128)(2,1)S(1)} %get-tuple-element.92._after._after_edge), channel_id=1, source_target_pairs={{0,1},{1,0},{2,3},{3,2},{4,5},{5,4},{6,7},{7,6},{8,9},{9,8},{10,11... | collective-permute-start | bytes 1572872 | tf_op jit(solution)/shard_map/ppermute | solution.py:520
  87.3 23.1 %collective-permute-start.19 = (bf16[1,512,128]{2,1,0:T(8,128)(2,1)S(1)}, bf16[1,512,128]{2,1,0:T(8,128)(2,1)S(1)}, u32[]{:S(2)}, u32[]{:S(2)}) collective-permute-start(bf16[1,512,128]{2,1,0:T(8,128)(2,1)S(1)} %get-tuple-element.104), channel_id=1, source_target_pairs={{0,6},{1,7},{2,0},{3,1},{4,2},{5,3},{6,4},{7,5},{8,14},{9,15},{10,... | collective-permute-start | bytes 393224 | tf_op jit(solution)/shard_map/ppermute | solution.py:517
  90.0 21.6 %collective-permute-start.20 = (bf16[1,512,128]{2,1,0:T(8,128)(2,1)S(1)}, bf16[1,512,128]{2,1,0:T(8,128)(2,1)S(1)}, u32[]{:S(2)}, u32[]{:S(2)}) collective-permute-start(bf16[1,512,128]{2,1,0:T(8,128)(2,1)S(1)} %get-tuple-element.105), channel_id=1, source_target_pairs={{0,4},{1,5},{2,6},{3,7},{4,0},{5,1},{6,2},{7,3},{8,12},{9,13},{10,... | collective-permute-start | bytes 393224 | tf_op jit(solution)/shard_map/ppermute | solution.py:517
  91.5 20.2 %collective-permute-start.21 = (bf16[1,512,128]{2,1,0:T(8,128)(2,1)S(1)}, bf16[1,512,128]{2,1,0:T(8,128)(2,1)S(1)}, u32[]{:S(2)}, u32[]{:S(2)}) collective-permute-start(bf16[1,512,128]{2,1,0:T(8,128)(2,1)S(1)} %get-tuple-element.106), channel_id=1, source_target_pairs={{0,2},{1,3},{2,4},{3,5},{4,6},{5,7},{6,0},{7,1},{8,10},{9,11},{10,... | collective-permute-start | bytes 393224 | tf_op jit(solution)/shard_map/ppermute | solution.py:517
  100.7 6.8 %collective-permute-start.18 = (f32[8,512]{1,0:T(8,128)S(1)}, f32[8,512]{1,0:T(8,128)S(1)}, u32[]{:S(2)}, u32[]{:S(2)}) collective-permute-start(f32[8,512]{1,0:T(8,128)S(1)} %get-tuple-element.97._after._after_edge), channel_id=1, source_target_pairs={{2,0},{3,1},{4,2},{5,3},{6,4},{7,5},{10,8},{11,9},{12,10},{13,11},... | collective-permute-start | bytes 49160 | tf_op jit(solution)/shard_map/ppermute | solution.py:693
  104.4 9.9 %collective-permute-start.22 = (bf16[2,512,128]{2,1,0:T(8,128)(2,1)S(1)}, bf16[2,512,128]{2,1,0:T(8,128)(2,1)S(1)}, u32[]{:S(2)}, u32[]{:S(2)}) collective-permute-start(bf16[2,512,128]{2,1,0:T(8,128)(2,1)S(1)} %get-tuple-element.107), channel_id=1, source_target_pairs={{0,6},{1,7},{2,0},{3,1},{4,2},{5,3},{6,4},{7,5},{8,14},{9,15},{10,... | collective-permute-start | bytes 786440 | tf_op jit(solution)/shard_map/ppermute | solution.py:517
  107.5 19.3 %collective-permute-start.23 = (bf16[2,512,128]{2,1,0:T(8,128)(2,1)S(1)}, bf16[2,512,128]{2,1,0:T(8,128)(2,1)S(1)}, u32[]{:S(2)}, u32[]{:S(2)}) collective-permute-start(bf16[2,512,128]{2,1,0:T(8,128)(2,1)S(1)} %get-tuple-element.108), channel_id=1, source_target_pairs={{0,4},{1,5},{2,6},{3,7},{4,0},{5,1},{6,2},{7,3},{8,12},{9,13},{10,... | collective-permute-start | bytes 786440 | tf_op jit(solution)/shard_map/ppermute | solution.py:517
  110.4 16.3 %collective-permute-start.25 = (bf16[3,512,256]{2,1,0:T(8,128)(2,1)S(1)}, bf16[3,512,256]{2,1,0:T(8,128)(2,1)S(1)}, u32[]{:S(2)}, u32[]{:S(2)}) collective-permute-start(bf16[3,512,256]{2,1,0:T(8,128)(2,1)S(1)} %get-tuple-element.103._after), channel_id=1, source_target_pairs={{0,1},{1,0},{2,3},{3,2},{4,5},{5,4},{6,7},{7,6},{8,9},{9,8},{10,11... | collective-permute-start | bytes 2359304 | tf_op jit(solution)/shard_map/ppermute | solution.py:520
  113.4 13.4 %collective-permute-start.24 = (bf16[2,512,128]{2,1,0:T(8,128)(2,1)S(1)}, bf16[2,512,128]{2,1,0:T(8,128)(2,1)S(1)}, u32[]{:S(2)}, u32[]{:S(2)}) collective-permute-start(bf16[2,512,128]{2,1,0:T(8,128)(2,1)S(1)} %unsort_last.1), channel_id=1, source_target_pairs={{0,2},{1,3},{2,4},{3,5},{4,6},{5,7},{6,0},{7,1},{8,10},{9,11},{10,... | collective-permute-start | bytes 786440 | tf_op jit(solution)/shard_map/ppermute | solution.py:517

commit v4 on v3

--- a/solution.py
+++ b/solution.py
@@ -89,12 +89,12 @@
             out[i] = held[i, :, pl.ds(pl.multiple_of(HR * HD + side * width, width), width)]
 
 
-def split_value_kernel(place, _after1, _after2, _after3, v_ref, x0, x1, x2, x3):
+def split_value_kernel(place, _after, _after1, _after2, _after3, v_ref, x0, x1, x2, x3):
     for d, x in enumerate((x0, x1, x2, x3)):
         x[...] = v_ref[:, head_columns(place, d)]
 
 
-def project_kernel(place, _after, _after_local, rows_ref, weight, g0, g1, g2, g3, own_ref, send_ref):
+def project_kernel(place, _after_local, rows_ref, weight, g0, g1, g2, g3, own_ref, send_ref):
     step = pl.program_id(0)
     part = dot_nt(rows_ref[...], weight[...]).astype(BF16)
 
@@ -172,12 +172,8 @@
     send_ref[2 * half :, :] = info.astype(BF16)
 
 
-def pack_value_kernel(unit, kept_ref, _after, slot_row, x0, x1, x2, x3, local_ref, sorted_ref, send_ref):
+def pack_value_kernel(unit, kept_ref, _after, _after_swap, slot_row, x0, x1, x2, x3, sorted_ref, send_ref):
     pack_one(unit, kept_ref, slot_row, (x0, x1, x2, x3), sorted_ref, send_ref)
-    tok = local_ref.shape[0]
-    for h in range(HL // 2):
-        at = CS // 2 + h * tok
-        send_ref[at : at + tok, :] = local_ref[:, h * HD : (h + 1) * HD]
 
 
 def pack_grad_kernel(
@@ -278,7 +274,7 @@
 
 
 def mix_kernel(
-    unit, place, kept_ref, got_ref, _after, sorted_ref, came_ref, p_ref, own, got, g_own, v_ref, ot_ref, edge_ref, vt
+    unit, place, kept_ref, got_ref, _after, sorted_ref, came_ref, p_ref, own, got, g_own, g_got, v_ref, ot_ref, edge_ref, vt
 ):
     tok = own.shape[1]
 
@@ -290,9 +286,7 @@
     @pl.when(place[1] == 1)
     def _():
         edge_ref[0] = got[0]
-        for h in range(HL // 2):
-            at = CS // 2 + h * tok
-            edge_ref[1, :, h * HD : (h + 1) * HD] = came_ref[at : at + tok, :]
+        edge_ref[1] = g_got[...]
 
     def kept(d, u, to):
         v_ref[rows(to * unit, unit), :] = sorted_ref[d, rows(u * unit, unit), :]
@@ -385,7 +379,7 @@
 
 
 def window_kernel(
-    place, _after, _after_edge, own, got, g_own, g_came, edge, dq_ref, early_ref, late_ref, stats_ref, *scratch
+    place, _after, _after_edge, own, got, g_own, g_got, edge, dq_ref, early_ref, late_ref, stats_ref, *scratch
 ):
     tok = own.shape[1]
     pair = 2 * tok
@@ -398,8 +392,7 @@
     for h in range(HL // 2):
         part = slice(h * HD, (h + 1) * HD)
         queries, grads, keys, values, kt, dk, dv = (ref.at[h] for ref in scratch)
-        g_got = g_came[CS // 2 + h * tok : CS // 2 + (h + 1) * tok, :]
-        for at, block, g_block in ((own_at, own, g_own[:, part]), (got_at, got, g_got)):
+        for at, block, g_block in ((own_at, own, g_own[:, part]), (got_at, got, g_got[:, part])):
             queries[rows(at, tok), :] = block[0, :, part]
             grads[rows(at, tok), :] = g_block
             keys[rows(at + WIN, tok), :] = block[1, :, part]
@@ -484,19 +477,24 @@
         out[:, head_columns(place, d)] = v[0]
 
 
-def join_kernel(place, value_ref, y0, y1, y2, y3, own, got, dq_ref, dk_ref, dv_ref):
+def join_kernel(place, value_ref, own, got, dq_ref, dk_ref, dv_ref):
     outs = (dq_ref, dk_ref, dv_ref)
     dv_ref[:, : HR * HD] = value_ref[...]
-    for d, y in enumerate((y0, y1, y2, y3)):
-        at = head_columns(place, d)
-        for i in range(2):
-            outs[i][:, at] = y[i]
     width = HL * HD // 2
     for n in range(2):
         side = place[1] if n == 0 else 1 - place[1]
         at = pl.ds(pl.multiple_of(HR * HD + side * width, width), width)
         for i in range(3):
             outs[i][:, at] = own[i] if n == 0 else got[i]
+
+
+def finish_kernel(place, y0, y1, y2, y3, _dq, _dk, dq_hbm, dk_hbm, sems):
+    copies = []
+    for d, y in enumerate((y0, y1, y2, y3)):
+        for i, out in enumerate((dq_hbm, dk_hbm)):
+            copies.append(pltpu.make_async_copy(y.at[i], out.at[:, head_columns(place, d)], sems.at[d, i]))
+    start_all(copies)
+    wait_all(copies)
 
 
 def struct(*shape, dtype=BF16):
@@ -534,15 +532,34 @@
     )(where, assign[0], query[0], key[0], value[0])
     arrived = [sent[0]] + [among_groups(sent[d], d) for d in range(1, HR)]
     local_got = swap(local_send)
+    *g_sent, g_own, g_send = pl.pallas_call(
+        project_kernel,
+        grid=(4,),
+        out_shape=[struct(tok, HD)] * HR + [struct(tok, width)] * 2,
+        in_specs=smem()
+        + [
+            pl.BlockSpec((1, 16, HD), lambda n: (0, 0, 0)),
+            pl.BlockSpec(boundary.shape, lambda n: (0, 0)),
+            pl.BlockSpec((2 * HD, boundary.shape[1]), lambda n: (n, 0)),
+        ],
+        out_specs=[pl.BlockSpec((tok, HD), lambda n: (0, 0))] * HR
+        + [pl.BlockSpec((tok, width), lambda n: (0, 0))] * 2,
+        compiler_params=params(20),
+        cost_estimate=takes(3.8),
+        name="project",
+    )(where, local_got, boundary, out_weight[0])
+    g_arrived = [g_sent[0]] + [among_groups(g_sent[d], d) for d in range(1, HR)]
+
+    g_got = swap(g_send)
     v_sent = pl.pallas_call(
         split_value_kernel,
         out_shape=[struct(tok, HD)] * HR,
-        in_specs=smem() + vmem(4),
+        in_specs=smem() + vmem(5),
         out_specs=vmem(4),
         compiler_params=params(20),
         cost_estimate=takes(1),
         name="split_value",
-    )(where, *arrived[1:], value[0])
+    )(where, g_sent[0], *arrived[1:], value[0])
     v_arrived = [v_sent[0]] + [among_groups(v_sent[d], d) for d in range(1, HR)]
 
     ordered, send, slot_row, slot_col, kept = pl.pallas_call(
@@ -557,39 +574,20 @@
         in_specs=smem() + vmem(5),
         out_specs=vmem(4) + smem(),
         compiler_params=params(20),
-        cost_estimate=takes(2.6),
+        cost_estimate=takes(0.1),
         name="pack",
     )(where, v_sent[0], *arrived)
     came = swap(send)
 
-    *g_sent, g_own, g_send = pl.pallas_call(
-        project_kernel,
-        grid=(4,),
-        out_shape=[struct(tok, HD)] * HR + [struct(tok, width)] * 2,
-        in_specs=smem()
-        + [
-            pl.BlockSpec((16, HD), lambda n: (0, 0)),
-            pl.BlockSpec((1, 16, HD), lambda n: (0, 0, 0)),
-            pl.BlockSpec(boundary.shape, lambda n: (0, 0)),
-            pl.BlockSpec((2 * HD, boundary.shape[1]), lambda n: (n, 0)),
-        ],
-        out_specs=[pl.BlockSpec((tok, HD), lambda n: (0, 0))] * HR
-        + [pl.BlockSpec((tok, width), lambda n: (0, 0))] * 2,
-        compiler_params=params(20),
-        cost_estimate=takes(3.8),
-        name="project",
-    )(where, send, local_got, boundary, out_weight[0])
-    g_arrived = [g_sent[0]] + [among_groups(g_sent[d], d) for d in range(1, HR)]
-
     v_ordered, v_out = pl.pallas_call(
         functools.partial(pack_value_kernel, unit),
-        out_shape=[struct(HR, tok, HD), struct(half + HL // 2 * tok, HD)],
+        out_shape=[struct(HR, tok, HD), struct(half, HD)],
         in_specs=smem() + vmem(7),
         out_specs=vmem(2),
         compiler_params=params(20),
-        cost_estimate=takes(1.6),
+        cost_estimate=takes(12),
         name="pack_value",
-    )(kept, g_sent[0], slot_row, *v_arrived, g_send)
+    )(kept, send, g_got, slot_row, *v_arrived)
     v_came = swap(v_out)
 
     got, q, k, kt, p = pl.pallas_call(
@@ -620,13 +618,13 @@
     v, ot, query_edge = pl.pallas_call(
         functools.partial(mix_kernel, unit),
         out_shape=[struct(CS, HD), struct(HD, CS, dtype=F32), struct(2, tok, width)],
-        in_specs=smem(3) + vmem(7),
+        in_specs=smem(3) + vmem(8),
         out_specs=vmem(3),
         scratch_shapes=[pltpu.VMEM((HD, CS), BF16)],
         compiler_params=params(20),
         cost_estimate=takes(1.7),
         name="mix",
-    )(where, kept, got, edge, v_ordered, v_came, p, local_own, local_got, g_own)
+    )(where, kept, got, edge, v_ordered, v_came, p, local_own, local_got, g_own, g_got)
     query_edge_got = lax.ppermute(query_edge, "seq", behind)
 
     g, own_v, back_v = pl.pallas_call(
@@ -689,9 +687,9 @@
         compiler_params=params(24),
         cost_estimate=takes(0.1),
         name="window",
-    )(where, natural_v[0], query_edge_got, local_own, local_got, g_own, v_came, edge_got)
+    )(where, natural_v[0], query_edge_got, local_own, local_got, g_own, g_got, edge_got)
     stats_got = lax.ppermute(stats, "seq", behind)
-    first_natural = unsort((0, 1, 2), stats, stats, own, returned, "unsort_first")
+    first_natural = unsort((0, 1, 3), stats, stats, own, returned, "unsort_first")
     settled_own, settled_send = pl.pallas_call(
         settle_kernel,
         out_shape=[struct(3, tok, width)] * 2,
@@ -712,19 +710,32 @@
         cost_estimate=takes(12),
         name="join_value",
     )(where, settled_send, *home_v)
-    last_natural = unsort((3,), value_left, value_left, own, returned, "unsort_last")
-    natural = [*first_natural, *last_natural]
+    last_natural = unsort((2,), value_left, value_left, own, returned, "unsort_last")
+    natural = [*first_natural]
+    natural.insert(2, *last_natural)
     home = [natural[0]] + [among_groups(natural[d], -d) for d in range(1, HR)]
 
-    outs = pl.pallas_call(
+    dq_part, dk_part, dv = pl.pallas_call(
         join_kernel,
         out_shape=[struct(tok, (HR + HL) * HD)] * 3,
-        in_specs=smem() + vmem(7),
+        in_specs=smem() + vmem(3),
         out_specs=vmem(3),
         compiler_params=params(20),
-        cost_estimate=takes(2.8),
+        cost_estimate=takes(2),
         name="join",
-    )(where, value_left, *home, settled_own, settled_got)
+    )(where, value_left, settled_own, settled_got)
+    dq, dk = pl.pallas_call(
+        finish_kernel,
+        out_shape=[struct(tok, (HR + HL) * HD)] * 2,
+        in_specs=smem() + vmem(4) + hbm * 2,
+        out_specs=hbm * 2,
+        input_output_aliases={5: 0, 6: 1},
+        scratch_shapes=[pltpu.SemaphoreType.DMA((HR, 2))],
+        compiler_params=params(16),
+        cost_estimate=takes(1.5),
+        name="finish",
+    )(where, *home, dq_part, dk_part)
+    outs = (dq, dk, dv)
     return tuple(out[None] for out in outs)
 
 

time: 130 us -> 127 us (0.977)
  waiting for transfers between devices: 39.9 us -> 32.2 us
  starting transfers between devices: 40.4 us -> 43.7 us
  Pallas kernels: 46.7 us -> 48.5 us
    ppermute x15, waiting for transfers between devices: 29 us -> 6.41 us  [among_groups(): return lax.ppermute(block, 'seq', route)]
    ppermute x7 -> x8, waiting for transfers between devices: 9.05 us -> 23.9 us  [swap(): return lax.ppermute(block, 'seq', [(i, i ^ 1) for i in range(devices)])]
    ppermute x15, starting transfers between devices: 26.2 us -> 28.6 us  [among_groups(): return lax.ppermute(block, 'seq', route)]
    ppermute x1, waiting for transfers between devices: 0.01 us -> 1.92 us  [pair_body(): stats_got = lax.ppermute(stats, 'seq', behind)]
    ppermute x1, waiting for transfers between devices: 1.86 us -> 0.01 us  [pair_body(): query_edge_got = lax.ppermute(query_edge, 'seq', behind)]
    pallas_call x0 -> x1, Pallas kernels: none -> 1.57 us  [pair_body(): pl.pallas_call(finish_kernel, out_shape=[struct(tok, (HR + HL) * HD)] * 2...]
    ppermute x1, starting transfers between devices: 1.35 us -> 2.81 us  [pair_body(): edge_got = lax.ppermute(edge, 'seq', ahead)]
    ppermute x7 -> x8, starting transfers between devices: 7.66 us -> 7.32 us  [swap(): return lax.ppermute(block, 'seq', [(i, i ^ 1) for i in range(devices)])]
  transfers between devices with their start and end apart: 26 -> 27, of which waited for: 8 -> 7; matrix products, arithmetic and copies ran while one was open for 1% -> 1% of each run, Pallas kernels for 34% -> 37%
where the time goes in v4:
time: 127 us; the launch traced here: 126 us
  Pallas kernels  48.5 us (38%)
  starting transfers between devices  43.7 us (34%)
  waiting for transfers between devices  32.2 us (25%)
    ppermute x15, starting transfers between devices, among_groups(): return lax.ppermute(block, 'seq', route)  28.6 us
    ppermute x8, waiting for transfers between devices, swap(): return lax.ppermute(block, 'seq', [(i, i ^ 1) for i in range(devices)])  23.9 us
    pallas_call x1, Pallas kernels, pair_body(): pl.pallas_call(window_kernel, out_shape=[struct(2, tok, width), struct(2,...  7.37 us
    ppermute x8, starting transfers between devices, swap(): return lax.ppermute(block, 'seq', [(i, i ^ 1) for i in range(devices)])  7.32 us
    ppermute x15, waiting for transfers between devices, among_groups(): return lax.ppermute(block, 'seq', route)  6.41 us
    pallas_call x3, Pallas kernels, unsort(): pl.pallas_call(functools.partial(unsort_kernel, unit, distances), out_sha...  6.05 us
    pallas_call x1, Pallas kernels, pair_body(): pl.pallas_call(functools.partial(probs_kernel, unit), out_shape=[struct(H...  5.08 us
    pallas_call x1, Pallas kernels, pair_body(): pl.pallas_call(functools.partial(grads_kernel, unit), out_shape=[struct(H...  4.63 us
  transfers between devices with their start and end apart: 27, of which 7 were waited for; matrix products, arithmetic and copies ran while one was open for 1% of the time, Pallas kernels for 37%

profile of v4, /device:TPU:0, one launch (start us, length us, event | category | flops | bytes accessed | tf_op | source)
XLA Modules:
  0.0 126.2 jit_solution(8557792482596861002)
XLA Ops:
  0.6 2.4 %collective-permute-start.1 = (bf16[1,512,2048]{2,1,0:T(8,128)(2,1)}, bf16[1,512,2048]{2,1,0:T(8,128)(2,1)S(1)}, u32[]{:S(2)}, u32[]{:S(2)}) collective-permute-start(bf16[1,512,2048]{2,1,0:T(8,128)(2,1)} %param.9), channel_id=1, source_target_pairs={{8,0},{16,8},{24,16},{0,24},{9,1},{17,9},{25,17},{1,25},{10,2},{18... | collective-permute-start | bytes 6291464 | tf_op jit(solution)/shard_map/ppermute | solution.py:745
  3.7 4.4 %split.1 = (bf16[1040,128]{1,0:T(8,128)(2,1)}, bf16[1040,128]{1,0:T(8,128)(2,1)}, bf16[1040,128]{1,0:T(8,128)(2,1)}, bf16[1040,128]{1,0:T(8,128)(2,1)}, bf16[3,5...) custom-call(s32[2]{0:T(128)} %pad_add_fusion.place, s32[4,512]{1,0:T(4,128)} %bitcast.17, bf16[512,1024]{1,0:T(8,128)(2,1)} %bitcast.15, ...), custom_call_target="tpu_custom_call" | custom-call | flops 2200000000 | bytes 7000000 | tf_op jit(solution)/shard_map/split/pallas_call | solution.py:523
  8.2 1.6 %collective-permute-start = (bf16[3,512,256]{2,1,0:T(8,128)(2,1)}, bf16[3,512,256]{2,1,0:T(8,128)(2,1)S(1)}, u32[]{:S(2)}, u32[]{:S(2)}) collective-permute-start(bf16[3,512,256]{2,1,0:T(8,128)(2,1)} %get-tuple-element.60), channel_id=1, source_target_pairs={{0,1},{1,0},{2,3},{3,2},{4,5},{5,4},{6,7},{7,6},{8,9},{9,8},{10,11... | collective-permute-start | bytes 2359304 | tf_op jit(solution)/shard_map/ppermute | solution.py:518
  9.7 1.6 %collective-permute-start.2 = (bf16[1040,128]{1,0:T(8,128)(2,1)}, bf16[1040,128]{1,0:T(8,128)(2,1)S(1)}, u32[]{:S(2)}, u32[]{:S(2)}) collective-permute-start(bf16[1040,128]{1,0:T(8,128)(2,1)} %get-tuple-element.62), channel_id=1, source_target_pairs={{0,2},{1,3},{2,4},{3,5},{4,6},{5,7},{6,0},{7,1},{8,10},{9,11},{10,... | collective-permute-start | bytes 798728 | tf_op jit(solution)/shard_map/ppermute | solution.py:515
  11.3 2.6 %collective-permute-start.3 = (bf16[1040,128]{1,0:T(8,128)(2,1)}, bf16[1040,128]{1,0:T(8,128)(2,1)S(1)}, u32[]{:S(2)}, u32[]{:S(2)}) collective-permute-start(bf16[1040,128]{1,0:T(8,128)(2,1)} %get-tuple-element.63), channel_id=1, source_target_pairs={{0,4},{1,5},{2,6},{3,7},{4,0},{5,1},{6,2},{7,3},{8,12},{9,13},{10,... | collective-permute-start | bytes 798728 | tf_op jit(solution)/shard_map/ppermute | solution.py:515
  15.3 12.0 %collective-permute-done._after_local.got = bf16[3,512,256]{2,1,0:T(8,128)(2,1)S(1)} collective-permute-done((bf16[3,512,256]{2,1,0:T(8,128)(2,1)}, bf16[3,512,256]{2,1,0:T(8,128)(2,1)S(1)}, u32[]{:S(2)}, u32[]{:S(2)}) %collective-permute-start) | collective-permute-done | bytes 786464 | tf_op jit(solution)/shard_map/ppermute | solution.py:518
  27.3 3.8 %project.1 = (bf16[512,128]{1,0:T(8,128)(2,1)S(1)}, bf16[512,128]{1,0:T(8,128)(2,1)S(1)}, bf16[512,128]{1,0:T(8,128)(2,1)S(1)}, bf16[512,128]{1,0:T(8,128)(2,1)S...) custom-call(s32[2]{0:T(128)S(1)} %copy-done.2, ...), custom_call_target="tpu_custom_call" | custom-call | flops 4180000000 | bytes 13300000 | tf_op jit(solution)/shard_map/project/pallas_call | solution.py:535
  31.1 1.8 %collective-permute-start.5 = (bf16[512,256]{1,0:T(8,128)(2,1)S(1)}, bf16[512,256]{1,0:T(8,128)(2,1)S(1)}, u32[]{:S(2)}, u32[]{:S(2)}) collective-permute-start(bf16[512,256]{1,0:T(8,128)(2,1)S(1)} %get-tuple-element.69), channel_id=1, source_target_pairs={{0,1},{1,0},{2,3},{3,2},{4,5},{5,4},{6,7},{7,6},{8,9},{9,8},{10,11... | collective-permute-start | bytes 786440 | tf_op jit(solution)/shard_map/ppermute | solution.py:518
  33.6 4.3 %collective-permute-start.6 = (bf16[512,128]{1,0:T(8,128)(2,1)S(1)}, bf16[512,128]{1,0:T(8,128)(2,1)S(1)}, u32[]{:S(2)}, u32[]{:S(2)}) collective-permute-start(bf16[512,128]{1,0:T(8,128)(2,1)S(1)} %get-tuple-element.71), channel_id=1, source_target_pairs={{0,2},{1,3},{2,4},{3,5},{4,6},{5,7},{6,0},{7,1},{8,10},{9,11},{10,... | collective-permute-start | bytes 393224 | tf_op jit(solution)/shard_map/ppermute | solution.py:515
  37.9 1.6 %collective-permute-start.7 = (bf16[512,128]{1,0:T(8,128)(2,1)S(1)}, bf16[512,128]{1,0:T(8,128)(2,1)S(1)}, u32[]{:S(2)}, u32[]{:S(2)}) collective-permute-start(bf16[512,128]{1,0:T(8,128)(2,1)S(1)} %get-tuple-element.72), channel_id=1, source_target_pairs={{0,4},{1,5},{2,6},{3,7},{4,0},{5,1},{6,2},{7,3},{8,12},{9,13},{10,... | collective-permute-start | bytes 393224 | tf_op jit(solution)/shard_map/ppermute | solution.py:515
  40.3 2.7 %pack.1 = (bf16[4,2,512,128]{3,2,1,0:T(8,128)(2,1)S(1)}, bf16[2064,128]{1,0:T(8,128)(2,1)S(1)}, f32[8,512]{1,0:T(8,128)S(1)}, f32[512,128]{1,0:T(8,128)S(1)}, s32[4]{0:T(128)S(1)}) custom-call(s32[2]{0:T(128)S(1)} %copy-done.2, bf16[512,128]{1,0:T(8,128)(2,1)S(1)} %get-tuple-element.65._after.x0, bf16[1040,128]{1,0:T(8,128)(2,1)S(1)} %copy-done.1, ...), custom_call_target="tpu_custom_call" | custom-call | flops 110000000 | bytes 350000 | tf_op jit(solution)/shard_map/pack/pallas_call | solution.py:565
  44.7 3.2 %collective-permute-done.7.x2 = bf16[512,128]{1,0:T(8,128)(2,1)S(1)} collective-permute-done((bf16[512,128]{1,0:T(8,128)(2,1)S(1)}, bf16[512,128]{1,0:T(8,128)(2,1)S(1)}, u32[]{:S(2)}, u32[]{:S(2)}) %collective-permute-start.7) | collective-permute-done | bytes 131104 | tf_op jit(solution)/shard_map/ppermute | solution.py:515
  48.1 5.4 %collective-permute-start.12 = (bf16[512,128]{1,0:T(8,128)(2,1)S(1)}, bf16[512,128]{1,0:T(8,128)(2,1)S(1)}, u32[]{:S(2)}, u32[]{:S(2)}) collective-permute-start(bf16[512,128]{1,0:T(8,128)(2,1)S(1)} %get-tuple-element.80), channel_id=1, source_target_pairs={{0,6},{1,7},{2,0},{3,1},{4,2},{5,3},{6,4},{7,5},{8,14},{9,15},{10,... | collective-permute-start | bytes 393224 | tf_op jit(solution)/shard_map/ppermute | solution.py:515
  55.3 1.8 %collective-permute-done.9.came_ref = bf16[2064,128]{1,0:T(8,128)(2,1)S(1)} collective-permute-done((bf16[2064,128]{1,0:T(8,128)(2,1)S(1)}, bf16[2064,128]{1,0:T(8,128)(2,1)S(1)}, u32[]{:S(2)}, u32[]{:S(2)}) %collective-permute-start.9) | collective-permute-done | bytes 528416 | tf_op jit(solution)/shard_map/ppermute | solution.py:518
  57.2 5.1 %probs.1 = (s32[4]{0:T(128)S(1)}, bf16[2048,128]{1,0:T(8,128)(2,1)S(1)}, bf16[2048,128]{1,0:T(8,128)(2,1)S(1)}, bf16[128,2048]{1,0:T(8,128)(2,1)S(1)}, bf16[2048,2048]{1,0:T(8,128)(2,1)S(1)}) custom-call(s32[2]{0:T(128)S(1)} %copy-done.2, s32[4]{0:T(128)S(1)} %get-tuple-element.67.kept_ref, bf16[1024,128]{1,0:T(8,128)(2,1)S(1)} %get-tuple-element.74._after, ...), custom_call_target="tpu_custom_call" | custom-call | flops 5500000256 | bytes 17500000 | tf_op jit(solution)/shard_map/probs/pallas_call | solution.py:593
  64.3 2.8 %collective-permute-start.17 = (bf16[2,512,256]{2,1,0:T(8,128)(2,1)S(1)}, bf16[2,512,256]{2,1,0:T(8,128)(2,1)S(1)}, u32[]{:S(2)}, u32[]{:S(2)}) collective-permute-start(bf16[2,512,256]{2,1,0:T(8,128)(2,1)S(1)} %get-tuple-element.82._after.edge), channel_id=1, source_target_pairs={{0,2},{1,3},{2,4},{3,5},{4,6},{5,7},{8,10},{9,11},{10,12},{11,13},... | collective-permute-start | bytes 1572872 | tf_op jit(solution)/shard_map/ppermute | solution.py:616
  67.1 1.7 %mix.1 = (bf16[2048,128]{1,0:T(8,128)(2,1)S(1)}, f32[128,2048]{1,0:T(8,128)S(1)}, bf16[2,512,256]{2,1,0:T(8,128)(2,1)S(1)}) custom-call(s32[2]{0:T(128)S(1)} %copy-done.2, s32[4]{0:T(128)S(1)} %get-tuple-element.67.kept_ref, s32[4]{0:T(128)S(1)} %get-tuple-element.76.got_ref, bf16[2,512,256]{2,1,0:T(8,128)(2,1)S(1)} %get-tuple-element.82._after.edge, ...), custom_call_target="tpu_custom_call" | custom-call | flops 1870000000 | bytes 5950000 | tf_op jit(solution)/shard_map/mix/pallas_call | solution.py:618
  70.2 2.7 %value_grads.1 = (bf16[2048,128]{1,0:T(8,128)(2,1)S(1)}, bf16[4,1,512,128]{3,2,1,0:T(8,128)(2,1)S(1)}, bf16[1,1024,128]{2,1,0:T(8,128)(2,1)S(1)}) custom-call(s32[2]{0:T(128)S(1)} %copy-done.2, s32[4]{0:T(128)S(1)} %get-tuple-element.67.kept_ref, s32[4]{0:T(128)S(1)} %get-tuple-element.76.got_ref, f32[128,2048]{1,0:T(8,128)S(1)} %get-tuple-element.86._after.ot_ref, ...), custom_call_target="tpu_custom_call" | custom-call | flops 2640000000 | bytes 8400000 | tf_op jit(solution)/shard_map/value_grads/pallas_call | solution.py:630
  73.4 4.6 %grads.1 = (bf16[4,2,512,128]{3,2,1,0:T(8,128)(2,1)S(1)}, bf16[2,1024,128]{2,1,0:T(8,128)(2,1)S(1)}) custom-call(s32[2]{0:T(128)S(1)} %copy-done.2, s32[4]{0:T(128)S(1)} %get-tuple-element.67.kept_ref, s32[4]{0:T(128)S(1)} %get-tuple-element.76.got_ref, bf16[1,1024,128]{2,1,0:T(8,128)(2,1)S(1)} %get-tuple-element.89._after, ...), custom_call_target="tpu_custom_call" | custom-call | flops 5500000256 | bytes 17500000 | tf_op jit(solution)/shard_map/grads/pallas_call | solution.py:640
  78.1 1.6 %collective-permute-start.18 = (bf16[2,1024,128]{2,1,0:T(8,128)(2,1)S(1)}, bf16[2,1024,128]{2,1,0:T(8,128)(2,1)S(1)}, u32[]{:S(2)}, u32[]{:S(2)}) collective-permute-start(bf16[2,1024,128]{2,1,0:T(8,128)(2,1)S(1)} %get-tuple-element.94._after._after_edge), channel_id=1, source_target_pairs={{0,1},{1,0},{2,3},{3,2},{4,5},{5,4},{6,7},{7,6},{8,9},{9,8},{10,11... | collective-permute-start | bytes 1572872 | tf_op jit(solution)/shard_map/ppermute | solution.py:518
  80.6 2.6 %unsort_value.1 = (bf16[1,512,128]{2,1,0:T(8,128)(2,1)S(1)}, bf16[1,512,128]{2,1,0:T(8,128)(2,1)S(1)}, bf16[1,512,128]{2,1,0:T(8,128)(2,1)S(1)}, bf16[1,512,128]{2,1,0:T(8,128)(2,1)S(1)}) custom-call(s32[4]{0:T(128)S(1)} %get-tuple-element.67.kept_ref, bf16[2,1024,128]{2,1,0:T(8,128)(2,1)S(1)} %get-tuple-element.94._after._after_edge, ...), custom_call_target="tpu_custom_call" | custom-call | flops 2860000000 | bytes 9100000 | tf_op jit(solution)/shard_map/unsort_value/pallas_call | solution.py:653
  83.2 3.2 %collective-permute-start.21 = (bf16[1,512,128]{2,1,0:T(8,128)(2,1)S(1)}, bf16[1,512,128]{2,1,0:T(8,128)(2,1)S(1)}, u32[]{:S(2)}, u32[]{:S(2)}) collective-permute-start(bf16[1,512,128]{2,1,0:T(8,128)(2,1)S(1)} %get-tuple-element.107), channel_id=1, source_target_pairs={{0,6},{1,7},{2,0},{3,1},{4,2},{5,3},{6,4},{7,5},{8,14},{9,15},{10,... | collective-permute-start | bytes 393224 | tf_op jit(solution)/shard_map/ppermute | solution.py:515
  87.1 1.9 %collective-permute-start.23 = (bf16[1,512,128]{2,1,0:T(8,128)(2,1)S(1)}, bf16[1,512,128]{2,1,0:T(8,128)(2,1)S(1)}, u32[]{:S(2)}, u32[]{:S(2)}) collective-permute-start(bf16[1,512,128]{2,1,0:T(8,128)(2,1)S(1)} %get-tuple-element.109), channel_id=1, source_target_pairs={{0,2},{1,3},{2,4},{3,5},{4,6},{5,7},{6,0},{7,1},{8,10},{9,11},{10,... | collective-permute-start | bytes 393224 | tf_op jit(solution)/shard_map/ppermute | solution.py:515
  89.0 7.4 %window.1 = (bf16[2,512,256]{2,1,0:T(8,128)(2,1)S(1)}, bf16[2,512,256]{2,1,0:T(8,128)(2,1)S(1)}, f32[2,512,256]{2,1,0:T(8,128)S(1)}, f32[8,512]{1,0:T(8,128)S(1)}) custom-call(s32[2]{0:T(128)S(1)} %copy-done.2, bf16[1,512,128]{2,1,0:T(8,128)(2,1)S(1)} %get-tuple-element.97._after.v0, bf16[2,512,256]{2,1,0:T(8,128)(2,1)S(1)} %collective-permute-done.16._after_edge.ahead, ...), custom_call_target="tpu_custom_call" | custom-call | flops 110000000 | bytes 350000 | tf_op jit(solution)/shard_map/window/pallas_call | solution.py:668
  97.7 2.4 %unsort_first.1 = (bf16[2,512,128]{2,1,0:T(8,128)(2,1)S(1)}, bf16[2,512,128]{2,1,0:T(8,128)(2,1)S(1)}, bf16[2,512,128]{2,1,0:T(8,128)(2,1)S(1)}) custom-call(s32[4]{0:T(128)S(1)} %get-tuple-element.67.kept_ref, f32[8,512]{1,0:T(8,128)S(1)} %get-tuple-element.99._after._after_edge, f32[8,512]{1,0:T(8,128)S(1)} %get-tuple-element.99._after._after_edge, ...), custom_call_target="tpu_custom_call" | custom-call | flops 110000000 | bytes 350000 | tf_op jit(solution)/shard_map/unsort_first/pallas_call | solution.py:653
  100.1 1.9 %collective-permute-done.20.stats = f32[8,512]{1,0:T(8,128)S(1)} collective-permute-done((f32[8,512]{1,0:T(8,128)S(1)}, f32[8,512]{1,0:T(8,128)S(1)}, u32[]{:S(2)}, u32[]{:S(2)}) %collective-permute-start.20) | collective-permute-done | bytes 16416 | tf_op jit(solution)/shard_map/ppermute | solution.py:691
  102.1 1.9 %settle.1 = (bf16[3,512,256]{2,1,0:T(8,128)(2,1)S(1)}, bf16[3,512,256]{2,1,0:T(8,128)(2,1)S(1)}) custom-call(s32[2]{0:T(128)S(1)} %copy-done.2, bf16[2,512,128]{2,1,0:T(8,128)(2,1)S(1)} %get-tuple-element.101._after.y0, bf16[2,512,256]{2,1,0:T(8,128)(2,1)S(1)} %get-tuple-element.103.dq_ref, bf16[2,512,256]{2,1,0:T(8,128)(2,1)S(1)} %get-tuple-element.104.early_ref, ...), custom_call_target="tpu_custom_call" | custom-call | flops 110000000 | bytes 350000 | tf_op jit(solution)/shard_map/settle/pallas_call | solution.py:693
  105.8 1.7 %collective-permute-start.24 = (bf16[2,512,128]{2,1,0:T(8,128)(2,1)S(1)}, bf16[2,512,128]{2,1,0:T(8,128)(2,1)S(1)}, u32[]{:S(2)}, u32[]{:S(2)}) collective-permute-start(bf16[2,512,128]{2,1,0:T(8,128)(2,1)S(1)} %unsort_last.1), channel_id=1, source_target_pairs={{0,4},{1,5},{2,6},{3,7},{4,0},{5,1},{6,2},{7,3},{8,12},{9,13},{10,... | collective-permute-start | bytes 786440 | tf_op jit(solution)/shard_map/ppermute | solution.py:515
  107.5 2.2 %collective-permute-start.19 = (bf16[2,512,128]{2,1,0:T(8,128)(2,1)S(1)}, bf16[2,512,128]{2,1,0:T(8,128)(2,1)S(1)}, u32[]{:S(2)}, u32[]{:S(2)}) collective-permute-start(bf16[2,512,128]{2,1,0:T(8,128)(2,1)S(1)} %get-tuple-element.102), channel_id=1, source_target_pairs={{0,6},{1,7},{2,0},{3,1},{4,2},{5,3},{6,4},{7,5},{8,14},{9,15},{10,... | collective-permute-start | bytes 786440 | tf_op jit(solution)/shard_map/ppermute | solution.py:515
  109.7 9.1 %collective-permute-done.26.got = bf16[3,512,256]{2,1,0:T(8,128)(2,1)S(1)} collective-permute-done((bf16[3,512,256]{2,1,0:T(8,128)(2,1)S(1)}, bf16[3,512,256]{2,1,0:T(8,128)(2,1)S(1)}, u32[]{:S(2)}, u32[]{:S(2)}) %collective-permute-start.26) | collective-permute-done | bytes 786464 | tf_op jit(solution)/shard_map/ppermute | solution.py:518
  118.8 2.5 %join.1 = (bf16[512,1024]{1,0:T(8,128)(2,1)}, bf16[512,1024]{1,0:T(8,128)(2,1)}, bf16[512,1024]{1,0:T(8,128)(2,1)}) custom-call(s32[2]{0:T(128)S(1)} %copy-done.2, bf16[512,512]{1,0:T(8,128)(2,1)S(1)} %join_value.1._after._after_edge.value_ref, bf16[3,512,256]{2,1,0:T(8,128)(2,1)S(1)} %get-tuple-element.111.own, ...), custom_call_target="tpu_custom_call" | custom-call | flops 2200000000 | bytes 7000000 | tf_op jit(solution)/shard_map/join/pallas_call | solution.py:718
  121.2 3.2 %collective-permute-done.24.y2 = bf16[2,512,128]{2,1,0:T(8,128)(2,1)S(1)} collective-permute-done((bf16[2,512,128]{2,1,0:T(8,128)(2,1)S(1)}, bf16[2,512,128]{2,1,0:T(8,128)(2,1)S(1)}, u32[]{:S(2)}, u32[]{:S(2)}) %collective-permute-start.24) | collective-permute-done | bytes 262176 | tf_op jit(solution)/shard_map/ppermute | solution.py:515
  (51 shorter events, 17.6 us)
Async XLA Ops:
  0.6 26.6 %collective-permute-start.1 = (bf16[1,512,2048]{2,1,0:T(8,128)(2,1)}, bf16[1,512,2048]{2,1,0:T(8,128)(2,1)S(1)}, u32[]{:S(2)}, u32[]{:S(2)}) collective-permute-start(bf16[1,512,2048]{2,1,0:T(8,128)(2,1)} %param.9), channel_id=1, source_target_pairs={{8,0},{16,8},{24,16},{0,24},{9,1},{17,9},{25,17},{1,25},{10,2},{18... | collective-permute-start | bytes 6291464 | tf_op jit(solution)/shard_map/ppermute | solution.py:745
  3.1 24.2 %copy-start.3 = (bf16[1,1024,2048]{2,1,0:T(8,128)(2,1)S(1)}, bf16[1,1024,2048]{2,1,0:T(8,128)(2,1)}, u32[]{:S(2)}) copy-start(bf16[1,1024,2048]{2,1,0:T(8,128)(2,1)} %param.10) | copy-start | bytes 12582916
  3.7 23.5 %copy-start.2 = (s32[2]{0:T(128)S(1)}, s32[2]{0:T(128)}, u32[]{:S(2)}) copy-start(s32[2]{0:T(128)} %pad_add_fusion.place) | copy-start | bytes 28
  8.2 19.1 %collective-permute-start = (bf16[3,512,256]{2,1,0:T(8,128)(2,1)}, bf16[3,512,256]{2,1,0:T(8,128)(2,1)S(1)}, u32[]{:S(2)}, u32[]{:S(2)}) collective-permute-start(bf16[3,512,256]{2,1,0:T(8,128)(2,1)} %get-tuple-element.60), channel_id=1, source_target_pairs={{0,1},{1,0},{2,3},{3,2},{4,5},{5,4},{6,7},{7,6},{8,9},{9,8},{10,11... | collective-permute-start | bytes 2359304 | tf_op jit(solution)/shard_map/ppermute | solution.py:518
  9.7 23.2 %collective-permute-start.2 = (bf16[1040,128]{1,0:T(8,128)(2,1)}, bf16[1040,128]{1,0:T(8,128)(2,1)S(1)}, u32[]{:S(2)}, u32[]{:S(2)}) collective-permute-start(bf16[1040,128]{1,0:T(8,128)(2,1)} %get-tuple-element.62), channel_id=1, source_target_pairs={{0,2},{1,3},{2,4},{3,5},{4,6},{5,7},{6,0},{7,1},{8,10},{9,11},{10,... | collective-permute-start | bytes 798728 | tf_op jit(solution)/shard_map/ppermute | solution.py:515
  11.3 21.6 %collective-permute-start.3 = (bf16[1040,128]{1,0:T(8,128)(2,1)}, bf16[1040,128]{1,0:T(8,128)(2,1)S(1)}, u32[]{:S(2)}, u32[]{:S(2)}) collective-permute-start(bf16[1040,128]{1,0:T(8,128)(2,1)} %get-tuple-element.63), channel_id=1, source_target_pairs={{0,4},{1,5},{2,6},{3,7},{4,0},{5,1},{6,2},{7,3},{8,12},{9,13},{10,... | collective-permute-start | bytes 798728 | tf_op jit(solution)/shard_map/ppermute | solution.py:515
  13.9 19.0 %collective-permute-start.4 = (bf16[1040,128]{1,0:T(8,128)(2,1)}, bf16[1040,128]{1,0:T(8,128)(2,1)S(1)}, u32[]{:S(2)}, u32[]{:S(2)}) collective-permute-start(bf16[1040,128]{1,0:T(8,128)(2,1)} %get-tuple-element.64), channel_id=1, source_target_pairs={{0,6},{1,7},{2,0},{3,1},{4,2},{5,3},{6,4},{7,5},{8,14},{9,15},{10,... | collective-permute-start | bytes 798728 | tf_op jit(solution)/shard_map/ppermute | solution.py:515
  27.2 5.7 %copy-start.4 = (bf16[1,512,1024]{2,1,0:T(8,128)(2,1)S(1)}, bf16[1,512,1024]{2,1,0:T(8,128)(2,1)}, u32[]{:S(2)}) copy-start(bf16[1,512,1024]{2,1,0:T(8,128)(2,1)} %param.8) | copy-start | bytes 3145732
  31.1 9.2 %copy-start.1 = (bf16[1040,128]{1,0:T(8,128)(2,1)S(1)}, bf16[1040,128]{1,0:T(8,128)(2,1)}, u32[]{:S(2)}) copy-start(bf16[1040,128]{1,0:T(8,128)(2,1)} %get-tuple-element.66.x0) | copy-start | bytes 798724
  31.1 22.3 %collective-permute-start.5 = (bf16[512,256]{1,0:T(8,128)(2,1)S(1)}, bf16[512,256]{1,0:T(8,128)(2,1)S(1)}, u32[]{:S(2)}, u32[]{:S(2)}) collective-permute-start(bf16[512,256]{1,0:T(8,128)(2,1)S(1)} %get-tuple-element.69), channel_id=1, source_target_pairs={{0,1},{1,0},{2,3},{3,2},{4,5},{5,4},{6,7},{7,6},{8,9},{9,8},{10,11... | collective-permute-start | bytes 786440 | tf_op jit(solution)/shard_map/ppermute | solution.py:518
  33.6 10.0 %collective-permute-start.6 = (bf16[512,128]{1,0:T(8,128)(2,1)S(1)}, bf16[512,128]{1,0:T(8,128)(2,1)S(1)}, u32[]{:S(2)}, u32[]{:S(2)}) collective-permute-start(bf16[512,128]{1,0:T(8,128)(2,1)S(1)} %get-tuple-element.71), channel_id=1, source_target_pairs={{0,2},{1,3},{2,4},{3,5},{4,6},{5,7},{6,0},{7,1},{8,10},{9,11},{10,... | collective-permute-start | bytes 393224 | tf_op jit(solution)/shard_map/ppermute | solution.py:515
  37.9 10.0 %collective-permute-start.7 = (bf16[512,128]{1,0:T(8,128)(2,1)S(1)}, bf16[512,128]{1,0:T(8,128)(2,1)S(1)}, u32[]{:S(2)}, u32[]{:S(2)}) collective-permute-start(bf16[512,128]{1,0:T(8,128)(2,1)S(1)} %get-tuple-element.72), channel_id=1, source_target_pairs={{0,4},{1,5},{2,6},{3,7},{4,0},{5,1},{6,2},{7,3},{8,12},{9,13},{10,... | collective-permute-start | bytes 393224 | tf_op jit(solution)/shard_map/ppermute | solution.py:515
  39.5 8.6 %collective-permute-start.8 = (bf16[512,128]{1,0:T(8,128)(2,1)S(1)}, bf16[512,128]{1,0:T(8,128)(2,1)S(1)}, u32[]{:S(2)}, u32[]{:S(2)}) collective-permute-start(bf16[512,128]{1,0:T(8,128)(2,1)S(1)} %get-tuple-element.73), channel_id=1, source_target_pairs={{0,6},{1,7},{2,0},{3,1},{4,2},{5,3},{6,4},{7,5},{8,14},{9,15},{10,... | collective-permute-start | bytes 393224 | tf_op jit(solution)/shard_map/ppermute | solution.py:515
  43.0 14.2 %collective-permute-start.9 = (bf16[2064,128]{1,0:T(8,128)(2,1)S(1)}, bf16[2064,128]{1,0:T(8,128)(2,1)S(1)}, u32[]{:S(2)}, u32[]{:S(2)}) collective-permute-start(bf16[2064,128]{1,0:T(8,128)(2,1)S(1)} %get-tuple-element.68._after), channel_id=1, source_target_pairs={{0,1},{1,0},{2,3},{3,2},{4,5},{5,4},{6,7},{7,6},{8,9},{9,8},{10,11... | collective-permute-start | bytes 1585160 | tf_op jit(solution)/shard_map/ppermute | solution.py:518
  43.6 18.7 %collective-permute-start.10 = (bf16[512,128]{1,0:T(8,128)(2,1)S(1)}, bf16[512,128]{1,0:T(8,128)(2,1)S(1)}, u32[]{:S(2)}, u32[]{:S(2)}) collective-permute-start(bf16[512,128]{1,0:T(8,128)(2,1)S(1)} %get-tuple-element.78), channel_id=1, source_target_pairs={{0,2},{1,3},{2,4},{3,5},{4,6},{5,7},{6,0},{7,1},{8,10},{9,11},{10,... | collective-permute-start | bytes 393224 | tf_op jit(solution)/shard_map/ppermute | solution.py:515
  47.9 14.4 %collective-permute-start.11 = (bf16[512,128]{1,0:T(8,128)(2,1)S(1)}, bf16[512,128]{1,0:T(8,128)(2,1)S(1)}, u32[]{:S(2)}, u32[]{:S(2)}) collective-permute-start(bf16[512,128]{1,0:T(8,128)(2,1)S(1)} %get-tuple-element.79), channel_id=1, source_target_pairs={{0,4},{1,5},{2,6},{3,7},{4,0},{5,1},{6,2},{7,3},{8,12},{9,13},{10,... | collective-permute-start | bytes 393224 | tf_op jit(solution)/shard_map/ppermute | solution.py:515
  48.1 14.2 %collective-permute-start.12 = (bf16[512,128]{1,0:T(8,128)(2,1)S(1)}, bf16[512,128]{1,0:T(8,128)(2,1)S(1)}, u32[]{:S(2)}, u32[]{:S(2)}) collective-permute-start(bf16[512,128]{1,0:T(8,128)(2,1)S(1)} %get-tuple-element.80), channel_id=1, source_target_pairs={{0,6},{1,7},{2,0},{3,1},{4,2},{5,3},{6,4},{7,5},{8,14},{9,15},{10,... | collective-permute-start | bytes 393224 | tf_op jit(solution)/shard_map/ppermute | solution.py:515
  54.8 12.3 %collective-permute-start.13 = (bf16[1024,128]{1,0:T(8,128)(2,1)S(1)}, bf16[1024,128]{1,0:T(8,128)(2,1)S(1)}, u32[]{:S(2)}, u32[]{:S(2)}) collective-permute-start(bf16[1024,128]{1,0:T(8,128)(2,1)S(1)} %get-tuple-element.74._after), channel_id=1, source_target_pairs={{0,1},{1,0},{2,3},{3,2},{4,5},{5,4},{6,7},{7,6},{8,9},{9,8},{10,11... | collective-permute-start | bytes 786440 | tf_op jit(solution)/shard_map/ppermute | solution.py:518
  57.2 5.1 %copy-start = (bf16[3,512,256]{2,1,0:T(8,128)(2,1)S(1)}, bf16[3,512,256]{2,1,0:T(8,128)(2,1)}, u32[]{:S(2)}) copy-start(bf16[3,512,256]{2,1,0:T(8,128)(2,1)} %get-tuple-element.81.own) | copy-start | bytes 2359300
  63.7 6.4 %collective-permute-start.14 = (bf16[1024,128]{1,0:T(8,128)(2,1)S(1)}, bf16[1024,128]{1,0:T(8,128)(2,1)S(1)}, u32[]{:S(2)}, u32[]{:S(2)}) collective-permute-start(bf16[1024,128]{1,0:T(8,128)(2,1)S(1)} %get-tuple-element.88), channel_id=1, source_target_pairs={{0,1},{1,0},{2,3},{3,2},{4,5},{5,4},{6,7},{7,6},{8,9},{9,8},{10,11... | collective-permute-start | bytes 786440 | tf_op jit(solution)/shard_map/ppermute | solution.py:518
  64.3 24.8 %collective-permute-start.17 = (bf16[2,512,256]{2,1,0:T(8,128)(2,1)S(1)}, bf16[2,512,256]{2,1,0:T(8,128)(2,1)S(1)}, u32[]{:S(2)}, u32[]{:S(2)}) collective-permute-start(bf16[2,512,256]{2,1,0:T(8,128)(2,1)S(1)} %get-tuple-element.82._after.edge), channel_id=1, source_target_pairs={{0,2},{1,3},{2,4},{3,5},{4,6},{5,7},{8,10},{9,11},{10,12},{11,13},... | collective-permute-start | bytes 1572872 | tf_op jit(solution)/shard_map/ppermute | solution.py:616
  68.9 18.2 %collective-permute-start.16 = (bf16[2,512,256]{2,1,0:T(8,128)(2,1)S(1)}, bf16[2,512,256]{2,1,0:T(8,128)(2,1)S(1)}, u32[]{:S(2)}, u32[]{:S(2)}) collective-permute-start(bf16[2,512,256]{2,1,0:T(8,128)(2,1)S(1)} %get-tuple-element.98), channel_id=1, source_target_pairs={{2,0},{3,1},{4,2},{5,3},{6,4},{7,5},{10,8},{11,9},{12,10},{13,11},... | collective-permute-start | bytes 1572872 | tf_op jit(solution)/shard_map/ppermute | solution.py:628
  72.9 7.8 %collective-permute-start.15 = (bf16[1,1024,128]{2,1,0:T(8,128)(2,1)S(1)}, bf16[1,1024,128]{2,1,0:T(8,128)(2,1)S(1)}, u32[]{:S(2)}, u32[]{:S(2)}) collective-permute-start(bf16[1,1024,128]{2,1,0:T(8,128)(2,1)S(1)} %get-tuple-element.89._after), channel_id=1, source_target_pairs={{0,1},{1,0},{2,3},{3,2},{4,5},{5,4},{6,7},{7,6},{8,9},{9,8},{10,11... | collective-permute-start | bytes 786440 | tf_op jit(solution)/shard_map/ppermute | solution.py:518
  78.1 19.7 %collective-permute-start.18 = (bf16[2,1024,128]{2,1,0:T(8,128)(2,1)S(1)}, bf16[2,1024,128]{2,1,0:T(8,128)(2,1)S(1)}, u32[]{:S(2)}, u32[]{:S(2)}) collective-permute-start(bf16[2,1024,128]{2,1,0:T(8,128)(2,1)S(1)} %get-tuple-element.94._after._after_edge), channel_id=1, source_target_pairs={{0,1},{1,0},{2,3},{3,2},{4,5},{5,4},{6,7},{7,6},{8,9},{9,8},{10,11... | collective-permute-start | bytes 1572872 | tf_op jit(solution)/shard_map/ppermute | solution.py:518
  83.2 20.8 %collective-permute-start.21 = (bf16[1,512,128]{2,1,0:T(8,128)(2,1)S(1)}, bf16[1,512,128]{2,1,0:T(8,128)(2,1)S(1)}, u32[]{:S(2)}, u32[]{:S(2)}) collective-permute-start(bf16[1,512,128]{2,1,0:T(8,128)(2,1)S(1)} %get-tuple-element.107), channel_id=1, source_target_pairs={{0,6},{1,7},{2,0},{3,1},{4,2},{5,3},{6,4},{7,5},{8,14},{9,15},{10,... | collective-permute-start | bytes 393224 | tf_op jit(solution)/shard_map/ppermute | solution.py:515
  86.4 17.6 %collective-permute-start.22 = (bf16[1,512,128]{2,1,0:T(8,128)(2,1)S(1)}, bf16[1,512,128]{2,1,0:T(8,128)(2,1)S(1)}, u32[]{:S(2)}, u32[]{:S(2)}) collective-permute-start(bf16[1,512,128]{2,1,0:T(8,128)(2,1)S(1)} %get-tuple-element.108), channel_id=1, source_target_pairs={{0,4},{1,5},{2,6},{3,7},{4,0},{5,1},{6,2},{7,3},{8,12},{9,13},{10,... | collective-permute-start | bytes 393224 | tf_op jit(solution)/shard_map/ppermute | solution.py:515
  87.1 16.9 %collective-permute-start.23 = (bf16[1,512,128]{2,1,0:T(8,128)(2,1)S(1)}, bf16[1,512,128]{2,1,0:T(8,128)(2,1)S(1)}, u32[]{:S(2)}, u32[]{:S(2)}) collective-permute-start(bf16[1,512,128]{2,1,0:T(8,128)(2,1)S(1)} %get-tuple-element.109), channel_id=1, source_target_pairs={{0,2},{1,3},{2,4},{3,5},{4,6},{5,7},{6,0},{7,1},{8,10},{9,11},{10,... | collective-permute-start | bytes 393224 | tf_op jit(solution)/shard_map/ppermute | solution.py:515
  96.4 5.6 %collective-permute-start.20 = (f32[8,512]{1,0:T(8,128)S(1)}, f32[8,512]{1,0:T(8,128)S(1)}, u32[]{:S(2)}, u32[]{:S(2)}) collective-permute-start(f32[8,512]{1,0:T(8,128)S(1)} %get-tuple-element.99._after._after_edge), channel_id=1, source_target_pairs={{2,0},{3,1},{4,2},{5,3},{6,4},{7,5},{10,8},{11,9},{12,10},{13,11},... | collective-permute-start | bytes 49160 | tf_op jit(solution)/shard_map/ppermute | solution.py:691
  103.9 14.9 %collective-permute-start.26 = (bf16[3,512,256]{2,1,0:T(8,128)(2,1)S(1)}, bf16[3,512,256]{2,1,0:T(8,128)(2,1)S(1)}, u32[]{:S(2)}, u32[]{:S(2)}) collective-permute-start(bf16[3,512,256]{2,1,0:T(8,128)(2,1)S(1)} %get-tuple-element.106._after), channel_id=1, source_target_pairs={{0,1},{1,0},{2,3},{3,2},{4,5},{5,4},{6,7},{7,6},{8,9},{9,8},{10,11... | collective-permute-start | bytes 2359304 | tf_op jit(solution)/shard_map/ppermute | solution.py:518
  105.8 18.6 %collective-permute-start.24 = (bf16[2,512,128]{2,1,0:T(8,128)(2,1)S(1)}, bf16[2,512,128]{2,1,0:T(8,128)(2,1)S(1)}, u32[]{:S(2)}, u32[]{:S(2)}) collective-permute-start(bf16[2,512,128]{2,1,0:T(8,128)(2,1)S(1)} %unsort_last.1), channel_id=1, source_target_pairs={{0,4},{1,5},{2,6},{3,7},{4,0},{5,1},{6,2},{7,3},{8,12},{9,13},{10,... | collective-permute-start | bytes 786440 | tf_op jit(solution)/shard_map/ppermute | solution.py:515
  107.5 17.0 %collective-permute-start.19 = (bf16[2,512,128]{2,1,0:T(8,128)(2,1)S(1)}, bf16[2,512,128]{2,1,0:T(8,128)(2,1)S(1)}, u32[]{:S(2)}, u32[]{:S(2)}) collective-permute-start(bf16[2,512,128]{2,1,0:T(8,128)(2,1)S(1)} %get-tuple-element.102), channel_id=1, source_target_pairs={{0,6},{1,7},{2,0},{3,1},{4,2},{5,3},{6,4},{7,5},{8,14},{9,15},{10,... | collective-permute-start | bytes 786440 | tf_op jit(solution)/shard_map/ppermute | solution.py:515
  109.7 14.8 %collective-permute-start.25 = (bf16[2,512,128]{2,1,0:T(8,128)(2,1)S(1)}, bf16[2,512,128]{2,1,0:T(8,128)(2,1)S(1)}, u32[]{:S(2)}, u32[]{:S(2)}) collective-permute-start(bf16[2,512,128]{2,1,0:T(8,128)(2,1)S(1)} %get-tuple-element.110), channel_id=1, source_target_pairs={{0,2},{1,3},{2,4},{3,5},{4,6},{5,7},{6,0},{7,1},{8,10},{9,11},{10,... | collective-permute-start | bytes 786440 | tf_op jit(solution)/shard_map/ppermute | solution.py:515

commit v5 on v4

--- a/solution.py
+++ b/solution.py
@@ -690,6 +690,15 @@
     )(where, natural_v[0], query_edge_got, local_own, local_got, g_own, g_got, edge_got)
     stats_got = lax.ppermute(stats, "seq", behind)
     first_natural = unsort((0, 1, 3), stats, stats, own, returned, "unsort_first")
+    value_left = pl.pallas_call(
+        join_value_kernel,
+        out_shape=struct(tok, HR * HD),
+        in_specs=smem() + vmem(5),
+        out_specs=vmem()[0],
+        compiler_params=params(16),
+        cost_estimate=takes(12),
+        name="join_value",
+    )(where, first_natural[0], *home_v)
     settled_own, settled_send = pl.pallas_call(
         settle_kernel,
         out_shape=[struct(3, tok, width)] * 2,
@@ -699,18 +708,9 @@
         compiler_params=params(20),
         cost_estimate=takes(0.1),
         name="settle",
-    )(where, first_natural[0], dq_local, early, late, edge, query_edge_got, stats_got)
+    )(where, value_left, dq_local, early, late, edge, query_edge_got, stats_got)
     settled_got = swap(settled_send)
-    value_left = pl.pallas_call(
-        join_value_kernel,
-        out_shape=struct(tok, HR * HD),
-        in_specs=smem() + vmem(5),
-        out_specs=vmem()[0],
-        compiler_params=params(16),
-        cost_estimate=takes(12),
-        name="join_value",
-    )(where, settled_send, *home_v)
-    last_natural = unsort((2,), value_left, value_left, own, returned, "unsort_last")
+    last_natural = unsort((2,), settled_send, settled_send, own, returned, "unsort_last")
     natural = [*first_natural]
     natural.insert(2, *last_natural)
     home = [natural[0]] + [among_groups(natural[d], -d) for d in range(1, HR)]

time: 127 us -> 127 us (level)
  transfers between devices with their start and end apart: 27 -> 27, of which waited for: 7 -> 7; matrix products, arithmetic and copies ran while one was open for 1% -> 1% of each run, Pallas kernels for 37% -> 36%
where the time goes in v5:
time: 127 us; the launch traced here: 126 us
  Pallas kernels  48.3 us (38%)
  starting transfers between devices  44.4 us (35%)
  waiting for transfers between devices  31.1 us (24%)
    ppermute x15, starting transfers between devices, among_groups(): return lax.ppermute(block, 'seq', route)  29.2 us
    ppermute x8, waiting for transfers between devices, swap(): return lax.ppermute(block, 'seq', [(i, i ^ 1) for i in range(devices)])  24.1 us
    pallas_call x1, Pallas kernels, pair_body(): pl.pallas_call(window_kernel, out_shape=[struct(2, tok, width), struct(2,...  7.37 us
    ppermute x8, starting transfers between devices, swap(): return lax.ppermute(block, 'seq', [(i, i ^ 1) for i in range(devices)])  7.32 us
    pallas_call x3, Pallas kernels, unsort(): pl.pallas_call(functools.partial(unsort_kernel, unit, distances), out_sha...  6.03 us
    ppermute x15, waiting for transfers between devices, among_groups(): return lax.ppermute(block, 'seq', route)  5.78 us
    pallas_call x1, Pallas kernels, pair_body(): pl.pallas_call(functools.partial(probs_kernel, unit), out_shape=[struct(H...  5.1 us
    pallas_call x1, Pallas kernels, pair_body(): pl.pallas_call(functools.partial(grads_kernel, unit), out_shape=[struct(H...  4.61 us
  transfers between devices with their start and end apart: 27, of which 7 were waited for; matrix products, arithmetic and copies ran while one was open for 1% of the time, Pallas kernels for 36%

profile of v5, /device:TPU:0, one launch (start us, length us, event | category | flops | bytes accessed | tf_op | source)
XLA Modules:
  0.0 125.5 jit_solution(14872509374432351556)
XLA Ops:
  0.6 2.4 %collective-permute-start.1 = (bf16[1,512,2048]{2,1,0:T(8,128)(2,1)}, bf16[1,512,2048]{2,1,0:T(8,128)(2,1)S(1)}, u32[]{:S(2)}, u32[]{:S(2)}) collective-permute-start(bf16[1,512,2048]{2,1,0:T(8,128)(2,1)} %param.9), channel_id=1, source_target_pairs={{8,0},{16,8},{24,16},{0,24},{9,1},{17,9},{25,17},{1,25},{10,2},{18... | collective-permute-start | bytes 6291464 | tf_op jit(solution)/shard_map/ppermute | solution.py:745
  3.7 4.4 %split.1 = (bf16[1040,128]{1,0:T(8,128)(2,1)}, bf16[1040,128]{1,0:T(8,128)(2,1)}, bf16[1040,128]{1,0:T(8,128)(2,1)}, bf16[1040,128]{1,0:T(8,128)(2,1)}, bf16[3,5...) custom-call(s32[2]{0:T(128)} %pad_add_fusion.place, s32[4,512]{1,0:T(4,128)} %bitcast.17, bf16[512,1024]{1,0:T(8,128)(2,1)} %bitcast.15, ...), custom_call_target="tpu_custom_call" | custom-call | flops 2200000000 | bytes 7000000 | tf_op jit(solution)/shard_map/split/pallas_call | solution.py:523
  8.2 1.6 %collective-permute-start = (bf16[3,512,256]{2,1,0:T(8,128)(2,1)}, bf16[3,512,256]{2,1,0:T(8,128)(2,1)S(1)}, u32[]{:S(2)}, u32[]{:S(2)}) collective-permute-start(bf16[3,512,256]{2,1,0:T(8,128)(2,1)} %get-tuple-element.60), channel_id=1, source_target_pairs={{0,1},{1,0},{2,3},{3,2},{4,5},{5,4},{6,7},{7,6},{8,9},{9,8},{10,11... | collective-permute-start | bytes 2359304 | tf_op jit(solution)/shard_map/ppermute | solution.py:518
  9.7 1.6 %collective-permute-start.2 = (bf16[1040,128]{1,0:T(8,128)(2,1)}, bf16[1040,128]{1,0:T(8,128)(2,1)S(1)}, u32[]{:S(2)}, u32[]{:S(2)}) collective-permute-start(bf16[1040,128]{1,0:T(8,128)(2,1)} %get-tuple-element.62), channel_id=1, source_target_pairs={{0,2},{1,3},{2,4},{3,5},{4,6},{5,7},{6,0},{7,1},{8,10},{9,11},{10,... | collective-permute-start | bytes 798728 | tf_op jit(solution)/shard_map/ppermute | solution.py:515
  11.3 2.6 %collective-permute-start.3 = (bf16[1040,128]{1,0:T(8,128)(2,1)}, bf16[1040,128]{1,0:T(8,128)(2,1)S(1)}, u32[]{:S(2)}, u32[]{:S(2)}) collective-permute-start(bf16[1040,128]{1,0:T(8,128)(2,1)} %get-tuple-element.63), channel_id=1, source_target_pairs={{0,4},{1,5},{2,6},{3,7},{4,0},{5,1},{6,2},{7,3},{8,12},{9,13},{10,... | collective-permute-start | bytes 798728 | tf_op jit(solution)/shard_map/ppermute | solution.py:515
  15.3 12.0 %collective-permute-done._after_local.got = bf16[3,512,256]{2,1,0:T(8,128)(2,1)S(1)} collective-permute-done((bf16[3,512,256]{2,1,0:T(8,128)(2,1)}, bf16[3,512,256]{2,1,0:T(8,128)(2,1)S(1)}, u32[]{:S(2)}, u32[]{:S(2)}) %collective-permute-start) | collective-permute-done | bytes 786464 | tf_op jit(solution)/shard_map/ppermute | solution.py:518
  27.3 3.8 %project.1 = (bf16[512,128]{1,0:T(8,128)(2,1)S(1)}, bf16[512,128]{1,0:T(8,128)(2,1)S(1)}, bf16[512,128]{1,0:T(8,128)(2,1)S(1)}, bf16[512,128]{1,0:T(8,128)(2,1)S...) custom-call(s32[2]{0:T(128)S(1)} %copy-done.2, ...), custom_call_target="tpu_custom_call" | custom-call | flops 4180000000 | bytes 13300000 | tf_op jit(solution)/shard_map/project/pallas_call | solution.py:535
  31.1 1.8 %collective-permute-start.5 = (bf16[512,256]{1,0:T(8,128)(2,1)S(1)}, bf16[512,256]{1,0:T(8,128)(2,1)S(1)}, u32[]{:S(2)}, u32[]{:S(2)}) collective-permute-start(bf16[512,256]{1,0:T(8,128)(2,1)S(1)} %get-tuple-element.69), channel_id=1, source_target_pairs={{0,1},{1,0},{2,3},{3,2},{4,5},{5,4},{6,7},{7,6},{8,9},{9,8},{10,11... | collective-permute-start | bytes 786440 | tf_op jit(solution)/shard_map/ppermute | solution.py:518
  33.6 4.3 %collective-permute-start.6 = (bf16[512,128]{1,0:T(8,128)(2,1)S(1)}, bf16[512,128]{1,0:T(8,128)(2,1)S(1)}, u32[]{:S(2)}, u32[]{:S(2)}) collective-permute-start(bf16[512,128]{1,0:T(8,128)(2,1)S(1)} %get-tuple-element.71), channel_id=1, source_target_pairs={{0,2},{1,3},{2,4},{3,5},{4,6},{5,7},{6,0},{7,1},{8,10},{9,11},{10,... | collective-permute-start | bytes 393224 | tf_op jit(solution)/shard_map/ppermute | solution.py:515
  37.9 1.6 %collective-permute-start.7 = (bf16[512,128]{1,0:T(8,128)(2,1)S(1)}, bf16[512,128]{1,0:T(8,128)(2,1)S(1)}, u32[]{:S(2)}, u32[]{:S(2)}) collective-permute-start(bf16[512,128]{1,0:T(8,128)(2,1)S(1)} %get-tuple-element.72), channel_id=1, source_target_pairs={{0,4},{1,5},{2,6},{3,7},{4,0},{5,1},{6,2},{7,3},{8,12},{9,13},{10,... | collective-permute-start | bytes 393224 | tf_op jit(solution)/shard_map/ppermute | solution.py:515
  40.3 2.6 %pack.1 = (bf16[4,2,512,128]{3,2,1,0:T(8,128)(2,1)S(1)}, bf16[2064,128]{1,0:T(8,128)(2,1)S(1)}, f32[8,512]{1,0:T(8,128)S(1)}, f32[512,128]{1,0:T(8,128)S(1)}, s32[4]{0:T(128)S(1)}) custom-call(s32[2]{0:T(128)S(1)} %copy-done.2, bf16[512,128]{1,0:T(8,128)(2,1)S(1)} %get-tuple-element.65._after.x0, bf16[1040,128]{1,0:T(8,128)(2,1)S(1)} %copy-done.1, ...), custom_call_target="tpu_custom_call" | custom-call | flops 110000000 | bytes 350000 | tf_op jit(solution)/shard_map/pack/pallas_call | solution.py:565
  44.7 3.2 %collective-permute-done.7.x2 = bf16[512,128]{1,0:T(8,128)(2,1)S(1)} collective-permute-done((bf16[512,128]{1,0:T(8,128)(2,1)S(1)}, bf16[512,128]{1,0:T(8,128)(2,1)S(1)}, u32[]{:S(2)}, u32[]{:S(2)}) %collective-permute-start.7) | collective-permute-done | bytes 131104 | tf_op jit(solution)/shard_map/ppermute | solution.py:515
  48.1 5.4 %collective-permute-start.12 = (bf16[512,128]{1,0:T(8,128)(2,1)S(1)}, bf16[512,128]{1,0:T(8,128)(2,1)S(1)}, u32[]{:S(2)}, u32[]{:S(2)}) collective-permute-start(bf16[512,128]{1,0:T(8,128)(2,1)S(1)} %get-tuple-element.80), channel_id=1, source_target_pairs={{0,6},{1,7},{2,0},{3,1},{4,2},{5,3},{6,4},{7,5},{8,14},{9,15},{10,... | collective-permute-start | bytes 393224 | tf_op jit(solution)/shard_map/ppermute | solution.py:515
  55.3 1.9 %collective-permute-done.9.came_ref = bf16[2064,128]{1,0:T(8,128)(2,1)S(1)} collective-permute-done((bf16[2064,128]{1,0:T(8,128)(2,1)S(1)}, bf16[2064,128]{1,0:T(8,128)(2,1)S(1)}, u32[]{:S(2)}, u32[]{:S(2)}) %collective-permute-start.9) | collective-permute-done | bytes 528416 | tf_op jit(solution)/shard_map/ppermute | solution.py:518
  57.2 5.1 %probs.1 = (s32[4]{0:T(128)S(1)}, bf16[2048,128]{1,0:T(8,128)(2,1)S(1)}, bf16[2048,128]{1,0:T(8,128)(2,1)S(1)}, bf16[128,2048]{1,0:T(8,128)(2,1)S(1)}, bf16[2048,2048]{1,0:T(8,128)(2,1)S(1)}) custom-call(s32[2]{0:T(128)S(1)} %copy-done.2, s32[4]{0:T(128)S(1)} %get-tuple-element.67.kept_ref, bf16[1024,128]{1,0:T(8,128)(2,1)S(1)} %get-tuple-element.74._after, ...), custom_call_target="tpu_custom_call" | custom-call | flops 5500000256 | bytes 17500000 | tf_op jit(solution)/shard_map/probs/pallas_call | solution.py:593
  64.2 2.9 %collective-permute-start.17 = (bf16[2,512,256]{2,1,0:T(8,128)(2,1)S(1)}, bf16[2,512,256]{2,1,0:T(8,128)(2,1)S(1)}, u32[]{:S(2)}, u32[]{:S(2)}) collective-permute-start(bf16[2,512,256]{2,1,0:T(8,128)(2,1)S(1)} %get-tuple-element.82._after.edge), channel_id=1, source_target_pairs={{0,2},{1,3},{2,4},{3,5},{4,6},{5,7},{8,10},{9,11},{10,12},{11,13},... | collective-permute-start | bytes 1572872 | tf_op jit(solution)/shard_map/ppermute | solution.py:616
  67.1 1.7 %mix.1 = (bf16[2048,128]{1,0:T(8,128)(2,1)S(1)}, f32[128,2048]{1,0:T(8,128)S(1)}, bf16[2,512,256]{2,1,0:T(8,128)(2,1)S(1)}) custom-call(s32[2]{0:T(128)S(1)} %copy-done.2, s32[4]{0:T(128)S(1)} %get-tuple-element.67.kept_ref, s32[4]{0:T(128)S(1)} %get-tuple-element.76.got_ref, bf16[2,512,256]{2,1,0:T(8,128)(2,1)S(1)} %get-tuple-element.82._after.edge, ...), custom_call_target="tpu_custom_call" | custom-call | flops 1870000000 | bytes 5950000 | tf_op jit(solution)/shard_map/mix/pallas_call | solution.py:618
  70.2 2.7 %value_grads.1 = (bf16[2048,128]{1,0:T(8,128)(2,1)S(1)}, bf16[4,1,512,128]{3,2,1,0:T(8,128)(2,1)S(1)}, bf16[1,1024,128]{2,1,0:T(8,128)(2,1)S(1)}) custom-call(s32[2]{0:T(128)S(1)} %copy-done.2, s32[4]{0:T(128)S(1)} %get-tuple-element.67.kept_ref, s32[4]{0:T(128)S(1)} %get-tuple-element.76.got_ref, f32[128,2048]{1,0:T(8,128)S(1)} %get-tuple-element.86._after.ot_ref, ...), custom_call_target="tpu_custom_call" | custom-call | flops 2640000000 | bytes 8400000 | tf_op jit(solution)/shard_map/value_grads/pallas_call | solution.py:630
  73.5 4.6 %grads.1 = (bf16[4,2,512,128]{3,2,1,0:T(8,128)(2,1)S(1)}, bf16[2,1024,128]{2,1,0:T(8,128)(2,1)S(1)}) custom-call(s32[2]{0:T(128)S(1)} %copy-done.2, s32[4]{0:T(128)S(1)} %get-tuple-element.67.kept_ref, s32[4]{0:T(128)S(1)} %get-tuple-element.76.got_ref, bf16[1,1024,128]{2,1,0:T(8,128)(2,1)S(1)} %get-tuple-element.89._after, ...), custom_call_target="tpu_custom_call" | custom-call | flops 5500000256 | bytes 17500000 | tf_op jit(solution)/shard_map/grads/pallas_call | solution.py:640
  78.1 1.6 %collective-permute-start.18 = (bf16[2,1024,128]{2,1,0:T(8,128)(2,1)S(1)}, bf16[2,1024,128]{2,1,0:T(8,128)(2,1)S(1)}, u32[]{:S(2)}, u32[]{:S(2)}) collective-permute-start(bf16[2,1024,128]{2,1,0:T(8,128)(2,1)S(1)} %get-tuple-element.94._after._after_edge), channel_id=1, source_target_pairs={{0,1},{1,0},{2,3},{3,2},{4,5},{5,4},{6,7},{7,6},{8,9},{9,8},{10,11... | collective-permute-start | bytes 1572872 | tf_op jit(solution)/shard_map/ppermute | solution.py:518
  80.8 2.6 %unsort_value.1 = (bf16[1,512,128]{2,1,0:T(8,128)(2,1)S(1)}, bf16[1,512,128]{2,1,0:T(8,128)(2,1)S(1)}, bf16[1,512,128]{2,1,0:T(8,128)(2,1)S(1)}, bf16[1,512,128]{2,1,0:T(8,128)(2,1)S(1)}) custom-call(s32[4]{0:T(128)S(1)} %get-tuple-element.67.kept_ref, bf16[2,1024,128]{2,1,0:T(8,128)(2,1)S(1)} %get-tuple-element.94._after._after_edge, ...), custom_call_target="tpu_custom_call" | custom-call | flops 2860000000 | bytes 9100000 | tf_op jit(solution)/shard_map/unsort_value/pallas_call | solution.py:653
  83.3 3.0 %collective-permute-start.20 = (bf16[1,512,128]{2,1,0:T(8,128)(2,1)S(1)}, bf16[1,512,128]{2,1,0:T(8,128)(2,1)S(1)}, u32[]{:S(2)}, u32[]{:S(2)}) collective-permute-start(bf16[1,512,128]{2,1,0:T(8,128)(2,1)S(1)} %get-tuple-element.103), channel_id=1, source_target_pairs={{0,6},{1,7},{2,0},{3,1},{4,2},{5,3},{6,4},{7,5},{8,14},{9,15},{10,... | collective-permute-start | bytes 393224 | tf_op jit(solution)/shard_map/ppermute | solution.py:515
  87.2 1.8 %collective-permute-start.22 = (bf16[1,512,128]{2,1,0:T(8,128)(2,1)S(1)}, bf16[1,512,128]{2,1,0:T(8,128)(2,1)S(1)}, u32[]{:S(2)}, u32[]{:S(2)}) collective-permute-start(bf16[1,512,128]{2,1,0:T(8,128)(2,1)S(1)} %get-tuple-element.105), channel_id=1, source_target_pairs={{0,2},{1,3},{2,4},{3,5},{4,6},{5,7},{6,0},{7,1},{8,10},{9,11},{10,... | collective-permute-start | bytes 393224 | tf_op jit(solution)/shard_map/ppermute | solution.py:515
  89.0 7.4 %window.1 = (bf16[2,512,256]{2,1,0:T(8,128)(2,1)S(1)}, bf16[2,512,256]{2,1,0:T(8,128)(2,1)S(1)}, f32[2,512,256]{2,1,0:T(8,128)S(1)}, f32[8,512]{1,0:T(8,128)S(1)}) custom-call(s32[2]{0:T(128)S(1)} %copy-done.2, bf16[1,512,128]{2,1,0:T(8,128)(2,1)S(1)} %get-tuple-element.97._after.v0, bf16[2,512,256]{2,1,0:T(8,128)(2,1)S(1)} %collective-permute-done.16._after_edge.ahead, ...), custom_call_target="tpu_custom_call" | custom-call | flops 110000000 | bytes 350000 | tf_op jit(solution)/shard_map/window/pallas_call | solution.py:668
  97.7 2.4 %unsort_first.1 = (bf16[2,512,128]{2,1,0:T(8,128)(2,1)S(1)}, bf16[2,512,128]{2,1,0:T(8,128)(2,1)S(1)}, bf16[2,512,128]{2,1,0:T(8,128)(2,1)S(1)}) custom-call(s32[4]{0:T(128)S(1)} %get-tuple-element.67.kept_ref, f32[8,512]{1,0:T(8,128)S(1)} %get-tuple-element.99._after._after_edge, f32[8,512]{1,0:T(8,128)S(1)} %get-tuple-element.99._after._after_edge, ...), custom_call_target="tpu_custom_call" | custom-call | flops 110000000 | bytes 350000 | tf_op jit(solution)/shard_map/unsort_first/pallas_call | solution.py:653
  102.0 1.9 %settle.1 = (bf16[3,512,256]{2,1,0:T(8,128)(2,1)S(1)}, bf16[3,512,256]{2,1,0:T(8,128)(2,1)S(1)}) custom-call(s32[2]{0:T(128)S(1)} %copy-done.2, bf16[512,512]{1,0:T(8,128)(2,1)S(1)} %join_value.1._after.value_ref, bf16[2,512,256]{2,1,0:T(8,128)(2,1)S(1)} %get-tuple-element.106.dq_ref, bf16[2,512,256]{2,1,0:T(8,128)(2,1)S(1)} %get-tuple-element.107.early_ref, ...), custom_call_target="tpu_custom_call" | custom-call | flops 110000000 | bytes 350000 | tf_op jit(solution)/shard_map/settle/pallas_call | solution.py:702
  105.1 2.5 %collective-permute-start.24 = (bf16[2,512,128]{2,1,0:T(8,128)(2,1)S(1)}, bf16[2,512,128]{2,1,0:T(8,128)(2,1)S(1)}, u32[]{:S(2)}, u32[]{:S(2)}) collective-permute-start(bf16[2,512,128]{2,1,0:T(8,128)(2,1)S(1)} %unsort_last.1), channel_id=1, source_target_pairs={{0,4},{1,5},{2,6},{3,7},{4,0},{5,1},{6,2},{7,3},{8,12},{9,13},{10,... | collective-permute-start | bytes 786440 | tf_op jit(solution)/shard_map/ppermute | solution.py:515
  107.6 1.5 %collective-permute-start.19 = (bf16[2,512,128]{2,1,0:T(8,128)(2,1)S(1)}, bf16[2,512,128]{2,1,0:T(8,128)(2,1)S(1)}, u32[]{:S(2)}, u32[]{:S(2)}) collective-permute-start(bf16[2,512,128]{2,1,0:T(8,128)(2,1)S(1)} %get-tuple-element.102), channel_id=1, source_target_pairs={{0,6},{1,7},{2,0},{3,1},{4,2},{5,3},{6,4},{7,5},{8,14},{9,15},{10,... | collective-permute-start | bytes 786440 | tf_op jit(solution)/shard_map/ppermute | solution.py:515
  109.6 9.1 %collective-permute-done.26.got = bf16[3,512,256]{2,1,0:T(8,128)(2,1)S(1)} collective-permute-done((bf16[3,512,256]{2,1,0:T(8,128)(2,1)S(1)}, bf16[3,512,256]{2,1,0:T(8,128)(2,1)S(1)}, u32[]{:S(2)}, u32[]{:S(2)}) %collective-permute-start.26) | collective-permute-done | bytes 786464 | tf_op jit(solution)/shard_map/ppermute | solution.py:518
  118.7 2.5 %join.1 = (bf16[512,1024]{1,0:T(8,128)(2,1)}, bf16[512,1024]{1,0:T(8,128)(2,1)}, bf16[512,1024]{1,0:T(8,128)(2,1)}) custom-call(s32[2]{0:T(128)S(1)} %copy-done.2, bf16[512,512]{1,0:T(8,128)(2,1)S(1)} %join_value.1._after.value_ref, bf16[3,512,256]{2,1,0:T(8,128)(2,1)S(1)} %get-tuple-element.111.own, bf16[3,512,256]{2,1,0:T(8,128)(2,1)S(1)} %collective-permute-done.26.got), custom_call_target="tpu_custom_call" | custom-call | flops 2200000000 | bytes 7000000 | tf_op jit(solution)/shard_map/join/pallas_call | solution.py:718
  121.2 2.6 %collective-permute-done.24.y2 = bf16[2,512,128]{2,1,0:T(8,128)(2,1)S(1)} collective-permute-done((bf16[2,512,128]{2,1,0:T(8,128)(2,1)S(1)}, bf16[2,512,128]{2,1,0:T(8,128)(2,1)S(1)}, u32[]{:S(2)}, u32[]{:S(2)}) %collective-permute-start.24) | collective-permute-done | bytes 262176 | tf_op jit(solution)/shard_map/ppermute | solution.py:515
  123.8 1.6 %finish.1 = (bf16[512,1024]{1,0:T(8,128)(2,1)}, bf16[512,1024]{1,0:T(8,128)(2,1)}) custom-call(s32[2]{0:T(128)S(1)} %copy-done.2, bf16[2,512,128]{2,1,0:T(8,128)(2,1)S(1)} %get-tuple-element.101._after.y0, bf16[2,512,128]{2,1,0:T(8,128)(2,1)S(1)} %collective-permute-done.19.y1, ...), custom_call_target="tpu_custom_call", output_to_operand_aliasing={{0}: (5, {}), {1}: (6, {})} | custom-call | flops 1650000000 | bytes 5250000 | tf_op jit(solution)/shard_map/finish/pallas_call | solution.py:727
  (51 shorter events, 18.1 us)
Async XLA Ops:
  0.6 26.6 %collective-permute-start.1 = (bf16[1,512,2048]{2,1,0:T(8,128)(2,1)}, bf16[1,512,2048]{2,1,0:T(8,128)(2,1)S(1)}, u32[]{:S(2)}, u32[]{:S(2)}) collective-permute-start(bf16[1,512,2048]{2,1,0:T(8,128)(2,1)} %param.9), channel_id=1, source_target_pairs={{8,0},{16,8},{24,16},{0,24},{9,1},{17,9},{25,17},{1,25},{10,2},{18... | collective-permute-start | bytes 6291464 | tf_op jit(solution)/shard_map/ppermute | solution.py:745
  3.1 24.2 %copy-start.3 = (bf16[1,1024,2048]{2,1,0:T(8,128)(2,1)S(1)}, bf16[1,1024,2048]{2,1,0:T(8,128)(2,1)}, u32[]{:S(2)}) copy-start(bf16[1,1024,2048]{2,1,0:T(8,128)(2,1)} %param.10) | copy-start | bytes 12582916
  3.7 23.5 %copy-start.2 = (s32[2]{0:T(128)S(1)}, s32[2]{0:T(128)}, u32[]{:S(2)}) copy-start(s32[2]{0:T(128)} %pad_add_fusion.place) | copy-start | bytes 28
  8.2 19.1 %collective-permute-start = (bf16[3,512,256]{2,1,0:T(8,128)(2,1)}, bf16[3,512,256]{2,1,0:T(8,128)(2,1)S(1)}, u32[]{:S(2)}, u32[]{:S(2)}) collective-permute-start(bf16[3,512,256]{2,1,0:T(8,128)(2,1)} %get-tuple-element.60), channel_id=1, source_target_pairs={{0,1},{1,0},{2,3},{3,2},{4,5},{5,4},{6,7},{7,6},{8,9},{9,8},{10,11... | collective-permute-start | bytes 2359304 | tf_op jit(solution)/shard_map/ppermute | solution.py:518
  9.7 23.2 %collective-permute-start.2 = (bf16[1040,128]{1,0:T(8,128)(2,1)}, bf16[1040,128]{1,0:T(8,128)(2,1)S(1)}, u32[]{:S(2)}, u32[]{:S(2)}) collective-permute-start(bf16[1040,128]{1,0:T(8,128)(2,1)} %get-tuple-element.62), channel_id=1, source_target_pairs={{0,2},{1,3},{2,4},{3,5},{4,6},{5,7},{6,0},{7,1},{8,10},{9,11},{10,... | collective-permute-start | bytes 798728 | tf_op jit(solution)/shard_map/ppermute | solution.py:515
  11.3 21.6 %collective-permute-start.3 = (bf16[1040,128]{1,0:T(8,128)(2,1)}, bf16[1040,128]{1,0:T(8,128)(2,1)S(1)}, u32[]{:S(2)}, u32[]{:S(2)}) collective-permute-start(bf16[1040,128]{1,0:T(8,128)(2,1)} %get-tuple-element.63), channel_id=1, source_target_pairs={{0,4},{1,5},{2,6},{3,7},{4,0},{5,1},{6,2},{7,3},{8,12},{9,13},{10,... | collective-permute-start | bytes 798728 | tf_op jit(solution)/shard_map/ppermute | solution.py:515
  13.9 19.0 %collective-permute-start.4 = (bf16[1040,128]{1,0:T(8,128)(2,1)}, bf16[1040,128]{1,0:T(8,128)(2,1)S(1)}, u32[]{:S(2)}, u32[]{:S(2)}) collective-permute-start(bf16[1040,128]{1,0:T(8,128)(2,1)} %get-tuple-element.64), channel_id=1, source_target_pairs={{0,6},{1,7},{2,0},{3,1},{4,2},{5,3},{6,4},{7,5},{8,14},{9,15},{10,... | collective-permute-start | bytes 798728 | tf_op jit(solution)/shard_map/ppermute | solution.py:515
  27.2 5.7 %copy-start.4 = (bf16[1,512,1024]{2,1,0:T(8,128)(2,1)S(1)}, bf16[1,512,1024]{2,1,0:T(8,128)(2,1)}, u32[]{:S(2)}) copy-start(bf16[1,512,1024]{2,1,0:T(8,128)(2,1)} %param.8) | copy-start | bytes 3145732
  31.1 9.2 %copy-start.1 = (bf16[1040,128]{1,0:T(8,128)(2,1)S(1)}, bf16[1040,128]{1,0:T(8,128)(2,1)}, u32[]{:S(2)}) copy-start(bf16[1040,128]{1,0:T(8,128)(2,1)} %get-tuple-element.66.x0) | copy-start | bytes 798724
  31.1 22.3 %collective-permute-start.5 = (bf16[512,256]{1,0:T(8,128)(2,1)S(1)}, bf16[512,256]{1,0:T(8,128)(2,1)S(1)}, u32[]{:S(2)}, u32[]{:S(2)}) collective-permute-start(bf16[512,256]{1,0:T(8,128)(2,1)S(1)} %get-tuple-element.69), channel_id=1, source_target_pairs={{0,1},{1,0},{2,3},{3,2},{4,5},{5,4},{6,7},{7,6},{8,9},{9,8},{10,11... | collective-permute-start | bytes 786440 | tf_op jit(solution)/shard_map/ppermute | solution.py:518
  33.6 9.9 %collective-permute-start.6 = (bf16[512,128]{1,0:T(8,128)(2,1)S(1)}, bf16[512,128]{1,0:T(8,128)(2,1)S(1)}, u32[]{:S(2)}, u32[]{:S(2)}) collective-permute-start(bf16[512,128]{1,0:T(8,128)(2,1)S(1)} %get-tuple-element.71), channel_id=1, source_target_pairs={{0,2},{1,3},{2,4},{3,5},{4,6},{5,7},{6,0},{7,1},{8,10},{9,11},{10,... | collective-permute-start | bytes 393224 | tf_op jit(solution)/shard_map/ppermute | solution.py:515
  37.9 10.0 %collective-permute-start.7 = (bf16[512,128]{1,0:T(8,128)(2,1)S(1)}, bf16[512,128]{1,0:T(8,128)(2,1)S(1)}, u32[]{:S(2)}, u32[]{:S(2)}) collective-permute-start(bf16[512,128]{1,0:T(8,128)(2,1)S(1)} %get-tuple-element.72), channel_id=1, source_target_pairs={{0,4},{1,5},{2,6},{3,7},{4,0},{5,1},{6,2},{7,3},{8,12},{9,13},{10,... | collective-permute-start | bytes 393224 | tf_op jit(solution)/shard_map/ppermute | solution.py:515
  39.5 8.6 %collective-permute-start.8 = (bf16[512,128]{1,0:T(8,128)(2,1)S(1)}, bf16[512,128]{1,0:T(8,128)(2,1)S(1)}, u32[]{:S(2)}, u32[]{:S(2)}) collective-permute-start(bf16[512,128]{1,0:T(8,128)(2,1)S(1)} %get-tuple-element.73), channel_id=1, source_target_pairs={{0,6},{1,7},{2,0},{3,1},{4,2},{5,3},{6,4},{7,5},{8,14},{9,15},{10,... | collective-permute-start | bytes 393224 | tf_op jit(solution)/shard_map/ppermute | solution.py:515
  42.9 14.2 %collective-permute-start.9 = (bf16[2064,128]{1,0:T(8,128)(2,1)S(1)}, bf16[2064,128]{1,0:T(8,128)(2,1)S(1)}, u32[]{:S(2)}, u32[]{:S(2)}) collective-permute-start(bf16[2064,128]{1,0:T(8,128)(2,1)S(1)} %get-tuple-element.68._after), channel_id=1, source_target_pairs={{0,1},{1,0},{2,3},{3,2},{4,5},{5,4},{6,7},{7,6},{8,9},{9,8},{10,11... | collective-permute-start | bytes 1585160 | tf_op jit(solution)/shard_map/ppermute | solution.py:518
  43.5 18.8 %collective-permute-start.10 = (bf16[512,128]{1,0:T(8,128)(2,1)S(1)}, bf16[512,128]{1,0:T(8,128)(2,1)S(1)}, u32[]{:S(2)}, u32[]{:S(2)}) collective-permute-start(bf16[512,128]{1,0:T(8,128)(2,1)S(1)} %get-tuple-element.78), channel_id=1, source_target_pairs={{0,2},{1,3},{2,4},{3,5},{4,6},{5,7},{6,0},{7,1},{8,10},{9,11},{10,... | collective-permute-start | bytes 393224 | tf_op jit(solution)/shard_map/ppermute | solution.py:515
  47.9 14.4 %collective-permute-start.11 = (bf16[512,128]{1,0:T(8,128)(2,1)S(1)}, bf16[512,128]{1,0:T(8,128)(2,1)S(1)}, u32[]{:S(2)}, u32[]{:S(2)}) collective-permute-start(bf16[512,128]{1,0:T(8,128)(2,1)S(1)} %get-tuple-element.79), channel_id=1, source_target_pairs={{0,4},{1,5},{2,6},{3,7},{4,0},{5,1},{6,2},{7,3},{8,12},{9,13},{10,... | collective-permute-start | bytes 393224 | tf_op jit(solution)/shard_map/ppermute | solution.py:515
  48.1 14.2 %collective-permute-start.12 = (bf16[512,128]{1,0:T(8,128)(2,1)S(1)}, bf16[512,128]{1,0:T(8,128)(2,1)S(1)}, u32[]{:S(2)}, u32[]{:S(2)}) collective-permute-start(bf16[512,128]{1,0:T(8,128)(2,1)S(1)} %get-tuple-element.80), channel_id=1, source_target_pairs={{0,6},{1,7},{2,0},{3,1},{4,2},{5,3},{6,4},{7,5},{8,14},{9,15},{10,... | collective-permute-start | bytes 393224 | tf_op jit(solution)/shard_map/ppermute | solution.py:515
  54.7 12.4 %collective-permute-start.13 = (bf16[1024,128]{1,0:T(8,128)(2,1)S(1)}, bf16[1024,128]{1,0:T(8,128)(2,1)S(1)}, u32[]{:S(2)}, u32[]{:S(2)}) collective-permute-start(bf16[1024,128]{1,0:T(8,128)(2,1)S(1)} %get-tuple-element.74._after), channel_id=1, source_target_pairs={{0,1},{1,0},{2,3},{3,2},{4,5},{5,4},{6,7},{7,6},{8,9},{9,8},{10,11... | collective-permute-start | bytes 786440 | tf_op jit(solution)/shard_map/ppermute | solution.py:518
  57.2 5.1 %copy-start = (bf16[3,512,256]{2,1,0:T(8,128)(2,1)S(1)}, bf16[3,512,256]{2,1,0:T(8,128)(2,1)}, u32[]{:S(2)}) copy-start(bf16[3,512,256]{2,1,0:T(8,128)(2,1)} %get-tuple-element.81.own) | copy-start | bytes 2359300
  63.7 6.5 %collective-permute-start.14 = (bf16[1024,128]{1,0:T(8,128)(2,1)S(1)}, bf16[1024,128]{1,0:T(8,128)(2,1)S(1)}, u32[]{:S(2)}, u32[]{:S(2)}) collective-permute-start(bf16[1024,128]{1,0:T(8,128)(2,1)S(1)} %get-tuple-element.88), channel_id=1, source_target_pairs={{0,1},{1,0},{2,3},{3,2},{4,5},{5,4},{6,7},{7,6},{8,9},{9,8},{10,11... | collective-permute-start | bytes 786440 | tf_op jit(solution)/shard_map/ppermute | solution.py:518
  64.2 24.8 %collective-permute-start.17 = (bf16[2,512,256]{2,1,0:T(8,128)(2,1)S(1)}, bf16[2,512,256]{2,1,0:T(8,128)(2,1)S(1)}, u32[]{:S(2)}, u32[]{:S(2)}) collective-permute-start(bf16[2,512,256]{2,1,0:T(8,128)(2,1)S(1)} %get-tuple-element.82._after.edge), channel_id=1, source_target_pairs={{0,2},{1,3},{2,4},{3,5},{4,6},{5,7},{8,10},{9,11},{10,12},{11,13},... | collective-permute-start | bytes 1572872 | tf_op jit(solution)/shard_map/ppermute | solution.py:616
  68.9 18.3 %collective-permute-start.16 = (bf16[2,512,256]{2,1,0:T(8,128)(2,1)S(1)}, bf16[2,512,256]{2,1,0:T(8,128)(2,1)S(1)}, u32[]{:S(2)}, u32[]{:S(2)}) collective-permute-start(bf16[2,512,256]{2,1,0:T(8,128)(2,1)S(1)} %get-tuple-element.98), channel_id=1, source_target_pairs={{2,0},{3,1},{4,2},{5,3},{6,4},{7,5},{10,8},{11,9},{12,10},{13,11},... | collective-permute-start | bytes 1572872 | tf_op jit(solution)/shard_map/ppermute | solution.py:628
  72.9 7.9 %collective-permute-start.15 = (bf16[1,1024,128]{2,1,0:T(8,128)(2,1)S(1)}, bf16[1,1024,128]{2,1,0:T(8,128)(2,1)S(1)}, u32[]{:S(2)}, u32[]{:S(2)}) collective-permute-start(bf16[1,1024,128]{2,1,0:T(8,128)(2,1)S(1)} %get-tuple-element.89._after), channel_id=1, source_target_pairs={{0,1},{1,0},{2,3},{3,2},{4,5},{5,4},{6,7},{7,6},{8,9},{9,8},{10,11... | collective-permute-start | bytes 786440 | tf_op jit(solution)/shard_map/ppermute | solution.py:518
  78.1 19.6 %collective-permute-start.18 = (bf16[2,1024,128]{2,1,0:T(8,128)(2,1)S(1)}, bf16[2,1024,128]{2,1,0:T(8,128)(2,1)S(1)}, u32[]{:S(2)}, u32[]{:S(2)}) collective-permute-start(bf16[2,1024,128]{2,1,0:T(8,128)(2,1)S(1)} %get-tuple-element.94._after._after_edge), channel_id=1, source_target_pairs={{0,1},{1,0},{2,3},{3,2},{4,5},{5,4},{6,7},{7,6},{8,9},{9,8},{10,11... | collective-permute-start | bytes 1572872 | tf_op jit(solution)/shard_map/ppermute | solution.py:518
  83.3 16.8 %collective-permute-start.20 = (bf16[1,512,128]{2,1,0:T(8,128)(2,1)S(1)}, bf16[1,512,128]{2,1,0:T(8,128)(2,1)S(1)}, u32[]{:S(2)}, u32[]{:S(2)}) collective-permute-start(bf16[1,512,128]{2,1,0:T(8,128)(2,1)S(1)} %get-tuple-element.103), channel_id=1, source_target_pairs={{0,6},{1,7},{2,0},{3,1},{4,2},{5,3},{6,4},{7,5},{8,14},{9,15},{10,... | collective-permute-start | bytes 393224 | tf_op jit(solution)/shard_map/ppermute | solution.py:515
  86.3 13.8 %collective-permute-start.21 = (bf16[1,512,128]{2,1,0:T(8,128)(2,1)S(1)}, bf16[1,512,128]{2,1,0:T(8,128)(2,1)S(1)}, u32[]{:S(2)}, u32[]{:S(2)}) collective-permute-start(bf16[1,512,128]{2,1,0:T(8,128)(2,1)S(1)} %get-tuple-element.104), channel_id=1, source_target_pairs={{0,4},{1,5},{2,6},{3,7},{4,0},{5,1},{6,2},{7,3},{8,12},{9,13},{10,... | collective-permute-start | bytes 393224 | tf_op jit(solution)/shard_map/ppermute | solution.py:515
  87.2 12.9 %collective-permute-start.22 = (bf16[1,512,128]{2,1,0:T(8,128)(2,1)S(1)}, bf16[1,512,128]{2,1,0:T(8,128)(2,1)S(1)}, u32[]{:S(2)}, u32[]{:S(2)}) collective-permute-start(bf16[1,512,128]{2,1,0:T(8,128)(2,1)S(1)} %get-tuple-element.105), channel_id=1, source_target_pairs={{0,2},{1,3},{2,4},{3,5},{4,6},{5,7},{6,0},{7,1},{8,10},{9,11},{10,... | collective-permute-start | bytes 393224 | tf_op jit(solution)/shard_map/ppermute | solution.py:515
  96.4 5.6 %collective-permute-start.23 = (f32[8,512]{1,0:T(8,128)S(1)}, f32[8,512]{1,0:T(8,128)S(1)}, u32[]{:S(2)}, u32[]{:S(2)}) collective-permute-start(f32[8,512]{1,0:T(8,128)S(1)} %get-tuple-element.99._after._after_edge), channel_id=1, source_target_pairs={{2,0},{3,1},{4,2},{5,3},{6,4},{7,5},{10,8},{11,9},{12,10},{13,11},... | collective-permute-start | bytes 49160 | tf_op jit(solution)/shard_map/ppermute | solution.py:691
  103.9 14.8 %collective-permute-start.26 = (bf16[3,512,256]{2,1,0:T(8,128)(2,1)S(1)}, bf16[3,512,256]{2,1,0:T(8,128)(2,1)S(1)}, u32[]{:S(2)}, u32[]{:S(2)}) collective-permute-start(bf16[3,512,256]{2,1,0:T(8,128)(2,1)S(1)} %get-tuple-element.109._after._after_edge), channel_id=1, source_target_pairs={{0,1},{1,0},{2,3},{3,2},{4,5},{5,4},{6,7},{7,6},{8,9},{9,8},{10,11... | collective-permute-start | bytes 2359304 | tf_op jit(solution)/shard_map/ppermute | solution.py:518
  105.1 18.7 %collective-permute-start.24 = (bf16[2,512,128]{2,1,0:T(8,128)(2,1)S(1)}, bf16[2,512,128]{2,1,0:T(8,128)(2,1)S(1)}, u32[]{:S(2)}, u32[]{:S(2)}) collective-permute-start(bf16[2,512,128]{2,1,0:T(8,128)(2,1)S(1)} %unsort_last.1), channel_id=1, source_target_pairs={{0,4},{1,5},{2,6},{3,7},{4,0},{5,1},{6,2},{7,3},{8,12},{9,13},{10,... | collective-permute-start | bytes 786440 | tf_op jit(solution)/shard_map/ppermute | solution.py:515
  107.6 16.2 %collective-permute-start.19 = (bf16[2,512,128]{2,1,0:T(8,128)(2,1)S(1)}, bf16[2,512,128]{2,1,0:T(8,128)(2,1)S(1)}, u32[]{:S(2)}, u32[]{:S(2)}) collective-permute-start(bf16[2,512,128]{2,1,0:T(8,128)(2,1)S(1)} %get-tuple-element.102), channel_id=1, source_target_pairs={{0,6},{1,7},{2,0},{3,1},{4,2},{5,3},{6,4},{7,5},{8,14},{9,15},{10,... | collective-permute-start | bytes 786440 | tf_op jit(solution)/shard_map/ppermute | solution.py:515
  109.0 14.7 %collective-permute-start.25 = (bf16[2,512,128]{2,1,0:T(8,128)(2,1)S(1)}, bf16[2,512,128]{2,1,0:T(8,128)(2,1)S(1)}, u32[]{:S(2)}, u32[]{:S(2)}) collective-permute-start(bf16[2,512,128]{2,1,0:T(8,128)(2,1)S(1)} %get-tuple-element.110), channel_id=1, source_target_pairs={{0,2},{1,3},{2,4},{3,5},{4,6},{5,7},{6,0},{7,1},{8,10},{9,11},{10,... | collective-permute-start | bytes 786440 | tf_op jit(solution)/shard_map/ppermute | solution.py:515
